TPU v7x, 32 devices: a whole 2x2x4 slice. The times are simulated.
32 devices in a mesh: dp: 16 (over z, x, core), blk: 2 (over y).
Axes of the slice: x: 2, y: 2, z: 4, core: 2. Of those that a mesh axis runs over, the one named last changes fastest.
Arguments:
- tokens: bfloat16 [32, 512, 768], P('dp', 'blk'), may hold values from -6 to 6
- boxes: int32 [2, 32, 512], P(None, 'dp', 'blk'), may hold values from 0 to 1000
- lengths: int32 [32], P('dp'), may hold values from 40 to 512, as said below
- wqkv: bfloat16 [768, 2304], P('dp', 'blk'), may hold values from -0.21875 to 0.21875
- wbox: bfloat16 [768, 768], P('dp', 'blk'), may hold values from -0.375 to 0.375
- wout: bfloat16 [768, 768], P('dp', 'blk'), may hold values from -1.75 to 1.75
- wup: bfloat16 [768, 3072], P('dp', 'blk'), may hold values from -0.21875 to 0.21875
- wdown: bfloat16 [3072, 768], P('dp', 'blk'), may hold values from -0.109375 to 0.109375
- vectors: bfloat16 [9216], P(('dp', 'blk')), may hold values from -1.5 to 1.6
- cotangent: bfloat16 [32, 512, 768], P('dp', 'blk'), may hold values from -6 to 6
Outputs:
- output: bfloat16 [32, 512, 768], P('dp', 'blk')
- tokens_grad: float32 [32, 512, 768], P('dp', 'blk')
- wqkv_grad: float32 [768, 2304], P('dp', 'blk')
- wbox_grad: float32 [768, 768], P('dp', 'blk')
- wout_grad: float32 [768, 768], P('dp', 'blk')
- wup_grad: float32 [768, 3072], P('dp', 'blk')
- wdown_grad: float32 [3072, 768], P('dp', 'blk')
- vectors_grad: float32 [9216], P(('dp', 'blk'))
Inputs may be any that keep to these rules, and one draw needn't show every extreme that they name: `lengths`: in each run of 2 pages that one index of dp holds, one page, drawn from the seed, has more than 256 real tokens; one page of all, drawn from the seed, has all 512.
All inputs are finite; a program needn't handle non-finite values.
Results may differ from a plain program's by a relative error of at most 0.023.
Values may be sent and summed in bfloat16 or wider, within the bound.
A program may use at most 256 MiB of HBM per device.

v0:
```python
from functools import partial
import math

import jax
import jax.numpy as jnp
from jax import lax
from jax.sharding import PartitionSpec as P

HEADS = 12
HEAD = 64
FREQ = 192
BOX_DIM = 768


EPSILON = 1e-12
MASKED = -1e30


def box_table(boxes):
    frequency = jnp.exp(jnp.arange(FREQ, dtype=jnp.float32) * (-math.log(10000.0) / FREQ))
    across = boxes[0].astype(jnp.float32)[..., None] * frequency
    upward = boxes[1].astype(jnp.float32)[..., None] * frequency
    return jnp.concatenate(
        [jnp.cos(across), jnp.sin(across), jnp.cos(upward), jnp.sin(upward)], axis=-1
    )


def rotate(coeffs, own_table):
    cos_across, sin_across, cos_upward, sin_upward = jnp.split(own_table[..., None, :], 4, axis=-1)
    on_sine_across, on_cosine_across, on_sine_upward, on_cosine_upward = jnp.split(
        coeffs, 4, axis=-1
    )
    return jnp.concatenate(
        [
            on_sine_across * sin_across + on_cosine_across * cos_across,
            on_cosine_across * sin_across - on_sine_across * cos_across,
            on_sine_upward * sin_upward + on_cosine_upward * cos_upward,
            on_cosine_upward * sin_upward - on_sine_upward * cos_upward,
        ],
        axis=-1,
    )


def unrotate(grad_rows, own_table):
    cos_across, sin_across, cos_upward, sin_upward = jnp.split(own_table[..., None, :], 4, axis=-1)
    first_across, second_across, first_upward, second_upward = jnp.split(grad_rows, 4, axis=-1)
    return jnp.concatenate(
        [
            first_across * sin_across - second_across * cos_across,
            first_across * cos_across + second_across * sin_across,
            first_upward * sin_upward - second_upward * cos_upward,
            first_upward * cos_upward + second_upward * sin_upward,
        ],
        axis=-1,
    )


def layer_norm(hidden, norm_gain, norm_shift):
    row_mean = jnp.mean(hidden, axis=-1, keepdims=True)
    centered = hidden - row_mean
    variance = jnp.mean(centered * centered, axis=-1, keepdims=True)
    return centered * lax.rsqrt(variance + EPSILON) * norm_gain + norm_shift


def unpack(vector_all, model_width, hidden_units):
    cuts = [model_width] * 5 + [hidden_units] + [model_width] * 3
    pieces = []
    offset = 0
    for length_here in cuts:
        pieces.append(vector_all[offset : offset + length_here])
        offset = offset + length_here
    return pieces


def on_device(tokens, boxes, lengths, wqkv, wbox, wout, wup, wdown, vectors, cotangent):
    page_count, block_rows, model_width = tokens.shape
    score_scale = HEAD ** (-0.5)
    parted = (
        lax.all_gather(wqkv, "blk", axis=1, tiled=True),
        lax.all_gather(wbox, "blk", axis=1, tiled=True),
        lax.all_gather(wout, "blk", axis=1, tiled=True),
        lax.all_gather(wup, "blk", axis=1, tiled=True),
        lax.all_gather(wdown, "blk", axis=1, tiled=True),
        lax.all_gather(vectors, "blk", axis=0, tiled=True),
    )
    full_qkv, full_box, full_out, full_up, full_down, full_vec = (
        lax.all_gather(parted[0], "dp", axis=0, tiled=True),
        lax.all_gather(parted[1], "dp", axis=0, tiled=True),
        lax.all_gather(parted[2], "dp", axis=0, tiled=True),
        lax.all_gather(parted[3], "dp", axis=0, tiled=True),
        lax.all_gather(parted[4], "dp", axis=0, tiled=True),
        lax.all_gather(parted[5], "dp", axis=0, tiled=True),
    )
    hidden_units = full_up.shape[1]
    (
        bias_query,
        bias_value,
        bias_out,
        gain_one,
        shift_one,
        bias_up,
        bias_down,
        gain_two,
        shift_two,
    ) = unpack(full_vec.astype(jnp.float32), model_width, hidden_units)
    flat_tokens = tokens.reshape(-1, model_width)
    projected = jnp.dot(flat_tokens, full_qkv, preferred_element_type=jnp.float32)
    query_low = (projected[:, :model_width] + bias_query).astype(jnp.bfloat16)
    key_low = projected[:, model_width : 2 * model_width].astype(jnp.bfloat16)
    value_low = (projected[:, 2 * model_width :] + bias_value).astype(jnp.bfloat16)
    head_shape = (page_count, block_rows, HEADS, HEAD)
    heads_q = query_low.reshape(head_shape)
    heads_k = key_low.reshape(head_shape)
    heads_v = value_low.reshape(head_shape)
    own_table = box_table(boxes)
    coeffs = jnp.einsum(
        "pqhd,hdc->pqhc",
        heads_q,
        full_box.reshape(HEADS, HEAD, BOX_DIM),
        preferred_element_type=jnp.float32,
    )
    box_query = rotate(coeffs, own_table).astype(jnp.bfloat16)
    box_keys = own_table.astype(jnp.bfloat16)

    def key_table(pieces):
        return pieces[-1]

    def scores_for(key_heads, piece_table):
        key_count = key_heads.shape[1]
        text_part = jnp.einsum(
            "pqhd,pkhd->phqk", heads_q, key_heads, preferred_element_type=jnp.float32
        )
        box_part = jnp.einsum(
            "pqhc,pkc->phqk", box_query, piece_table, preferred_element_type=jnp.float32
        )
        positions = jnp.arange(key_count, dtype=jnp.int32)
        is_valid = (positions[None, :] < lengths[:, None])[:, None, None, :]
        return ((text_part + box_part) * score_scale, is_valid)

    stat_shape = (page_count, HEADS, block_rows)
    pieces = (
        lax.all_gather(heads_k, "blk", axis=1, tiled=True),
        lax.all_gather(box_keys, "blk", axis=1, tiled=True),
    )
    row_high = jnp.full(stat_shape, -jnp.inf, jnp.float32)
    row_total = jnp.zeros(stat_shape, jnp.float32)
    raw_scores, is_valid = scores_for(pieces[0], key_table(pieces))
    masked = jnp.where(is_valid, raw_scores, MASKED)
    new_high = jnp.max(masked, axis=-1)
    kept = jnp.where(is_valid, jnp.exp(masked - new_high[..., None]), 0.0)
    row_high, row_total = (
        new_high,
        row_total * jnp.exp(row_high - new_high) + jnp.sum(kept, axis=-1),
    )
    log_total = row_high + jnp.log(row_total)
    pieces = (
        lax.all_gather(heads_k, "blk", axis=1, tiled=True),
        lax.all_gather(heads_v, "blk", axis=1, tiled=True),
        lax.all_gather(box_keys, "blk", axis=1, tiled=True),
    )
    raw_scores, is_valid = scores_for(pieces[0], key_table(pieces))
    probs_low = jnp.where(is_valid, jnp.exp(raw_scores - log_total[..., None]), 0.0).astype(
        jnp.bfloat16
    )
    mixed_heads = jnp.einsum(
        "phqk,pkhd->pqhd", probs_low, pieces[1], preferred_element_type=jnp.float32
    )
    mixed_low = mixed_heads.astype(jnp.bfloat16).reshape(-1, model_width)
    attended = jnp.dot(mixed_low, full_out, preferred_element_type=jnp.float32) + bias_out
    first_sum = flat_tokens.astype(jnp.float32) + attended
    first_norm = layer_norm(first_sum, gain_one, shift_one)
    first_low = first_norm.astype(jnp.bfloat16)
    pre_act = jnp.dot(first_low, full_up, preferred_element_type=jnp.float32) + bias_up
    hidden_low = jax.nn.gelu(pre_act, approximate=False).astype(jnp.bfloat16)
    branch = jnp.dot(hidden_low, full_down, preferred_element_type=jnp.float32) + bias_down
    second_sum = first_norm + branch
    output = layer_norm(second_sum, gain_two, shift_two).astype(jnp.bfloat16).reshape(tokens.shape)
    parted_again = (
        lax.all_gather(wqkv, "blk", axis=1, tiled=True),
        lax.all_gather(wbox, "blk", axis=1, tiled=True),
        lax.all_gather(wout, "blk", axis=1, tiled=True),
        lax.all_gather(wup, "blk", axis=1, tiled=True),
        lax.all_gather(wdown, "blk", axis=1, tiled=True),
    )
    back_qkv, back_box, back_out, back_up, back_down = (
        lax.all_gather(parted_again[0], "dp", axis=0, tiled=True),
        lax.all_gather(parted_again[1], "dp", axis=0, tiled=True),
        lax.all_gather(parted_again[2], "dp", axis=0, tiled=True),
        lax.all_gather(parted_again[3], "dp", axis=0, tiled=True),
        lax.all_gather(parted_again[4], "dp", axis=0, tiled=True),
    )
    seed_grad = cotangent.reshape(-1, model_width).astype(jnp.float32)
    second_back = jax.vjp(layer_norm, second_sum, gain_two, shift_two)[1]
    d_second, d_gain_two, d_shift_two = second_back(seed_grad)
    d_branch = d_second.astype(jnp.bfloat16)
    d_hidden = jnp.dot(d_branch, back_down.T, preferred_element_type=jnp.float32)
    gelu_back = jax.vjp(partial(jax.nn.gelu, approximate=False), pre_act)[1]
    d_pre = gelu_back(d_hidden)[0].astype(jnp.bfloat16)
    d_first = jnp.dot(d_pre, back_up.T, preferred_element_type=jnp.float32) + d_second
    first_back = jax.vjp(layer_norm, first_sum, gain_one, shift_one)[1]
    d_first_sum, d_gain_one, d_shift_one = first_back(d_first)
    d_attended = d_first_sum.astype(jnp.bfloat16)
    d_mixed = (
        jnp.dot(d_attended, back_out.T, preferred_element_type=jnp.float32)
        .astype(jnp.bfloat16)
        .reshape(head_shape)
    )
    row_delta = jnp.einsum("pqhd,pqhd->phq", d_mixed.astype(jnp.float32), mixed_heads)
    pieces = (
        lax.all_gather(heads_k, "blk", axis=1, tiled=True),
        lax.all_gather(heads_v, "blk", axis=1, tiled=True),
        lax.all_gather(box_keys, "blk", axis=1, tiled=True),
    )
    key_count = pieces[0].shape[1]
    piece_table = key_table(pieces)
    raw_scores, is_valid = scores_for(pieces[0], piece_table)
    probs = jnp.where(is_valid, jnp.exp(raw_scores - log_total[..., None]), 0.0)
    d_probs = jnp.einsum("pqhd,pkhd->phqk", d_mixed, pieces[1], preferred_element_type=jnp.float32)
    d_raw = (probs * (d_probs - row_delta[..., None])).astype(jnp.bfloat16)
    d_query = (
        jnp.einsum("phqk,pkhd->pqhd", d_raw, pieces[0], preferred_element_type=jnp.float32)
        * score_scale
    )
    d_box_query = (
        jnp.einsum("phqk,pkc->pqhc", d_raw, piece_table, preferred_element_type=jnp.float32)
        * score_scale
    )
    key_part = (
        jnp.einsum("phqk,pqhd->pkhd", d_raw, heads_q, preferred_element_type=jnp.float32)
        * score_scale
    )
    value_part = jnp.einsum(
        "phqk,pqhd->pkhd", probs.astype(jnp.bfloat16), d_mixed, preferred_element_type=jnp.float32
    )
    d_keys_all = key_part
    d_values_all = value_part
    d_query, d_box_query, d_keys_all, d_values_all = (
        d_query,
        d_box_query,
        d_keys_all,
        d_values_all,
    )
    d_keys_own, d_values_own = (
        lax.psum_scatter(
            d_keys_all.astype(jnp.bfloat16), "blk", scatter_dimension=1, tiled=True
        ).astype(jnp.float32),
        lax.psum_scatter(
            d_values_all.astype(jnp.bfloat16), "blk", scatter_dimension=1, tiled=True
        ).astype(jnp.float32),
    )
    box_heads = back_box.reshape(HEADS, HEAD, BOX_DIM)
    d_coeffs = unrotate(d_box_query, own_table).astype(jnp.bfloat16)
    d_query_low = (
        d_query
        + jnp.einsum("pqhc,hdc->pqhd", d_coeffs, box_heads, preferred_element_type=jnp.float32)
    ).astype(jnp.bfloat16)
    d_wbox = jnp.einsum(
        "pqhd,pqhc->hdc", heads_q, d_coeffs, preferred_element_type=jnp.float32
    ).reshape(model_width, BOX_DIM)
    d_key_low = d_keys_own.astype(jnp.bfloat16).reshape(-1, model_width)
    d_value_low = d_values_own.astype(jnp.bfloat16).reshape(-1, model_width)
    d_projected = jnp.concatenate(
        [d_query_low.reshape(-1, model_width), d_key_low, d_value_low], axis=1
    )
    d_wqkv = jnp.dot(flat_tokens.T, d_projected, preferred_element_type=jnp.float32)
    d_tokens = jnp.dot(d_projected, back_qkv.T, preferred_element_type=jnp.float32) + d_first_sum
    d_wout = jnp.dot(mixed_low.T, d_attended, preferred_element_type=jnp.float32)
    d_wup = jnp.dot(first_low.T, d_pre, preferred_element_type=jnp.float32)
    d_wdown = jnp.dot(hidden_low.T, d_branch, preferred_element_type=jnp.float32)
    vector_grad = jnp.concatenate(
        [
            jnp.sum(d_query_low.reshape(-1, model_width), axis=0, dtype=jnp.float32),
            jnp.sum(d_value_low, axis=0, dtype=jnp.float32),
            jnp.sum(d_attended, axis=0, dtype=jnp.float32),
            d_gain_one,
            d_shift_one,
            jnp.sum(d_pre, axis=0, dtype=jnp.float32),
            jnp.sum(d_branch, axis=0, dtype=jnp.float32),
            d_gain_two,
            d_shift_two,
        ]
    )
    by_pages = (
        lax.psum_scatter(d_wqkv.astype(jnp.bfloat16), "dp", scatter_dimension=0, tiled=True).astype(
            jnp.float32
        ),
        lax.psum_scatter(d_wbox.astype(jnp.bfloat16), "dp", scatter_dimension=0, tiled=True).astype(
            jnp.float32
        ),
        lax.psum_scatter(d_wout.astype(jnp.bfloat16), "dp", scatter_dimension=0, tiled=True).astype(
            jnp.float32
        ),
        lax.psum_scatter(d_wup.astype(jnp.bfloat16), "dp", scatter_dimension=0, tiled=True).astype(
            jnp.float32
        ),
        lax.psum_scatter(
            d_wdown.astype(jnp.bfloat16), "dp", scatter_dimension=0, tiled=True
        ).astype(jnp.float32),
        lax.psum_scatter(
            vector_grad.astype(jnp.bfloat16), "dp", scatter_dimension=0, tiled=True
        ).astype(jnp.float32),
    )
    owned = (
        lax.psum_scatter(
            by_pages[0].astype(jnp.bfloat16), "blk", scatter_dimension=1, tiled=True
        ).astype(jnp.float32),
        lax.psum_scatter(
            by_pages[1].astype(jnp.bfloat16), "blk", scatter_dimension=1, tiled=True
        ).astype(jnp.float32),
        lax.psum_scatter(
            by_pages[2].astype(jnp.bfloat16), "blk", scatter_dimension=1, tiled=True
        ).astype(jnp.float32),
        lax.psum_scatter(
            by_pages[3].astype(jnp.bfloat16), "blk", scatter_dimension=1, tiled=True
        ).astype(jnp.float32),
        lax.psum_scatter(
            by_pages[4].astype(jnp.bfloat16), "blk", scatter_dimension=1, tiled=True
        ).astype(jnp.float32),
        lax.psum_scatter(
            by_pages[5].astype(jnp.bfloat16), "blk", scatter_dimension=0, tiled=True
        ).astype(jnp.float32),
    )
    return (
        output,
        d_tokens.reshape(tokens.shape),
        owned[0],
        owned[1],
        owned[2],
        owned[3],
        owned[4],
        owned[5],
    )


def solution(mesh):
    in_specs = (
        P("dp", "blk", None),
        P(None, "dp", "blk"),
        P("dp"),
        P("dp", "blk"),
        P("dp", "blk"),
        P("dp", "blk"),
        P("dp", "blk"),
        P("dp", "blk"),
        P(("dp", "blk")),
        P("dp", "blk", None),
    )
    out_specs = (
        P("dp", "blk", None),
        P("dp", "blk", None),
        P("dp", "blk"),
        P("dp", "blk"),
        P("dp", "blk"),
        P("dp", "blk"),
        P("dp", "blk"),
        P(("dp", "blk")),
    )
    return jax.shard_map(
        on_device, mesh=mesh, in_specs=in_specs, out_specs=out_specs, check_vma=False
    )
```

profile of v0, /device:TPU:0, one launch (start us, length us, event | category | flops | bytes accessed | tf_op | source)
XLA Modules:
  0.0 864.4 jit_solution(16868173511637534861)
XLA Ops:
  7.2 8.7 %all_gather.60 = bf16[48,2304]{1,0:T(8,128)(2,1)} all-gather(bf16[48,1152]{1,0:T(8,128)(2,1)} %param.13), channel_id=1, replica_groups=mesh['dp'=16,'blk'=2] {'blk'}, dimensions={1}, use_global_device_ids=true | all-gather | bytes 331776 | tf_op jit(solution)/shard_map/all_gather | solution.py:79
  16.0 5.0 all_gather.67
  21.7 3.7 multiply_cosine_fusion.1
  26.7 36.4 %all-gather.9.cloned.1.call-done = bf16[768,2304]{1,0:T(8,128)(2,1)} async-done(((bf16[48,2304]{1,0:T(8,128)(2,1)}), bf16[768,2304]{1,0:T(8,128)(2,1)}) %all-gather.9.cloned.1.call-update) | async-done | bytes 3538960 | tf_op jit(solution)/shard_map/all_gather | solution.py:87
  63.1 4.0 fusion.57
  67.1 2.1 copy-done.12
  72.7 2.2 copy.58
  77.1 4.9 all-reduce
  82.3 59.2 %all-reduce.1 = bf16[9216]{0:T(1024)(128)(2,1)S(1)} all-reduce(bf16[9216]{0:T(1024)(128)(2,1)S(1)} %dynamic-update-slice.1), channel_id=1, replica_groups=mesh['dp'=16,'blk'=2] {'dp'}, use_global_device_ids=true, to_apply=%add.1 | all-reduce | flops 9216 | bytes 36864
  141.5 3.1 fusion.18
  145.7 2.2 reshape.179
  149.0 5.9 all_gather.69
  155.0 9.0 %all_gather.71 = bf16[48,3072]{1,0:T(8,128)(2,1)} all-gather(bf16[48,1536]{1,0:T(8,128)(2,1)S(1)} %copy-done.19), channel_id=1, replica_groups=mesh['dp'=16,'blk'=2] {'blk'}, dimensions={1}, use_global_device_ids=true | all-gather | bytes 442368 | tf_op jit(solution)/shard_map/all_gather | solution.py:82
  164.1 5.9 all_gather.73
  171.0 2.6 copy.56
  173.6 2.4 reshape.180
  176.0 9.3 %convolution_bitcast_fusion = f32[2,256,12,768]{3,1,0,2:T(8,128)} fusion(bf16[12,64,768,1]{2,1,3,0:T(8,128)(2,1)} %bitcast.147, bf16[2,256,12,64]{1,0,3,2:T(2,128)(2,1)S(1)} %reshape.180), kind=kOutput, calls=%fused_computation.15 | convolution fusion | flops 603979776 | bytes 20840448 | tf_op jit(solution)/shard_map/pqhd,hdc->pqhc/dot_general | solution.py:116
  185.3 15.7 %add_convert_fusion.4 = (bf16[2,256,12,192]{3,1,0,2:T(8,128)(2,1)}, bf16[2,256,12,192]{3,1,0,2:T(8,128)(2,1)}, bf16[2,256,12,192]{3,1,0,2:T(8,128)(2,1)}, bf16[2,256,12,192]{3,1,0,2:T(8,128)(2,1)}) fusion(f32[2,256,12,768]{3,1,0,2:T(8,128)} %convolution_bitcast_fusion, f32[2,256,192]{2,1,0:T(8,128)S(1)} %get-tuple-element.67, ...), kind=kLoop, calls=%fused_computation.39 | loop fusion | flops 18874368 | bytes 29884416 | tf_op jit(solution)/shard_map/convert.16
  201.0 11.4 %fusion.4 = f32[2,512,256,12]{1,2,3,0:T(8,128)} fusion(bf16[2,512,768]{2,1,0:T(8,128)(2,1)} %all-gather.15.cloned.1.call-done, bf16[2,256,12,192]{3,1,0,2:T(8,128)(2,1)} %get-tuple-element.59, bf16[2,256,12,192]{3,1,0,2:T(8,128)(2,1)} %get-tuple-element.60, bf16[2,256,12,192]{3,1,0,2:T(8,128)(2,1)} %get-tuple-element.54, ...), kind=kOutput, calls=%fused_computation.13 | convolution fusion | flops 4869586944 | bytes 23592960 | tf_op jit(solution)/shard_map/pqhc,pkc->phqk/dot_general | solution.py:133
  212.4 6.6 select_reduce_fusion.1
  219.1 3.4 select_reduce_fusion
  223.7 7.5 bitcast_convert_fusion.1
  233.1 2.1 all-gather.19.cloned.1.call-done
  235.2 2.6 fusion.54
  238.2 51.5 %all-gather.21.cloned.1.call-done = bf16[768,3072]{1,0:T(8,128)(2,1)} async-done(((bf16[48,3072]{1,0:T(8,128)(2,1)}), bf16[768,3072]{1,0:T(8,128)(2,1)}) %all-gather.21.cloned.1.call-update) | async-done | bytes 4718608 | tf_op jit(solution)/shard_map/all_gather | solution.py:90
  289.7 19.6 %multiply_convert_fusion.1 = (bf16[512,3072]{1,0:T(8,128)(2,1)}, f32[512,3072]{1,0:T(8,128)}, f32[512,3072]{1,0:T(8,128)}) fusion(f32[3072]{0:T(1024)S(1)} %slice.65, bf16[768,3072]{1,0:T(8,128)(2,1)} %all-gather.21.cloned.1.call-done, f32[512,768]{1,0:T(8,128)S(1)} %get-tuple-element.93, f32[768]{0:T(1024)S(1)} %get-tuple-element.72, ...), kind=kOutput, calls=%fused_computation.23 | convolution fusion | flops 2521694208 | bytes 22042624 | tf_op jit(solution)/shard_map/dot_general | solution.py:173
  309.3 34.5 %all-gather.23.cloned.1.call-done = bf16[3072,768]{1,0:T(8,128)(2,1)} async-done(((bf16[192,768]{1,0:T(8,128)(2,1)}), bf16[3072,768]{1,0:T(8,128)(2,1)}) %all-gather.23.cloned.1.call-update) | async-done | bytes 4718608 | tf_op jit(solution)/shard_map/all_gather | solution.py:91
  343.8 6.5 fusion.55
  354.1 9.3 %fusion.46 = (bf16[3072]{0:T(1024)(128)(2,1)}, bf16[512,3072]{1,0:T(8,128)(2,1)S(1)}) fusion(f32[512,3072]{1,0:T(8,128)} %get-tuple-element.48, f32[512,3072]{1,0:T(8,128)} %get-tuple-element.94, f32[3072]{0:T(1024)S(1)} %slice.65, bf16[512,768]{1,0:T(8,128)(2,1)S(1)} %get-tuple-element.38, bf16[3072,768]{1,0:T(8,128)(2,1)S(1)} %copy-done.29), kind=kOutput, calls=%fused_computation.127 | convolution fusion | flops 2441081856 | bytes 21252096 | tf_op jit(solution)/shard_map/dot_general | solution.py:196
  363.4 3.7 multiply_reduce_fusion
  371.9 2.3 convolution_convert_fusion.5
  375.4 2.2 reshape.185
  379.5 2.2 fusion.22
  381.7 7.6 multiply_convert_fusion
  389.3 2.7 copy-done.2
  392.0 9.0 %multiply_bitcast_fusion = f32[2,256,12,768]{3,1,0,2:T(8,128)} fusion(bf16[2,12,256,512]{3,2,1,0:T(8,128)(2,1)S(1)} %multiply_convert_fusion, bf16[2,512,768]{2,1,0:T(8,128)(2,1)S(1)} %copy-done.30), kind=kOutput, calls=%fused_computation | convolution fusion | flops 4836556800 | bytes 26738688 | tf_op jit(solution)/shard_map/phqk,pkc->pqhc/dot_general | solution.py:225
  401.0 14.9 %subtract_convert_fusion.1 = (bf16[2,256,12,192]{3,1,0,2:T(8,128)(2,1)S(1)}, bf16[2,256,12,192]{3,1,0,2:T(8,128)(2,1)S(1)}, bf16[2,256,12,192]{3,1,0,2:T(8,128)(2,1)}, bf16[2,256,12,192]{3,1,0,2:T(8,128)(2,1)}) fusion(f32[2,256,12,768]{3,1,0,2:T(8,128)} %multiply_bitcast_fusion, f32[2,256,192]{2,1,0:T(8,128)} %copy-done.11, ...), kind=kLoop, calls=%fused_computation.21 | loop fusion | flops 18874368 | bytes 29884416 | tf_op jit(solution)/shard_map/convert.12
  415.8 7.2 pad_maximum_fusion.1
  423.1 3.3 bitcast_convert_fusion
  427.1 7.2 fusion.24
  434.7 5.1 fusion.25
  439.9 6.7 convolution_convert_fusion
  448.0 6.5 convolution_convert_fusion.1
  455.8 7.9 fusion.2
  465.5 5.4 fusion.56
  472.8 24.0 %reduce-scatter.27.cloned.1.call-done = bf16[48,768]{1,0:T(8,128)(2,1)} async-done(((bf16[768,768]{1,0:T(8,128)(2,1)}), bf16[48,768]{1,0:T(8,128)(2,1)}) %reduce-scatter.27.cloned.1.call-update) | async-done | bytes 73744 | tf_op jit(solution)/shard_map/reduce_scatter | solution.py:287
  498.9 25.4 %reduce-scatter.23.cloned.1.call-done = bf16[2,256,12,64]{1,3,2,0:T(8,128)(2,1)} async-done(((bf16[2,512,12,64]{1,3,2,0:T(8,128)(2,1)}), bf16[2,256,12,64]{1,3,2,0:T(8,128)(2,1)}) %reduce-scatter.23.cloned.1.call-update) | async-done | bytes 786448 | tf_op jit(solution)/shard_map/reduce_scatter | solution.py:247
  524.3 1.9 copy.73
  526.4 26.1 %reduce-scatter.21.cloned.1.call-done = bf16[2,256,12,64]{1,3,2,0:T(8,128)(2,1)} async-done(((bf16[2,512,12,64]{1,3,2,0:T(8,128)(2,1)}), bf16[2,256,12,64]{1,3,2,0:T(8,128)(2,1)}) %reduce-scatter.21.cloned.1.call-update) | async-done | bytes 786448 | tf_op jit(solution)/shard_map/reduce_scatter | solution.py:244
  552.5 1.9 copy.71
  556.7 5.5 fusion.13
  562.2 5.9 copy.90
  568.1 63.9 %reduce-scatter.35.cloned.1.call-done = bf16[192,768]{1,0:T(8,128)(2,1)} async-done(((bf16[3072,768]{1,0:T(8,128)(2,1)}), bf16[192,768]{1,0:T(8,128)(2,1)}) %reduce-scatter.35.cloned.1.call-update) | async-done | bytes 294928 | tf_op jit(solution)/shard_map/reduce_scatter | solution.py:296
  632.0 1.9 copy.96
  633.9 76.9 %reduce-scatter.31.cloned.1.call-done = bf16[48,3072]{1,0:T(8,128)(2,1)} async-done(((bf16[768,3072]{1,0:T(8,128)(2,1)}), bf16[48,3072]{1,0:T(8,128)(2,1)}) %reduce-scatter.31.cloned.1.call-update) | async-done | bytes 294928 | tf_op jit(solution)/shard_map/reduce_scatter | solution.py:293
  712.5 11.0 %reduce-scatter.41.cloned.1.call-done = bf16[384,48]{1,0:T(8,128)(2,1)} async-done(((bf16[768,48]{1,0:T(8,128)(2,1)}), bf16[384,48]{1,0:T(8,128)(2,1)}) %reduce-scatter.41.cloned.1.call-update) | async-done | bytes 36880
  725.1 12.0 %reduce-scatter.39.cloned.1.call-done = bf16[384,48]{1,0:T(8,128)(2,1)} async-done(((bf16[768,48]{1,0:T(8,128)(2,1)}), bf16[384,48]{1,0:T(8,128)(2,1)}) %reduce-scatter.39.cloned.1.call-update) | async-done | bytes 36880
  740.7 62.1 %all-reduce.2 = bf16[9216]{0:T(1024)(128)(2,1)S(1)} all-reduce(bf16[9216]{0:T(1024)(128)(2,1)S(1)} %dynamic-update-slice.10), channel_id=14, replica_groups=mesh['dp'=16,'blk'=2] {'dp'}, use_global_device_ids=true, to_apply=%region_31.32.clone | all-reduce | flops 9216 | bytes 36864
  802.9 4.9 all-reduce.3
  809.3 2.0 copy.91
  811.3 5.9 add_add_fusion.4
  817.2 6.2 reduce-scatter.43.cloned.1.call-done
  825.2 12.6 %reduce-scatter.33.cloned.1.call-done = bf16[48,1536]{1,0:T(8,128)(2,1)} async-done(((bf16[48,3072]{1,0:T(8,128)(2,1)}), bf16[48,1536]{1,0:T(8,128)(2,1)}) %reduce-scatter.33.cloned.1.call-update) | async-done | bytes 147472 | tf_op jit(solution)/shard_map/reduce_scatter | solution.py:313
  839.4 15.9 %reduce-scatter.25.cloned.1.call-done = bf16[48,1152]{0,1:T(8,128)(2,1)} async-done(((bf16[48,2304]{0,1:T(8,128)(2,1)}), bf16[48,1152]{0,1:T(8,128)(2,1)}) %reduce-scatter.25.cloned.1.call-update) | async-done | bytes 110608 | tf_op jit(solution)/shard_map/reduce_scatter | solution.py:304
  (189 shorter events, 49.5 us)
Async XLA Ops:
  7.2 55.9 %copy-start.31 = (bf16[2,256,768]{2,1,0:T(8,128)(2,1)S(1)}, bf16[2,256,768]{2,1,0:T(8,128)(2,1)}, u32[]{:S(2)}) copy-start(bf16[2,256,768]{2,1,0:T(8,128)(2,1)} %param.10) | copy-start | bytes 2359300
  7.2 55.9 %all-gather.9.cloned.1.call-start = ((), (), s32[]{:S(2)}) async-start(), calls=%async_computation.12 | async-start | bytes 3760128 | tf_op jit(solution)/shard_map/all_gather | solution.py:87
  15.9 160.1 %all-gather.17.cloned.1.call-start = ((), (), s32[]{:S(2)}) async-start(), calls=%async_computation.16 | async-start | bytes 1253376 | tf_op jit(solution)/shard_map/all_gather | solution.py:88
  20.9 180.1 %all-gather.15.cloned.1.call-start = ((), (), s32[]{:S(2)}) async-start(), calls=%async_computation.15 | async-start | bytes 2359296 | tf_op jit(solution)/shard_map/all_gather | solution.py:159
  26.6 185.8 %all-gather.13.cloned.1.call-start = ((), (), s32[]{:S(2)}) async-start(), calls=%async_computation.14 | async-start | bytes 2359296 | tf_op jit(solution)/shard_map/all_gather | solution.py:157
  67.1 2.1 copy-start.12
  69.3 5.7 copy-start.23
  69.3 5.7 copy-start.24
  69.3 7.6 copy-start.27
  74.9 148.8 %all-gather.11.cloned.1.call-start = ((), (), s32[]{:S(2)}) async-start(), calls=%async_computation.13 | async-start | bytes 2359296 | tf_op jit(solution)/shard_map/all_gather | solution.py:158
  144.5 4.5 copy-start.21
  144.5 10.4 %copy-start.19 = (bf16[48,1536]{1,0:T(8,128)(2,1)S(1)}, bf16[48,1536]{1,0:T(8,128)(2,1)}, u32[]{:S(2)}) copy-start(bf16[48,1536]{1,0:T(8,128)(2,1)} %param.16) | copy-start | bytes 442372
  144.5 19.6 %copy-start.20 = (bf16[192,384]{1,0:T(8,128)(2,1)S(1)}, bf16[192,384]{1,0:T(8,128)(2,1)}, u32[]{:S(2)}) copy-start(bf16[192,384]{1,0:T(8,128)(2,1)} %param.17) | copy-start | bytes 442372
  149.0 86.2 %all-gather.19.cloned.1.call-start = ((), (), s32[]{:S(2)}) async-start(), calls=%async_computation.17 | async-start | bytes 1253376 | tf_op jit(solution)/shard_map/all_gather | solution.py:89
  154.9 134.8 %all-gather.21.cloned.1.call-start = ((), (), s32[]{:S(2)}) async-start(), calls=%async_computation.18 | async-start | bytes 5013504 | tf_op jit(solution)/shard_map/all_gather | solution.py:90
  164.1 179.7 %all-gather.23.cloned.1.call-start = ((), (), s32[]{:S(2)}) async-start(), calls=%async_computation.19 | async-start | bytes 5013504 | tf_op jit(solution)/shard_map/all_gather | solution.py:91
  170.1 0.8 copy-start.28
  170.1 293.7 %reduce-scatter.29.cloned.1.call-start = ((), (), s32[]{:S(2)}) async-start(), calls=%async_computation.24 | async-start | bytes 1253376 | tf_op jit(solution)/shard_map/reduce_scatter | solution.py:290
  170.9 14.4 %copy-start.10 = (f32[2,256,192]{2,1,0:T(8,128)}, f32[2,256,192]{2,1,0:T(8,128)S(1)}, u32[]{:S(2)}) copy-start(f32[2,256,192]{2,1,0:T(8,128)S(1)} %get-tuple-element.66) | copy-start | bytes 1179652
  170.9 14.4 %copy-start.11 = (f32[2,256,192]{2,1,0:T(8,128)}, f32[2,256,192]{2,1,0:T(8,128)S(1)}, u32[]{:S(2)}) copy-start(f32[2,256,192]{2,1,0:T(8,128)S(1)} %get-tuple-element.67) | copy-start | bytes 1179652
  219.0 4.6 copy-start
  237.8 71.5 %copy-start.7 = (f32[512,768]{1,0:T(8,128)}, f32[512,768]{1,0:T(8,128)S(1)}, u32[]{:S(2)}) copy-start(f32[512,768]{1,0:T(8,128)S(1)} %get-tuple-element.93) | copy-start | bytes 4718596
  343.8 6.9 copy-start.3
  351.4 2.6 copy-start.29
  353.1 10.3 %slice-start = ((s8[4718592]{0:T(1024)(128)(4,1)}), s8[4194304]{0:T(1024)(128)(4,1)S(1)}, s32[]{:S(2)}) async-start(s8[4718592]{0:T(1024)(128)(4,1)} %bitcast.158), calls=%async_computation.32 | async-start | bytes 8388608
  353.3 10.1 %copy-start.16 = (bf16[512,768]{1,0:T(8,128)(2,1)}, bf16[512,768]{1,0:T(8,128)(2,1)S(1)}, u32[]{:S(2)}) copy-start(bf16[512,768]{1,0:T(8,128)(2,1)S(1)} %get-tuple-element.38) | copy-start | bytes 2359300
  354.1 9.3 %copy-start.8 = (f32[512,768]{1,0:T(8,128)S(1)}, f32[512,768]{1,0:T(8,128)}, u32[]{:S(2)}) copy-start(f32[512,768]{1,0:T(8,128)} %copy-done.7) | copy-start | bytes 4718596
  354.1 9.3 %slice-start.1 = ((s8[4718592]{0:T(1024)(128)(4,1)}), s8[524288]{0:T(1024)(128)(4,1)S(1)}, s32[]{:S(2)}) async-start(s8[4718592]{0:T(1024)(128)(4,1)} %bitcast.158), calls=%async_computation.33 | async-start | bytes 1048576
  363.4 3.7 copy-start.33
  367.1 2.9 copy-start.15
  367.8 1.2 copy-start.5
  369.1 0.9 copy-start.18
  379.5 117.4 %reduce-scatter.27.cloned.1.call-start = ((), (), s32[]{:S(2)}) async-start(), calls=%async_computation.23 | async-start | bytes 1253376 | tf_op jit(solution)/shard_map/reduce_scatter | solution.py:287
  381.7 10.3 %copy-start.30 = (bf16[2,512,768]{2,1,0:T(8,128)(2,1)S(1)}, bf16[2,512,768]{2,1,0:T(8,128)(2,1)}, u32[]{:S(2)}) copy-start(bf16[2,512,768]{2,1,0:T(8,128)(2,1)} %all-gather.15.cloned.1.call-done) | copy-start | bytes 4718596
  389.3 2.7 copy-start.2
  423.1 4.0 copy-start.1
  427.1 97.2 %reduce-scatter.23.cloned.1.call-start = ((), (), s32[]{:S(2)}) async-start(), calls=%async_computation.21 | async-start | bytes 2359296 | tf_op jit(solution)/shard_map/reduce_scatter | solution.py:247
  434.4 5.5 copy-start.17
  434.4 118.1 %reduce-scatter.21.cloned.1.call-start = ((), (), s32[]{:S(2)}) async-start(), calls=%async_computation.20 | async-start | bytes 2359296 | tf_op jit(solution)/shard_map/reduce_scatter | solution.py:244
  439.8 192.2 %reduce-scatter.35.cloned.1.call-start = ((), (), s32[]{:S(2)}) async-start(), calls=%async_computation.27 | async-start | bytes 5013504 | tf_op jit(solution)/shard_map/reduce_scatter | solution.py:296
  446.6 1.4 copy-start.9
  446.6 264.2 %reduce-scatter.31.cloned.1.call-start = ((), (), s32[]{:S(2)}) async-start(), calls=%async_computation.25 | async-start | bytes 5013504 | tf_op jit(solution)/shard_map/reduce_scatter | solution.py:293
  454.5 1.3 copy-start.14
  454.6 269.0 %reduce-scatter.41.cloned.1.call-start = ((), (), s32[]{:S(2)}) async-start(), calls=%async_computation.30 | async-start | bytes 294912
  455.8 9.7 %copy-start.4 = (bf16[2,512,12,64]{1,3,2,0:T(8,128)(2,1)S(1)}, bf16[2,512,12,64]{1,3,2,0:T(8,128)(2,1)}, u32[]{:S(2)}) copy-start(bf16[2,512,12,64]{1,3,2,0:T(8,128)(2,1)} %all-gather.13.cloned.1.call-done) | copy-start | bytes 4718596
  465.5 271.7 %reduce-scatter.39.cloned.1.call-start = ((), (), s32[]{:S(2)}) async-start(), calls=%async_computation.29 | async-start | bytes 294912
  498.6 310.7 %reduce-scatter.37.cloned.1.call-start = ((), (), s32[]{:S(2)}) async-start(), calls=%async_computation.28 | async-start | bytes 3760128
  526.4 30.3 %copy-start.32 = (bf16[2,256,768]{2,1,0:T(8,128)(2,1)S(1)}, bf16[2,256,768]{2,1,0:T(8,128)(2,1)}, u32[]{:S(2)}) copy-start(bf16[2,256,768]{2,1,0:T(8,128)(2,1)} %param.10) | copy-start | bytes 2359300
  568.0 170.7 %copy-start.13 = (bf16[2,256,12,64]{1,3,2,0:T(8,128)(2,1)S(1)}, bf16[2,256,12,64]{1,3,2,0:T(8,128)(2,1)}, u32[]{:S(2)}) copy-start(bf16[2,256,12,64]{1,3,2,0:T(8,128)(2,1)} %reduce-scatter.23.cloned.1.call-done) | copy-start | bytes 2359300
  568.0 171.4 %copy-start.26 = (bf16[768]{0:T(1024)(128)(2,1)S(1)}, bf16[768]{0:T(1024)(128)(2,1)}, u32[]{:S(2)}) copy-start(bf16[768]{0:T(1024)(128)(2,1)} %get-tuple-element.32) | copy-start | bytes 4612
  568.0 171.6 %copy-start.25 = (bf16[768]{0:T(1024)(128)(2,1)S(1)}, bf16[768]{0:T(1024)(128)(2,1)}, u32[]{:S(2)}) copy-start(bf16[768]{0:T(1024)(128)(2,1)} %get-tuple-element.36) | copy-start | bytes 4612
  568.0 171.8 %copy-start.22 = (bf16[3072]{0:T(1024)(128)(2,1)S(1)}, bf16[3072]{0:T(1024)(128)(2,1)}, u32[]{:S(2)}) copy-start(bf16[3072]{0:T(1024)(128)(2,1)} %get-tuple-element.39) | copy-start | bytes 18436
  568.0 243.2 %copy-start.6 = (f32[512,768]{1,0:T(8,128)S(1)}, f32[512,768]{1,0:T(8,128)}, u32[]{:S(2)}) copy-start(f32[512,768]{1,0:T(8,128)} %copy-done.5) | copy-start | bytes 4718596
  568.1 255.3 %reduce-scatter.43.cloned.1.call-start = ((), (), s32[]{:S(2)}) async-start(), calls=%async_computation.31 | async-start | bytes 589824
  633.9 203.9 %reduce-scatter.33.cloned.1.call-start = ((), (), s32[]{:S(2)}) async-start(), calls=%async_computation.26 | async-start | bytes 442368 | tf_op jit(solution)/shard_map/reduce_scatter | solution.py:313
  710.9 144.4 %reduce-scatter.25.cloned.1.call-start = ((), (), s32[]{:S(2)}) async-start(), calls=%async_computation.22 | async-start | bytes 884736 | tf_op jit(solution)/shard_map/reduce_scatter | solution.py:304
Sparse Core Ops, SparseCore 0:
  16.0 47.0 all-gather.8
  65.4 37.4 all-gather.16
  104.5 26.2 all-gather.14
  132.1 31.3 all-gather.12
  165.4 29.2 all-gather.10
  196.8 38.3 all-gather.18
  237.5 52.1 all-gather.20
  292.0 51.7 all-gather.22
  379.6 56.5 reduce-scatter.28
  439.7 57.1 reduce-scatter.26
  499.1 25.0 reduce-scatter.22
  526.4 26.0 reduce-scatter.20
  556.4 75.5 reduce-scatter.34
  636.2 74.5 reduce-scatter.30
  713.5 9.9 reduce-scatter.40
  726.2 10.9 reduce-scatter.38
  740.9 68.3 reduce-scatter.36
  811.4 12.0 reduce-scatter.42
  825.7 12.0 reduce-scatter.32
  840.0 15.2 reduce-scatter.24
where the time goes:
time: 874 us; the launch traced here: 864 us
  waiting for transfers between devices  400 us (46%)
  blocking collectives  166 us (19%)
  matrix products  155 us (18%)
  other arithmetic  63 us (7%)
  local copies, waits for them, and re-layouts  62.3 us (7%)
  between operations  17.8 us (2%)
    unnamed x4, blocking collectives  131 us
    reduce_scatter x1, waiting for transfers between devices, on_device(): lax.psum_scatter(d_wup.astype(jnp.bfloat16), 'dp', scatter_dimension=0, t...  76.9 us
    reduce_scatter x1, waiting for transfers between devices, on_device(): lax.psum_scatter(d_wdown.astype(jnp.bfloat16), 'dp', scatter_dimension=0,...  63.9 us
    all_gather x1, waiting for transfers between devices, on_device(): lax.all_gather(parted[3], 'dp', axis=0, tiled=True)  51.5 us
    unnamed x101, local copies, waits for them, and re-layouts  36.6 us
    all_gather x1, waiting for transfers between devices, on_device(): lax.all_gather(parted[0], 'dp', axis=0, tiled=True)  36.4 us
    all_gather x1, waiting for transfers between devices, on_device(): lax.all_gather(parted[4], 'dp', axis=0, tiled=True)  34.5 us
    another operation x2, other arithmetic  30.6 us
  transfers between devices with their start and end apart: 20, of which 15 were waited for; matrix products, arithmetic and copies ran while one was open for 27% of the time, Pallas kernels for 0%

commit v1 on v0

v1 whole, which is shorter than its diff:
```python
from functools import partial
import math

import jax
import jax.numpy as jnp
from jax import lax
from jax.sharding import PartitionSpec as P

HEADS = 12
HEAD = 64
FREQ = 192
BOX_DIM = 768

EPSILON = 1e-12
MASKED = -1e30


def box_table(boxes):
    frequency = jnp.exp(jnp.arange(FREQ, dtype=jnp.float32) * (-math.log(10000.0) / FREQ))
    across = boxes[0].astype(jnp.float32)[..., None] * frequency
    upward = boxes[1].astype(jnp.float32)[..., None] * frequency
    return jnp.concatenate(
        [jnp.cos(across), jnp.sin(across), jnp.cos(upward), jnp.sin(upward)], axis=-1
    )


def rotate(coeffs, own_table):
    cos_across, sin_across, cos_upward, sin_upward = jnp.split(own_table[..., None, :], 4, axis=-1)
    sa, ca, sb, cb = jnp.split(coeffs, 4, axis=-1)
    return jnp.concatenate(
        [
            sa * sin_across + ca * cos_across,
            ca * sin_across - sa * cos_across,
            sb * sin_upward + cb * cos_upward,
            cb * sin_upward - sb * cos_upward,
        ],
        axis=-1,
    )


def unrotate(grad_rows, own_table):
    cos_across, sin_across, cos_upward, sin_upward = jnp.split(own_table[..., None, :], 4, axis=-1)
    d1a, d2a, d1b, d2b = jnp.split(grad_rows, 4, axis=-1)
    return jnp.concatenate(
        [
            d1a * sin_across - d2a * cos_across,
            d1a * cos_across + d2a * sin_across,
            d1b * sin_upward - d2b * cos_upward,
            d1b * cos_upward + d2b * sin_upward,
        ],
        axis=-1,
    )


def normalize(hidden):
    row_mean = jnp.mean(hidden, axis=-1, keepdims=True)
    centered = hidden - row_mean
    inverse = lax.rsqrt(jnp.mean(centered * centered, axis=-1, keepdims=True) + EPSILON)
    return centered * inverse, inverse


def normalize_back(grad, unit, inverse, gain):
    scaled = grad * gain
    mean_grad = jnp.mean(scaled, axis=-1, keepdims=True)
    mean_unit = jnp.mean(scaled * unit, axis=-1, keepdims=True)
    d_hidden = inverse * (scaled - mean_grad - unit * mean_unit)
    return d_hidden, jnp.sum(grad * unit, axis=0), jnp.sum(grad, axis=0)


def unpack(vector_all, model_width, hidden_units):
    cuts = [model_width] * 5 + [hidden_units] + [model_width] * 3
    pieces = []
    offset = 0
    for length_here in cuts:
        pieces.append(vector_all[offset : offset + length_here])
        offset = offset + length_here
    return pieces


def dot32(a, b):
    return jnp.dot(a, b, preferred_element_type=jnp.float32)


def gather_weight(shard):
    part = lax.all_gather(shard, "blk", axis=1, tiled=True)
    return lax.all_gather(part, "dp", axis=0, tiled=True)


def scatter_weight(grad):
    part = lax.psum_scatter(grad.astype(jnp.bfloat16), "dp", scatter_dimension=0, tiled=True)
    return lax.psum_scatter(part, "blk", scatter_dimension=1, tiled=True).astype(jnp.float32)


def general_layer(tokens, boxes, lengths, wqkv, wbox, wout, wup, wdown, vectors, cotangent):
    blocks = lax.axis_size("blk")
    pages_here = tokens.shape[0] // blocks
    model_width = tokens.shape[2]
    to_pages = partial(
        lax.all_to_all, axis_name="blk", split_axis=0, concat_axis=1, tiled=True
    )
    from_pages = partial(
        lax.all_to_all, axis_name="blk", split_axis=1, concat_axis=0, tiled=True
    )
    page_tokens = to_pages(tokens)
    page_boxes = lax.all_to_all(boxes, "blk", split_axis=1, concat_axis=2, tiled=True)
    page_lengths = lax.dynamic_slice(lengths, (lax.axis_index("blk") * pages_here,), (pages_here,))
    full_qkv = gather_weight(wqkv)
    full_box = gather_weight(wbox)
    full_out = gather_weight(wout)
    full_up = gather_weight(wup)
    full_down = gather_weight(wdown)
    full_vec = lax.all_gather(vectors, ("dp", "blk"), axis=0, tiled=True).astype(jnp.float32)
    page_cotangent = to_pages(cotangent)
    hidden_units = full_up.shape[1]
    bq, bv, bo, g1, e1, b1, b2, g2, e2 = unpack(full_vec, model_width, hidden_units)
    page_len = page_tokens.shape[1]
    score_scale = HEAD ** (-0.5)

    x = page_tokens.reshape(-1, model_width)
    projected = dot32(x, full_qkv)
    head_shape = (pages_here, page_len, HEADS, HEAD)
    q = (projected[:, :model_width] + bq).astype(jnp.bfloat16).reshape(head_shape)
    k = projected[:, model_width : 2 * model_width].astype(jnp.bfloat16).reshape(head_shape)
    v = (projected[:, 2 * model_width :] + bv).astype(jnp.bfloat16).reshape(head_shape)
    table = box_table(page_boxes)
    box_heads = full_box.reshape(HEADS, HEAD, BOX_DIM)
    coeffs = jnp.einsum("pqhd,hdc->pqhc", q, box_heads, preferred_element_type=jnp.float32)
    box_query = rotate(coeffs, table).astype(jnp.bfloat16)
    box_keys = table.astype(jnp.bfloat16)
    scores = (
        jnp.einsum("pqhd,pkhd->phqk", q, k, preferred_element_type=jnp.float32)
        + jnp.einsum("pqhc,pkc->phqk", box_query, box_keys, preferred_element_type=jnp.float32)
    ) * score_scale
    is_valid = (jnp.arange(page_len)[None, :] < page_lengths[:, None])[:, None, None, :]
    masked = jnp.where(is_valid, scores, MASKED)
    probs = jax.nn.softmax(masked, axis=-1)
    probs_low = probs.astype(jnp.bfloat16)
    mixed = jnp.einsum("phqk,pkhd->pqhd", probs_low, v, preferred_element_type=jnp.float32)
    mixed_low = mixed.astype(jnp.bfloat16).reshape(-1, model_width)
    unit1, inv1 = normalize(x.astype(jnp.float32) + dot32(mixed_low, full_out) + bo)
    y1 = unit1 * g1 + e1
    y1_low = y1.astype(jnp.bfloat16)
    pre = dot32(y1_low, full_up) + b1
    hidden = jax.nn.gelu(pre, approximate=False).astype(jnp.bfloat16)
    unit2, inv2 = normalize(y1 + dot32(hidden, full_down) + b2)
    output = (unit2 * g2 + e2).astype(jnp.bfloat16)

    seed = page_cotangent.reshape(-1, model_width).astype(jnp.float32)
    d_h2, d_g2, d_e2 = normalize_back(seed, unit2, inv2, g2)
    d_f = d_h2.astype(jnp.bfloat16)
    d_hidden = dot32(d_f, full_down.T)
    d_pre = jax.vjp(partial(jax.nn.gelu, approximate=False), pre)[1](d_hidden)[0]
    d_pre = d_pre.astype(jnp.bfloat16)
    d_wdown = dot32(hidden.T, d_f)
    d_wup = dot32(y1_low.T, d_pre)
    d_y1 = dot32(d_pre, full_up.T) + d_h2
    d_h1, d_g1, d_e1 = normalize_back(d_y1, unit1, inv1, g1)
    d_a = d_h1.astype(jnp.bfloat16)
    d_wout = dot32(mixed_low.T, d_a)
    d_mixed = dot32(d_a, full_out.T).astype(jnp.bfloat16).reshape(head_shape)
    row_delta = jnp.einsum("pqhd,pqhd->phq", d_mixed.astype(jnp.float32), mixed)
    d_probs = jnp.einsum("pqhd,pkhd->phqk", d_mixed, v, preferred_element_type=jnp.float32)
    d_raw = (probs * (d_probs - row_delta[..., None])).astype(jnp.bfloat16)
    d_q = jnp.einsum("phqk,pkhd->pqhd", d_raw, k, preferred_element_type=jnp.float32)
    d_box_q = jnp.einsum("phqk,pkc->pqhc", d_raw, box_keys, preferred_element_type=jnp.float32)
    d_k = jnp.einsum("phqk,pqhd->pkhd", d_raw, q, preferred_element_type=jnp.float32)
    d_v = jnp.einsum("phqk,pqhd->pkhd", probs_low, d_mixed, preferred_element_type=jnp.float32)
    d_coeffs = unrotate(d_box_q * score_scale, table).astype(jnp.bfloat16)
    d_q = d_q * score_scale + jnp.einsum(
        "pqhc,hdc->pqhd", d_coeffs, box_heads, preferred_element_type=jnp.float32
    )
    d_wbox = jnp.einsum("pqhd,pqhc->hdc", q, d_coeffs, preferred_element_type=jnp.float32)
    flat = (-1, model_width)
    d_q = d_q.astype(jnp.bfloat16).reshape(flat)
    d_k = (d_k * score_scale).astype(jnp.bfloat16).reshape(flat)
    d_v = d_v.astype(jnp.bfloat16).reshape(flat)
    d_c = jnp.concatenate([d_q, d_k, d_v], axis=1)
    d_wqkv = dot32(x.T, d_c)
    d_x = dot32(d_c, full_qkv.T) + d_h1
    total = partial(jnp.sum, axis=0, dtype=jnp.float32)
    vector_grad = jnp.concatenate(
        [total(d_q), total(d_v), total(d_a), d_g1, d_e1, total(d_pre), total(d_f), d_g2, d_e2]
    )
    return (
        from_pages(output.reshape(page_tokens.shape)),
        from_pages(d_x.reshape(page_tokens.shape)),
        scatter_weight(d_wqkv),
        scatter_weight(d_wbox.reshape(model_width, BOX_DIM)),
        scatter_weight(d_wout),
        scatter_weight(d_wup),
        scatter_weight(d_wdown),
        lax.psum_scatter(vector_grad, ("dp", "blk"), scatter_dimension=0, tiled=True),
    )


def solution(mesh):
    in_specs = (
        P("dp", "blk", None),
        P(None, "dp", "blk"),
        P("dp"),
        P("dp", "blk"),
        P("dp", "blk"),
        P("dp", "blk"),
        P("dp", "blk"),
        P("dp", "blk"),
        P(("dp", "blk")),
        P("dp", "blk", None),
    )
    out_specs = (
        P("dp", "blk", None),
        P("dp", "blk", None),
        P("dp", "blk"),
        P("dp", "blk"),
        P("dp", "blk"),
        P("dp", "blk"),
        P("dp", "blk"),
        P(("dp", "blk")),
    )
    return jax.shard_map(
        general_layer, mesh=mesh, in_specs=in_specs, out_specs=out_specs, check_vma=False
    )
```

time: 874 us -> 767 us (0.88)
  waiting for transfers between devices: 400 us -> 339 us
  blocking collectives: 166 us -> 113 us
  starting transfers between devices: 1.29 us -> 18.5 us
  local copies, waits for them, and re-layouts: 62.3 us -> 53.1 us
    all_gather x8 -> x5, waiting for transfers between devices: 125 us -> 45.4 us  [gather_weight(): return lax.all_gather(part, 'dp', axis=0, tiled=True)]
    unnamed x4 -> x2, blocking collectives: 131 us -> 79.7 us
    unnamed x24 -> x19, waiting for transfers between devices: 30.3 us -> 79.6 us
    reduce_scatter x8 -> x6, waiting for transfers between devices: 245 us -> 204 us  [the longest x4 192 us: scatter_weight(): lax.psum_scatter(grad.astype(jnp.bfloat16), 'dp', scatter_dimension=0, ti...]
    another operation x2 -> x1, other arithmetic: 30.6 us -> 5.27 us
    concatenate x1 -> x2, other arithmetic: 7.22 us -> 30.4 us  [the longest x1 15.8 us: rotate(): jnp.concatenate([sa * sin_across + ca * cos_across, ca * sin_across - sa...]
    all_to_all x0 -> x5, starting transfers between devices: none -> 17.7 us  [the longest x1 3.74 us: general_layer(): from_pages(d_x.reshape(page_tokens.shape))]
    all_to_all x0 -> x5, waiting for transfers between devices: none -> 9.74 us  [the longest x1 9.56 us: general_layer(): page_tokens = to_pages(tokens)]
  transfers between devices with their start and end apart: 20 -> 20, of which waited for: 15 -> 11; matrix products, arithmetic and copies ran while one was open for 27% -> 24% of each run, Pallas kernels for 0% -> 0%
where the time goes in v1:
time: 767 us; the launch traced here: 758 us
  waiting for transfers between devices  339 us (44%)
  matrix products  157 us (20%)
  blocking collectives  113 us (15%)
  other arithmetic  62.5 us (8%)
  local copies, waits for them, and re-layouts  53.1 us (7%)
  starting transfers between devices  18.5 us (2%)
  between operations  15.1 us (2%)
    reduce_scatter x4, waiting for transfers between devices, scatter_weight(): lax.psum_scatter(grad.astype(jnp.bfloat16), 'dp', scatter_dimension=0, ti...  192 us
    unnamed x2, blocking collectives  79.7 us
    unnamed x19, waiting for transfers between devices  79.6 us
    dot_general x12, matrix products, dot32(): return jnp.dot(a, b, preferred_element_type=jnp.float32)  78.2 us
    all_gather x5, waiting for transfers between devices, gather_weight(): return lax.all_gather(part, 'dp', axis=0, tiled=True)  45.4 us
    unnamed x125, local copies, waits for them, and re-layouts  39.2 us
    all_gather x5, blocking collectives, gather_weight(): part = lax.all_gather(shard, 'blk', axis=1, tiled=True)  33.1 us
    concatenate x1, other arithmetic, rotate(): jnp.concatenate([sa * sin_across + ca * cos_across, ca * sin_across - sa...  15.8 us
  transfers between devices with their start and end apart: 20, of which 11 were waited for; matrix products, arithmetic and copies ran while one was open for 24% of the time, Pallas kernels for 0%

profile of v1, /device:TPU:0, one launch (start us, length us, event | category | flops | bytes accessed | tf_op | source)
XLA Modules:
  0.0 757.8 jit_solution(12602737985598875089)
XLA Ops:
  7.2 8.5 %all_gather.33 = bf16[48,2304]{1,0:T(8,128)(2,1)} all-gather(bf16[48,1152]{1,0:T(8,128)(2,1)} %param.13), channel_id=1, replica_groups=mesh['dp'=16,'blk'=2] {'blk'}, dimensions={1}, use_global_device_ids=true | all-gather | bytes 331776 | tf_op jit(solution)/shard_map/all_gather | solution.py:85
  15.8 5.0 all_gather.36
  20.9 5.6 all_gather.38
  26.6 6.3 all_gather.40
  34.2 3.2 all-to-all-start.1
  37.5 7.6 %all_gather.42 = bf16[192,768]{1,0:T(8,128)(2,1)} all-gather(bf16[192,384]{1,0:T(8,128)(2,1)} %param.17), channel_id=1, replica_groups=mesh['dp'=16,'blk'=2] {'blk'}, dimensions={1}, use_global_device_ids=true | all-gather | bytes 442368 | tf_op jit(solution)/shard_map/all_gather | solution.py:85
  46.1 39.9 %all-reduce = bf16[9216]{0:T(1024)(128)(2,1)S(1)} all-reduce(bf16[9216]{0:T(1024)(128)(2,1)S(1)} %dynamic-update-slice), channel_id=1, replica_groups=mesh['dp'=16,'blk'=2] {'dp','blk'}, use_global_device_ids=true, to_apply=%add | all-reduce | flops 9216 | bytes 36864
  87.9 3.6 all-to-all-start.3
  91.5 3.7 multiply_cosine_fusion.1
  95.2 5.3 fusion.50
  102.2 3.5 all-to-all-start
  106.7 9.6 %all-to-all-done = bf16[2,256,768]{2,1,0:T(8,128)(2,1)S(1)} async-done(((bf16[2,256,768]{2,1,0:T(8,128)(2,1)}), bf16[2,256,768]{2,1,0:T(8,128)(2,1)S(1)}, u32[]{:S(2)}, u32[]{:S(2)}) %all-to-all-start) | async-done | bytes 786464 | tf_op jit(solution)/shard_map/all_to_all | solution.py:104
  116.3 4.3 fusion.76
  124.8 9.6 %convolution_bitcast_fusion = f32[1,512,12,768]{3,1,2,0:T(8,128)} fusion(bf16[512,12,64]{0,2,1:T(8,128)(2,1)S(1)} %bitcast.191, bf16[12,64,768]{2,1,0:T(8,128)(2,1)} %bitcast.208), kind=kOutput, calls=%fused_computation.19 | convolution fusion | flops 603979776 | bytes 20840448 | tf_op jit(solution)/shard_map/pqhd,hdc->pqhc/dot_general | solution.py:127
  134.4 15.8 %fusion.26 = (bf16[512,12,192]{2,0,1:T(8,128)(2,1)}, bf16[512,12,192]{2,0,1:T(8,128)(2,1)}, bf16[512,12,192]{2,0,1:T(8,128)(2,1)}, bf16[512,12,192]{2,0,1:T(8,128)(2,1)}) fusion(f32[1,512,12,768]{3,1,2,0:T(8,128)} %convolution_bitcast_fusion, f32[512,192]{1,0:T(8,128)S(1)} %copy-done.14, f32[512,192]{1,0:T(8,128)S(1)} %get-tuple-element.69, ...), kind=kLoop, calls=%fused_computation.55 | loop fusion | flops 18874368 | bytes 29884416 | tf_op jit(solution)/shard_map/concatenate | solution.py:30
  150.3 12.7 %fusion.5 = f32[512,512,12]{1,0,2:T(8,128)} fusion(bf16[512,12,192]{2,0,1:T(8,128)(2,1)} %get-tuple-element.64, bf16[512,12,192]{2,0,1:T(8,128)(2,1)} %get-tuple-element.65, bf16[512,12,192]{2,0,1:T(8,128)(2,1)} %get-tuple-element.59, bf16[512,12,192]{2,0,1:T(8,128)(2,1)} %get-tuple-element.58, bf16[512,192]{1,0:T(8,128)(2,1)} %get-tuple-element.91, ...), kind=kOutput, calls=%fused_computation.10 | convolution fusion | flops 4872732672 | bytes 22806528 | tf_op jit(solution)/shard_map/pqhc,pkc->phqk/dot_general | solution.py:132
  163.0 6.3 fusion.73
  169.3 1.8 fusion.4
  171.1 2.9 copy-done
  174.0 2.5 fusion.25
  176.5 2.6 copy-done.1
  179.2 2.0 bitcast_convert_fusion
  181.2 2.6 fusion.74
  185.3 12.2 %all-gather.12.cloned.1.call-done = bf16[768,3072]{1,0:T(8,128)(2,1)} async-done(((bf16[48,3072]{1,0:T(8,128)(2,1)}), bf16[768,3072]{1,0:T(8,128)(2,1)}) %all-gather.12.cloned.1.call-update) | async-done | bytes 4718608 | tf_op jit(solution)/shard_map/all_gather | solution.py:86
  197.5 20.8 %multiply_convert_fusion = (bf16[512,3072]{1,0:T(8,128)(2,1)}, f32[512,3072]{1,0:T(8,128)}, f32[512,3072]{1,0:T(8,128)}) fusion(f32[3072]{0:T(1024)S(1)} %slice.70, bf16[768,3072]{1,0:T(8,128)(2,1)} %all-gather.12.cloned.1.call-done, f32[512,768]{1,0:T(8,128)} %copy-done.9, f32[768]{0:T(1024)S(1)} %get-tuple-element.77, f32[768]{0:T(1024)S(1)} %get-tuple-element.76, ...), kind=kOutput, calls=%fused_computation.32 | convolution fusion | flops 2521694208 | bytes 22042624 | tf_op jit(solution)/shard_map/dot_general | solution.py:81
  218.3 33.2 %all-gather.14.cloned.1.call-done = bf16[3072,768]{1,0:T(8,128)(2,1)} async-done(((bf16[192,768]{1,0:T(8,128)(2,1)}), bf16[3072,768]{1,0:T(8,128)(2,1)}) %all-gather.14.cloned.1.call-update) | async-done | bytes 4718608 | tf_op jit(solution)/shard_map/all_gather | solution.py:86
  251.5 6.6 fusion.75
  259.7 2.1 convert_reduce_fusion.2
  261.9 10.5 %convert_reduce_fusion = (f32[3072]{0:T(1024)}, bf16[512,3072]{1,0:T(8,128)(2,1)}) fusion(f32[512,3072]{1,0:T(8,128)} %get-tuple-element.53, bf16[3072,768]{1,0:T(8,128)(2,1)S(1)} %bitcast.232, f32[512,768]{1,0:T(8,128)S(1)} %get-tuple-element.49, f32[512,3072]{1,0:T(8,128)} %get-tuple-element.101, f32[3072]{0:T(1024)S(1)} %slice.70), kind=kOutput, calls=%fused_computation.26 | convolution fusion | flops 2443047936 | bytes 22044672 | tf_op jit(solution)/shard_map/dot_general | solution.py:81
  272.4 5.7 multiply_reduce_fusion
  280.3 1.7 convolution_convert_fusion.5
  282.1 2.3 copy.72
  285.9 6.9 fusion.14
  292.8 2.7 copy-done.2
  295.5 9.3 %multiply_bitcast_fusion = f32[1,512,12,768]{3,1,2,0:T(8,128)} fusion(bf16[12,512,512]{1,2,0:T(8,128)(2,1)S(1)} %fusion.14, bf16[512,192]{1,0:T(8,128)(2,1)S(1)} %copy-done.28, bf16[512,192]{1,0:T(8,128)(2,1)S(1)} %copy-done.29, bf16[512,192]{1,0:T(8,128)(2,1)S(1)} %copy-done.27, bf16[512,192]{1,0:T(8,128)(2,1)S(1)} %copy-done.26), kind=kOutput, calls=%fused_computation | convolution fusion | flops 4839702528 | bytes 25952256 | tf_op jit(solution)/shard_map/phqk,pkc->pqhc/dot_general | solution.py:165
  304.8 14.6 %fusion.30 = (bf16[512,12,192]{2,0,1:T(8,128)(2,1)S(1)}, bf16[512,12,192]{2,0,1:T(8,128)(2,1)S(1)}, bf16[512,12,192]{2,0,1:T(8,128)(2,1)}, bf16[512,12,192]{2,0,1:T(8,128)(2,1)}) fusion(f32[1,512,12,768]{3,1,2,0:T(8,128)} %multiply_bitcast_fusion, f32[512,192]{1,0:T(8,128)S(1)} %copy-done.15, f32[512,192]{1,0:T(8,128)S(1)} %get-tuple-element.69, ...), kind=kLoop, calls=%fused_computation.59 | loop fusion | flops 18874368 | bytes 29884416 | tf_op jit(solution)/shard_map/concatenate | solution.py:44
  319.5 10.1 %convolution_convert_fusion.4 = bf16[12,64,768]{2,1,0:T(8,128)(2,1)} fusion(bf16[512,12,64]{0,2,1:T(8,128)(2,1)S(1)} %bitcast.193, bf16[512,12,192]{2,0,1:T(8,128)(2,1)} %get-tuple-element.62, bf16[512,12,192]{2,0,1:T(8,128)(2,1)} %get-tuple-element.63, bf16[512,12,192]{2,0,1:T(8,128)(2,1)S(1)} %get-tuple-element.55, ...), kind=kOutput, calls=%fused_computation.102 | convolution fusion | flops 642318336 | bytes 11403264 | tf_op jit(solution)/shard_map/pqhd,pqhc->hdc/dot_general | solution.py:172
  329.7 3.6 convolution_convert_fusion.3
  333.3 6.2 convert_reduce_fusion.4
  339.5 2.9 multiply_convert_fusion.1
  342.5 4.5 fusion.77
  348.7 8.3 %convert_reduce_fusion.5 = (f32[12,64]{1,0:T(8,128)}, bf16[1,512,12,64]{1,3,2,0:T(8,128)(2,1)}) fusion(bf16[12,64,768]{2,1,0:T(8,128)(2,1)S(1)} %bitcast.209, bf16[512,12,192]{2,0,1:T(8,128)(2,1)S(1)} %copy-done.20, bf16[512,12,192]{2,0,1:T(8,128)(2,1)} %get-tuple-element.63, bf16[512,12,192]{2,0,1:T(8,128)(2,1)S(1)} %copy-done.19, ...), kind=kOutput, calls=%fused_computation.90 | convolution fusion | flops 643693824 | bytes 12979200 | tf_op jit(solution)/shard_map/pqhc,hdc->pqhd/dot_general | solution.py:169
  357.0 3.8 fusion.24
  360.9 4.1 copy.99
  365.0 7.2 convolution_convert_fusion
  373.6 6.5 convolution_convert_fusion.1
  380.2 6.1 reduce-scatter.21.cloned.1.call-done
  388.1 58.9 %reduce-scatter.23.cloned.1.call-done = bf16[48,768]{1,0:T(8,128)(2,1)} async-done(((bf16[768,768]{1,0:T(8,128)(2,1)}), bf16[48,768]{1,0:T(8,128)(2,1)}) %reduce-scatter.23.cloned.1.call-update) | async-done | bytes 73744 | tf_op jit(solution)/shard_map/reduce_scatter | solution.py:90
  449.0 69.0 %reduce-scatter.31.cloned.1.call-done = bf16[48,2304]{1,0:T(8,128)(2,1)} async-done(((bf16[768,2304]{1,0:T(8,128)(2,1)}), bf16[48,2304]{1,0:T(8,128)(2,1)}) %reduce-scatter.31.cloned.1.call-update) | async-done | bytes 221200
  518.0 2.0 copy.100
  520.0 2.5 copy.112
  523.0 6.3 reduce.13
  529.3 2.1 reshape.594
  531.4 3.6 all-to-all-start.2
  535.0 61.3 %reduce-scatter.29.cloned.1.call-done = bf16[192,768]{1,0:T(8,128)(2,1)} async-done(((bf16[3072,768]{1,0:T(8,128)(2,1)}), bf16[192,768]{1,0:T(8,128)(2,1)}) %reduce-scatter.29.cloned.1.call-update) | async-done | bytes 294928 | tf_op jit(solution)/shard_map/reduce_scatter | solution.py:90
  596.3 1.9 copy.105
  598.2 4.8 add_bitcast_fusion
  603.1 2.8 copy.80
  606.0 3.7 all-to-all-start.4
  609.8 65.3 %reduce-scatter.25.cloned.1.call-done = bf16[48,3072]{1,0:T(8,128)(2,1)} async-done(((bf16[768,3072]{1,0:T(8,128)(2,1)}), bf16[48,3072]{1,0:T(8,128)(2,1)}) %reduce-scatter.25.cloned.1.call-update) | async-done | bytes 294928 | tf_op jit(solution)/shard_map/reduce_scatter | solution.py:90
  675.3 39.8 %all-reduce.1 = f32[9216]{0:T(1024)S(1)} all-reduce(f32[9216]{0:T(1024)S(1)} %constant_dynamic-update-slice_fusion), channel_id=12, replica_groups=mesh['dp'=16,'blk'=2] {'dp','blk'}, use_global_device_ids=true, to_apply=%region_29.30.clone | all-reduce | flops 9216 | bytes 73728
  723.0 1.8 copy.81
  724.8 10.3 %reduce-scatter.37.cloned.1.call-done = bf16[384,192]{1,0:T(8,128)(2,1)} async-done(((bf16[768,192]{1,0:T(8,128)(2,1)}), bf16[384,192]{1,0:T(8,128)(2,1)}) %reduce-scatter.37.cloned.1.call-update) | async-done | bytes 147472
  736.9 12.3 %reduce-scatter.27.cloned.1.call-done = bf16[48,1536]{1,0:T(8,128)(2,1)} async-done(((bf16[48,3072]{1,0:T(8,128)(2,1)}), bf16[48,1536]{1,0:T(8,128)(2,1)}) %reduce-scatter.27.cloned.1.call-update) | async-done | bytes 147472 | tf_op jit(solution)/shard_map/reduce_scatter | solution.py:91
  (194 shorter events, 37.3 us)
Async XLA Ops:
  7.2 109.1 %all-gather.6.cloned.1.call-start = ((), (), s32[]{:S(2)}) async-start(), calls=%async_computation.15 | async-start | bytes 3760128 | tf_op jit(solution)/shard_map/all_gather | solution.py:86
  15.8 109.0 %all-gather.8.cloned.1.call-start = ((), (), s32[]{:S(2)}) async-start(), calls=%async_computation.16 | async-start | bytes 1253376 | tf_op jit(solution)/shard_map/all_gather | solution.py:86
  20.8 160.4 %all-gather.10.cloned.1.call-start = ((), (), s32[]{:S(2)}) async-start(), calls=%async_computation.17 | async-start | bytes 1253376 | tf_op jit(solution)/shard_map/all_gather | solution.py:86
  26.5 171.0 %all-gather.12.cloned.1.call-start = ((), (), s32[]{:S(2)}) async-start(), calls=%async_computation.18 | async-start | bytes 5013504 | tf_op jit(solution)/shard_map/all_gather | solution.py:86
  34.2 53.7 %all-to-all-start.1 = ((s32[2,2,256]{2,0,1:T(2,128)}), s32[2,2,256]{2,0,1:T(2,128)S(1)}, u32[]{:S(2)}, u32[]{:S(2)}) async-start(s32[2,2,256]{2,0,1:T(2,128)} %copy.69), calls=%async_computation.1 | async-start | bytes 8192 | tf_op jit(solution)/shard_map/all_to_all | solution.py:105
  37.5 214.0 %all-gather.14.cloned.1.call-start = ((), (), s32[]{:S(2)}) async-start(), calls=%async_computation.19 | async-start | bytes 5013504 | tf_op jit(solution)/shard_map/all_gather | solution.py:86
  86.0 165.5 %copy-start.38 = (f32[768]{0:T(1024)}, f32[768]{0:T(1024)S(1)}, u32[]{:S(2)}) copy-start(f32[768]{0:T(1024)S(1)} %get-tuple-element.77) | copy-start | bytes 9220
  87.9 14.3 %all-to-all-start.3 = ((bf16[2,256,768]{2,1,0:T(8,128)(2,1)}), bf16[2,256,768]{2,1,0:T(8,128)(2,1)S(1)}, u32[]{:S(2)}, u32[]{:S(2)}) async-start(bf16[2,256,768]{2,1,0:T(8,128)(2,1)} %param.19), calls=%async_computation.3 | async-start | bytes 1572864 | tf_op jit(solution)/shard_map/all_to_all | solution.py:113
  100.5 49.8 %copy-start.25 = (bf16[512,192]{1,0:T(8,128)(2,1)}, bf16[512,192]{1,0:T(8,128)(2,1)S(1)}, u32[]{:S(2)}) copy-start(bf16[512,192]{1,0:T(8,128)(2,1)S(1)} %get-tuple-element.83) | copy-start | bytes 589828
  102.0 32.4 %copy-start.12 = (f32[512,192]{1,0:T(8,128)}, f32[512,192]{1,0:T(8,128)S(1)}, u32[]{:S(2)}) copy-start(f32[512,192]{1,0:T(8,128)S(1)} %get-tuple-element.71) | copy-start | bytes 1179652
  102.2 18.4 %copy-start.3 = (bf16[2,256,768]{2,1,0:T(8,128)(2,1)}, bf16[2,256,768]{2,1,0:T(8,128)(2,1)S(1)}, u32[]{:S(2)}) copy-start(bf16[2,256,768]{2,1,0:T(8,128)(2,1)S(1)} %all-to-all-done.3) | copy-start | bytes 2359300
  102.2 14.1 %all-to-all-start = ((bf16[2,256,768]{2,1,0:T(8,128)(2,1)}), bf16[2,256,768]{2,1,0:T(8,128)(2,1)S(1)}, u32[]{:S(2)}, u32[]{:S(2)}) async-start(bf16[2,256,768]{2,1,0:T(8,128)(2,1)} %param.10), calls=%async_computation | async-start | bytes 1572864 | tf_op jit(solution)/shard_map/all_to_all | solution.py:104
  105.7 280.6 %reduce-scatter.21.cloned.1.call-start = ((), (), s32[]{:S(2)}) async-start(), calls=%async_computation.21 | async-start | bytes 1253376 | tf_op jit(solution)/shard_map/reduce_scatter | solution.py:90
  116.3 4.3 copy-start.24
  124.8 38.2 %copy-start.5 = (bf16[512,768]{0,1:T(8,128)(2,1)}, bf16[512,768]{0,1:T(8,128)(2,1)S(1)}, u32[]{:S(2)}) copy-start(bf16[512,768]{0,1:T(8,128)(2,1)S(1)} %copy.68) | copy-start | bytes 2359300
  124.8 9.6 %copy-start.14 = (f32[512,192]{1,0:T(8,128)S(1)}, f32[512,192]{1,0:T(8,128)}, u32[]{:S(2)}) copy-start(f32[512,192]{1,0:T(8,128)} %get-tuple-element.72) | copy-start | bytes 1179652
  169.3 4.7 copy-start
  174.0 5.1 copy-start.6
  176.5 2.7 copy-start.1
  185.3 92.8 %copy-start.35 = (f32[512]{0:T(512)}, f32[512]{0:T(512)S(1)}, u32[]{:S(2)}) copy-start(f32[512]{0:T(512)S(1)} %add_rsqrt_fusion.1) | copy-start | bytes 6148
  251.5 10.4 %slice-start.4 = ((s8[4718592]{0:T(1024)(128)(4,1)}), s8[4194304]{0:T(1024)(128)(4,1)S(1)}, s32[]{:S(2)}) async-start(s8[4718592]{0:T(1024)(128)(4,1)} %bitcast.231), calls=%async_computation.34 | async-start | bytes 8388608
  251.5 7.0 copy-start.4
  251.5 10.4 %slice-start.5 = ((s8[4718592]{0:T(1024)(128)(4,1)}), s8[524288]{0:T(1024)(128)(4,1)S(1)}, s32[]{:S(2)}) async-start(s8[4718592]{0:T(1024)(128)(4,1)} %bitcast.231), calls=%async_computation.35 | async-start | bytes 1048576
  259.7 12.6 %slice-start.2 = ((s8[4718592]{0:T(1024)(128)(4,1)}), s8[4194304]{0:T(1024)(128)(4,1)S(1)}, s32[]{:S(2)}) async-start(s8[4718592]{0:T(1024)(128)(4,1)} %bitcast.229), calls=%async_computation.32 | async-start | bytes 8388608
  261.8 10.5 %copy-start.22 = (f32[512,768]{1,0:T(8,128)}, f32[512,768]{1,0:T(8,128)S(1)}, u32[]{:S(2)}) copy-start(f32[512,768]{1,0:T(8,128)S(1)} %get-tuple-element.49) | copy-start | bytes 4718596
  261.9 10.5 %copy-start.10 = (f32[512,768]{1,0:T(8,128)S(1)}, f32[512,768]{1,0:T(8,128)}, u32[]{:S(2)}) copy-start(f32[512,768]{1,0:T(8,128)} %copy-done.9) | copy-start | bytes 4718596
  261.9 10.5 %slice-start.3 = ((s8[4718592]{0:T(1024)(128)(4,1)}), s8[524288]{0:T(1024)(128)(4,1)S(1)}, s32[]{:S(2)}) async-start(s8[4718592]{0:T(1024)(128)(4,1)} %bitcast.229), calls=%async_computation.33 | async-start | bytes 1048576
  278.1 2.2 copy-start.42
  285.8 9.6 %copy-start.26 = (bf16[512,192]{1,0:T(8,128)(2,1)S(1)}, bf16[512,192]{1,0:T(8,128)(2,1)}, u32[]{:S(2)}) copy-start(bf16[512,192]{1,0:T(8,128)(2,1)} %copy-done.25) | copy-start | bytes 589828
  285.8 9.6 %copy-start.27 = (bf16[512,192]{1,0:T(8,128)(2,1)S(1)}, bf16[512,192]{1,0:T(8,128)(2,1)}, u32[]{:S(2)}) copy-start(bf16[512,192]{1,0:T(8,128)(2,1)} %get-tuple-element.84) | copy-start | bytes 589828
  285.8 9.6 %copy-start.28 = (bf16[512,192]{1,0:T(8,128)(2,1)S(1)}, bf16[512,192]{1,0:T(8,128)(2,1)}, u32[]{:S(2)}) copy-start(bf16[512,192]{1,0:T(8,128)(2,1)} %get-tuple-element.91) | copy-start | bytes 589828
  285.8 9.6 %copy-start.29 = (bf16[512,192]{1,0:T(8,128)(2,1)S(1)}, bf16[512,192]{1,0:T(8,128)(2,1)}, u32[]{:S(2)}) copy-start(bf16[512,192]{1,0:T(8,128)(2,1)} %get-tuple-element.92) | copy-start | bytes 589828
  292.8 2.7 copy-start.2
  295.5 9.4 %copy-start.13 = (f32[512,192]{1,0:T(8,128)S(1)}, f32[512,192]{1,0:T(8,128)}, u32[]{:S(2)}) copy-start(f32[512,192]{1,0:T(8,128)} %copy-done.12) | copy-start | bytes 1179652
  295.5 9.4 %copy-start.15 = (f32[512,192]{1,0:T(8,128)S(1)}, f32[512,192]{1,0:T(8,128)}, u32[]{:S(2)}) copy-start(f32[512,192]{1,0:T(8,128)} %get-tuple-element.72) | copy-start | bytes 1179652
  319.4 10.1 %copy-start.16 = (bf16[512,12,192]{2,0,1:T(8,128)(2,1)}, bf16[512,12,192]{2,0,1:T(8,128)(2,1)S(1)}, u32[]{:S(2)}) copy-start(bf16[512,12,192]{2,0,1:T(8,128)(2,1)S(1)} %get-tuple-element.54) | copy-start | bytes 7077892
  319.4 10.2 %copy-start.18 = (bf16[512,12,192]{2,0,1:T(8,128)(2,1)}, bf16[512,12,192]{2,0,1:T(8,128)(2,1)S(1)}, u32[]{:S(2)}) copy-start(bf16[512,12,192]{2,0,1:T(8,128)(2,1)S(1)} %get-tuple-element.55) | copy-start | bytes 7077892
  329.6 117.3 %reduce-scatter.23.cloned.1.call-start = ((), (), s32[]{:S(2)}) async-start(), calls=%async_computation.22 | async-start | bytes 1253376 | tf_op jit(solution)/shard_map/reduce_scatter | solution.py:90
  329.7 9.8 %slice-start = ((s8[6291456]{0:T(1024)(128)(4,1)}), s8[2097152]{0:T(1024)(128)(4,1)S(1)}, s32[]{:S(2)}) async-start(s8[6291456]{0:T(1024)(128)(4,1)} %bitcast.189), calls=%async_computation.30 | async-start | bytes 4194304
  333.3 6.2 slice-start.1
  342.4 4.6 copy-start.17
  342.4 175.6 %reduce-scatter.31.cloned.1.call-start = ((), (), s32[]{:S(2)}) async-start(), calls=%async_computation.26 | async-start | bytes 3760128
  342.5 5.0 copy-start.19
  342.5 5.9 copy-start.20
  342.5 6.2 copy-start.23
  364.9 231.4 %reduce-scatter.29.cloned.1.call-start = ((), (), s32[]{:S(2)}) async-start(), calls=%async_computation.25 | async-start | bytes 5013504 | tf_op jit(solution)/shard_map/reduce_scatter | solution.py:90
  372.3 302.8 %reduce-scatter.25.cloned.1.call-start = ((), (), s32[]{:S(2)}) async-start(), calls=%async_computation.23 | async-start | bytes 5013504 | tf_op jit(solution)/shard_map/reduce_scatter | solution.py:90
  380.2 339.6 %reduce-scatter.33.cloned.1.call-start = ((), (), s32[]{:S(2)}) async-start(), calls=%async_computation.27 | async-start | bytes 294912
  388.0 333.3 %reduce-scatter.35.cloned.1.call-start = ((), (), s32[]{:S(2)}) async-start(), calls=%async_computation.28 | async-start | bytes 294912
  448.7 274.3 %reduce-scatter.19.cloned.1.call-start = ((), (), s32[]{:S(2)}) async-start(), calls=%async_computation.20 | async-start | bytes 884736 | tf_op jit(solution)/shard_map/reduce_scatter | solution.py:91
  520.0 78.2 %copy-start.8 = (f32[512,768]{1,0:T(8,128)S(1)}, f32[512,768]{1,0:T(8,128)}, u32[]{:S(2)}) copy-start(f32[512,768]{1,0:T(8,128)} %copy-done.7) | copy-start | bytes 4718596
  531.4 74.6 %all-to-all-start.2 = ((bf16[2,2,98304]{2,1,0:T(2,128)(2,1)}), bf16[2,2,98304]{2,1,0:T(2,128)(2,1)S(1)}, u32[]{:S(2)}, u32[]{:S(2)}) async-start(bf16[2,2,98304]{2,1,0:T(2,128)(2,1)} %reshape.594), calls=%async_computation.2 | async-start | bytes 1572864 | tf_op jit(solution)/shard_map/all_to_all | solution.py:185
  534.9 200.1 %reduce-scatter.37.cloned.1.call-start = ((), (), s32[]{:S(2)}) async-start(), calls=%async_computation.29 | async-start | bytes 589824
  598.2 7.6 %copy-start.37 = (f32[12,64]{1,0:T(8,128)S(1)}, f32[12,64]{1,0:T(8,128)}, u32[]{:S(2)}) copy-start(f32[12,64]{1,0:T(8,128)} %get-tuple-element.105) | copy-start | bytes 9220
  603.0 6.8 copy-start.32
  603.0 72.1 %copy-start.41 = (f32[768]{0:T(1024)S(1)}, f32[768]{0:T(1024)}, u32[]{:S(2)}) copy-start(f32[768]{0:T(1024)} %get-tuple-element.40) | copy-start | bytes 9220
  603.0 72.1 %copy-start.40 = (f32[768]{0:T(1024)S(1)}, f32[768]{0:T(1024)}, u32[]{:S(2)}) copy-start(f32[768]{0:T(1024)} %get-tuple-element.45) | copy-start | bytes 9220
  603.0 72.1 %copy-start.34 = (f32[3072]{0:T(1024)S(1)}, f32[3072]{0:T(1024)}, u32[]{:S(2)}) copy-start(f32[3072]{0:T(1024)} %get-tuple-element.109) | copy-start | bytes 36868
  603.0 72.2 %copy-start.33 = (f32[768]{0:T(1024)S(1)}, f32[768]{0:T(1024)}, u32[]{:S(2)}) copy-start(f32[768]{0:T(1024)} %get-tuple-element.48) | copy-start | bytes 9220
  603.1 72.2 %copy-start.31 = (f32[768]{0:T(1024)S(1)}, f32[768]{0:T(1024)}, u32[]{:S(2)}) copy-start(f32[768]{0:T(1024)} %get-tuple-element.42) | copy-start | bytes 9220
  603.1 72.2 %copy-start.30 = (f32[768]{0:T(1024)S(1)}, f32[768]{0:T(1024)}, u32[]{:S(2)}) copy-start(f32[768]{0:T(1024)} %get-tuple-element.46) | copy-start | bytes 9220
  606.0 109.1 %copy-start.21 = (bf16[2,2,98304]{2,1,0:T(2,128)(2,1)}, bf16[2,2,98304]{2,1,0:T(2,128)(2,1)S(1)}, u32[]{:S(2)}) copy-start(bf16[2,2,98304]{2,1,0:T(2,128)(2,1)S(1)} %all-to-all-done.2) | copy-start | bytes 2359300
  606.0 112.5 %all-to-all-start.4 = ((f32[1,512,768]{2,0,1:T(1,128)}), f32[1,512,768]{2,0,1:T(1,128)S(1)}, u32[]{:S(2)}, u32[]{:S(2)}) async-start(f32[1,512,768]{2,0,1:T(1,128)} %copy.80), calls=%async_computation.4 | async-start | bytes 3145728 | tf_op jit(solution)/shard_map/all_to_all | solution.py:186
  609.8 139.5 %reduce-scatter.27.cloned.1.call-start = ((), (), s32[]{:S(2)}) async-start(), calls=%async_computation.24 | async-start | bytes 442368 | tf_op jit(solution)/shard_map/reduce_scatter | solution.py:91
  (5 other events, 6.5 us)
Sparse Core Ops, SparseCore 0:
  15.9 47.8 all-gather.5
  66.1 37.4 all-gather.7
  105.9 37.2 all-gather.9
  145.3 52.1 all-gather.11
  199.7 51.7 all-gather.13
  329.7 56.4 reduce-scatter.20
  389.9 57.0 reduce-scatter.22
  450.8 67.0 reduce-scatter.30
  521.8 74.4 reduce-scatter.28
  600.5 74.5 reduce-scatter.24
  677.9 10.0 reduce-scatter.32
  690.6 11.0 reduce-scatter.34
  704.0 15.7 reduce-scatter.18
  721.9 13.1 reduce-scatter.36
  737.2 12.0 reduce-scatter.26

commit v2 on v1

--- a/solution.py
+++ b/solution.py
@@ -3,7 +3,10 @@
 
 import jax
 import jax.numpy as jnp
+import numpy as np
 from jax import lax
+from jax.experimental import pallas as pl
+from jax.experimental.pallas import tpu as pltpu
 from jax.sharding import PartitionSpec as P
 
 HEADS = 12
@@ -193,6 +196,707 @@
     )
 
 
+MESH = pl.DeviceIdType.MESH
+WEIGHTS = ("qkv", "box", "out", "up", "down")
+ROT = 4
+ALL = slice(None)
+
+
+def by_columns(name, height, first, left, right):
+    return (
+        name,
+        (0, height, first, left),
+        (0, height, first + left, right),
+        (0, height, first, left + right),
+    )
+
+
+def by_rows(name, height, first, count):
+    half = height // 2
+    return (
+        name,
+        (0, half, first, count),
+        (half, half, first, count),
+        (0, height, first, count),
+    )
+
+
+def window(piece):
+    return (pl.ds(piece[0], piece[1]), pl.ds(piece[2], piece[3]))
+
+
+class Place:
+    def __init__(self, depth):
+        self.depth = depth
+        dp = lax.axis_index("dp")
+        self.y = lax.axis_index("blk")
+        self.z = lax.div(dp, 4)
+        self.x = lax.rem(lax.div(dp, 2), 2)
+        self.c = lax.rem(dp, 2)
+        x, y, z, c = self.x, self.y, self.z, self.c
+        self.z_peers = [(lax.rem(z + k, depth) * 4 + x * 2 + c, y) for k in range(1, depth)]
+        self.z_from = [lax.rem(z + depth - k, depth) for k in range(1, depth)]
+        self.x_peer = (dp + 2 - 4 * x, y)
+        self.y_peer = (dp, 1 - y)
+        self.c_peer = (dp + 1 - 2 * c, y)
+
+    def greet(self):
+        barrier = pltpu.get_barrier_semaphore()
+        peers = self.z_peers + [self.x_peer, self.y_peer, self.c_peer]
+        for peer in peers:
+            pl.semaphore_signal(barrier, inc=1, device_id=peer, device_id_type=MESH)
+        pl.semaphore_wait(barrier, len(peers))
+
+
+def remote(src, dst, sems, at, peer):
+    return pltpu.make_async_remote_copy(
+        src, dst, sems[0].at[at], sems[1].at[at], device_id=peer, device_id_type=MESH
+    )
+
+
+class Gather:
+    def __init__(self, place, groups, shards, full, z_sems, xy_sems, c_sems, own_sem):
+        self.place, self.groups, self.shards, self.full = place, groups, shards, full
+        self.z_sems, self.xy_sems, self.c_sems, self.own_sem = z_sems, xy_sems, c_sems, own_sem
+        self.count = len(groups)
+
+    def z_copy(self, g, k, arriving=False):
+        p = self.place
+        name, _, _, both = self.groups[g]
+        cut = window(both)
+        z = p.z_from[k] if arriving else p.z
+        return remote(
+            self.shards[name].at[cut],
+            self.full[name].at[(p.y, z, p.x, p.c) + cut],
+            self.z_sems,
+            (g, k),
+            p.z_peers[k],
+        )
+
+    def own_copy(self, g):
+        p = self.place
+        name, _, _, both = self.groups[g]
+        cut = window(both)
+        return pltpu.make_async_copy(
+            self.shards[name].at[cut],
+            self.full[name].at[(p.y, p.z, p.x, p.c) + cut],
+            self.own_sem.at[g],
+        )
+
+    def xy_copy(self, g, i, arriving=False):
+        p = self.place
+        name, left, right, _ = self.groups[g]
+        a, b = window(left), window(right)
+        y = 1 - p.y if arriving else p.y
+        x = 1 - p.x if arriving else p.x
+        index, peer = (
+            ((y, ALL, p.x, p.c) + b, p.y_peer),
+            ((p.y, ALL, x, p.c) + a, p.x_peer),
+            ((y, ALL, ALL, p.c) + a, p.y_peer),
+            ((ALL, ALL, x, p.c) + b, p.x_peer),
+        )[i]
+        ref = self.full[name].at[index]
+        return remote(ref, ref, self.xy_sems, (g, i), peer)
+
+    def c_copy(self, g, arriving=False):
+        p = self.place
+        name, _, _, both = self.groups[g]
+        c = 1 - p.c if arriving else p.c
+        ref = self.full[name].at[(ALL, ALL, ALL, c) + window(both)]
+        return remote(ref, ref, self.c_sems, (g,), p.c_peer)
+
+    def start(self, g):
+        for k in range(self.place.depth - 1):
+            self.z_copy(g, k).start()
+        self.own_copy(g).start()
+
+    def first(self, g):
+        self.own_copy(g).wait()
+        for k in range(self.place.depth - 1):
+            self.z_copy(g, k, True).wait_recv()
+        self.xy_copy(g, 0).start()
+        self.xy_copy(g, 1).start()
+
+    def second(self, g):
+        self.xy_copy(g, 1, True).wait_recv()
+        self.xy_copy(g, 2).start()
+        self.xy_copy(g, 0, True).wait_recv()
+        self.xy_copy(g, 3).start()
+
+    def third(self, g):
+        self.xy_copy(g, 2, True).wait_recv()
+        self.xy_copy(g, 3, True).wait_recv()
+        self.c_copy(g).start()
+
+    def ready(self, g):
+        self.c_copy(g, True).wait_recv()
+
+    def ticks(self, ahead):
+        out = [[partial(self.start, g) for g in range(min(ahead, self.count))]]
+        for t in range(self.count + 3):
+            tick = []
+            if t < self.count:
+                if t + ahead < self.count:
+                    tick.append(partial(self.start, t + ahead))
+                tick.append(partial(self.first, t))
+            if 0 <= t - 1 < self.count:
+                tick.append(partial(self.second, t - 1))
+            if 0 <= t - 2 < self.count:
+                tick.append(partial(self.third, t - 2))
+            if 0 <= t - 3 < self.count:
+                tick.append(partial(self.ready, t - 3))
+            out.append(tick)
+        return out
+
+    def drain(self):
+        for g in range(self.count):
+            for k in range(self.place.depth - 1):
+                self.z_copy(g, k).wait_send()
+            for i in range(4):
+                self.xy_copy(g, i).wait_send()
+            self.c_copy(g).wait_send()
+
+
+def sine_cosine(angle):
+    turns = jnp.floor(angle * (2.0 / math.pi) + 0.5)
+    rest = angle - turns * 1.5703125
+    rest = rest - turns * 4.837512969970703125e-4
+    rest = rest - turns * 7.54978995489188216e-8
+    square = rest * rest
+    sine = rest + rest * square * (
+        -1.6666654611e-1 + square * (8.3321608736e-3 + square * -1.9515295891e-4)
+    )
+    cosine = (
+        1.0
+        - 0.5 * square
+        + square
+        * square
+        * (
+            4.166664568298827e-2
+            + square * (-1.388731625493765e-3 + square * 2.443315711809948e-5)
+        )
+    )
+    quarter = turns.astype(jnp.int32)
+    odd = (quarter & 1) == 1
+    sine_sign = jnp.where((quarter & 2) == 2, -1.0, 1.0)
+    cosine_sign = jnp.where(((quarter + 1) & 2) == 2, -1.0, 1.0)
+    return (
+        sine_sign * jnp.where(odd, cosine, sine),
+        cosine_sign * jnp.where(odd, sine, cosine),
+    )
+
+
+def dot_t(a, b):
+    return lax.dot_general(a, b, (((1,), (1,)), ((), ())), preferred_element_type=jnp.float32)
+
+
+def dot_n(a, b):
+    return lax.dot_general(a, b, (((0,), (0,)), ((), ())), preferred_element_type=jnp.float32)
+
+
+def lanes(start, size):
+    return pl.ds(pl.multiple_of(start, 128), size)
+
+
+BQ, BV, BO, G1, E1, B1, B2, G2, E2 = 0, 768, 1536, 2304, 3072, 3840, 6912, 7680, 8448
+VECTORS = 9216
+
+
+def forward_kernel(plan, *refs):
+    depth, groups, page_len, width = plan
+    block = page_len // 2
+    refs = iter(refs)
+    take = lambda n: [next(refs) for _ in range(n)]
+    tokens, cotangent, boxes, lengths, piece, frequency = take(6)
+    shards = dict(zip(WEIGHTS, take(5)))
+    full_out = dict(zip(WEIGHTS, take(5)))
+    (x_out, ct_out, qkv_out, table_out, p_out, o_out, unit1_out, inv1_out) = take(8)
+    (g_out, d_out, unit2_out, inv2_out, vec_out) = take(5)
+    full = dict(zip(WEIGHTS, take(5)))
+    (x_own, boxes_peer, pieces, vec, qkv, table, keys, box_w, p_slots, o_own, o_low) = take(11)
+    (unit1, inv1, y1_low, hidden, slope, unit2, inv2) = take(7)
+    z_sems, xy_sems, c_sems = take(2), take(2), take(2)
+    (own_sem,) = take(1)
+    vz_sems, vxy_sems, vc_sems = take(2), take(2), take(2)
+    ex_sems = take(2)
+    (local_sem, p_sem, out_sem) = take(3)
+
+    place = Place(depth)
+    y, z, x, c = place.y, place.z, place.x, place.c
+    gather = Gather(place, groups, shards, full, z_sems, xy_sems, c_sems, own_sem)
+
+    def swap(i, source, target, arriving=False):
+        at = (1 - y) if arriving else y
+        return remote(
+            source.at[1 - y], target.at[pl.ds(pl.multiple_of(at * block, block), block)],
+            ex_sems, (i,), place.y_peer,
+        )
+
+    def keep(i, source, target):
+        return pltpu.make_async_copy(
+            source.at[y], target.at[pl.ds(pl.multiple_of(y * block, block), block)],
+            local_sem.at[i],
+        )
+
+    box_swap = remote(boxes, boxes_peer, ex_sems, (2,), place.y_peer)
+
+    def vector_z(k, arriving=False):
+        at = place.z_from[k] if arriving else z
+        return remote(piece, pieces.at[y, at, x, c], vz_sems, (k,), place.z_peers[k])
+
+    def vector_xy(i, arriving=False):
+        at_x = 1 - x if arriving else x
+        at_y = 1 - y if arriving else y
+        index = ((y, ALL, at_x, c), (at_y, ALL, ALL, c))[i]
+        ref = pieces.at[index]
+        return remote(ref, ref, vxy_sems, (i,), (place.x_peer, place.y_peer)[i])
+
+    def vector_c(arriving=False):
+        ref = pieces.at[:, :, :, 1 - c if arriving else c]
+        return remote(ref, ref, vc_sems, (0,), place.c_peer)
+
+    vector_own = pltpu.make_async_copy(piece, pieces.at[y, z, x, c], local_sem.at[2])
+
+    ready = [False] * gather.count
+    ticks = gather.ticks(AHEAD)
+    position = [0]
+
+    def tick(n=1):
+        for _ in range(n):
+            if position[0] < len(ticks):
+                for event in ticks[position[0]]:
+                    event()
+                position[0] += 1
+
+    def need(g):
+        while position[0] < g + 5:
+            tick()
+
+    outgoing = []
+
+    def send_out(ref, out):
+        copy = pltpu.make_async_copy(ref, out, out_sem.at[len(outgoing)])
+        copy.start()
+        outgoing.append(copy)
+
+    place.greet()
+    box_swap.start()
+    swap(0, tokens, x_own).start()
+    for k in range(depth - 1):
+        vector_z(k).start()
+    vector_own.start()
+    tick()
+    keep(0, tokens, x_own).start()
+    keep(1, cotangent, ct_out).start()
+
+    vector_own.wait()
+    for k in range(depth - 1):
+        vector_z(k, True).wait_recv()
+    vector_xy(0).start()
+    tick()
+    vector_xy(0, True).wait_recv()
+    vector_xy(1).start()
+
+    box_swap.wait_recv()
+    mine, other = boxes[...], boxes_peer[...]
+    first_block = y == 0
+    mine = jnp.where(first_block, mine[:, 0, :], mine[:, 1, :])
+    other = jnp.where(first_block, other[:, 0, :], other[:, 1, :])
+    both = jnp.concatenate(
+        [jnp.where(first_block, mine, other), jnp.where(first_block, other, mine)], axis=1
+    ).astype(jnp.float32)
+    both = jnp.concatenate([both, jnp.zeros((6, page_len), jnp.float32)], axis=0)
+    across_up = both.T
+    lane = lax.broadcasted_iota(jnp.int32, (1, 2 * FREQ), 1)
+    angle = jnp.where(lane < FREQ, across_up[:, 0:1], across_up[:, 1:2]) * frequency[...]
+    sine, cosine = sine_cosine(angle)
+    table[0], table[1] = cosine, sine
+    keys[0], keys[1] = cosine.astype(jnp.bfloat16), sine.astype(jnp.bfloat16)
+    send_out(table, table_out)
+    tick()
+    vector_xy(1, True).wait_recv()
+    vector_c().start()
+
+    keep(0, tokens, x_own).wait()
+    swap(0, tokens, x_own, True).wait_recv()
+    send_out(x_own, x_out)
+    tick()
+    vector_c(True).wait_recv()
+    vec[...] = jnp.zeros_like(vec)
+    for dz in range(depth):
+        for dx in range(2):
+            for dc in range(2):
+                for dy in range(2):
+                    device = ((dz * 2 + dx) * 2 + dc) * 2 + dy
+                    start = device * (VECTORS // (8 * depth)) // 128 * 128
+                    vec[:, start : start + 384] += pieces[dy, dz, dx, dc]
+    send_out(vec, vec_out)
+
+    def vector(start, size=width):
+        return vec[:, start : start + size]
+
+    def project(first, count):
+        def body(h, carry):
+            w = full["qkv"].at[h][:, :, :, :, first : first + count].reshape(width, count)
+            out = jnp.dot(x_own[...], w, preferred_element_type=jnp.float32)
+            start = pl.multiple_of(h * 1152 + first, 128)
+            column = start + lax.broadcasted_iota(jnp.int32, (1, count), 1)
+            bias = bias_qkv[:, lanes(start, count)]
+            qkv[:, lanes(start, count)] = (out + bias).astype(jnp.bfloat16)
+            return carry
+
+        lax.fori_loop(0, 2, body, 0)
+
+    bias_qkv = next(refs)
+    bias_qkv[:, 0:width] = vector(BQ)
+    bias_qkv[:, width : 2 * width] = jnp.zeros((1, width), jnp.float32)
+    bias_qkv[:, 2 * width : 3 * width] = vector(BV)
+    for g, (name, left, right, cut) in enumerate(groups):
+        if name == "qkv":
+            need(g)
+            project(cut[2], cut[3])
+    send_out(qkv, qkv_out)
+
+    box_group = [g for g, group in enumerate(groups) if group[0] == "box"][-1]
+    need(box_group)
+    low = full["box"].at[0][...].reshape(width, 2 * FREQ)
+    high = full["box"].at[1][...].reshape(width, 2 * FREQ)
+    box_w[...] = jnp.concatenate(
+        [low[:, :FREQ], high[:, :FREQ], low[:, FREQ:], high[:, FREQ:]], axis=1
+    )
+    page_length = jnp.where(first_block, lengths[0], lengths[1])
+    valid = lax.broadcasted_iota(jnp.int32, (1, page_len), 1) < page_length
+    head_lane = lax.broadcasted_iota(jnp.int32, (1, 128), 1)
+
+    def p_copy(p, slot):
+        return pltpu.make_async_copy(p_slots.at[slot], p_out.at[p], p_sem.at[slot])
+
+    first_tick = position[0]
+    per_pair = PAIR_TICKS
+
+    def pair(p, carry):
+        for i, event_list in enumerate(ticks[first_tick : first_tick + len(per_pair)]):
+            @pl.when(p == per_pair[i])
+            def _():
+                for event in event_list:
+                    event()
+
+        slot = lax.rem(p, 2)
+
+        @pl.when(p >= 2)
+        def _():
+            p_copy(p - 2, slot).wait()
+
+        q = qkv[:, lanes(p * 128, 128)]
+        k = qkv[:, lanes(width + p * 128, 128)]
+        v = qkv[:, lanes(2 * width + p * 128, 128)]
+        w = box_w[pl.ds(pl.multiple_of(p * 128, 128), 128), :]
+        outs = []
+        for i in range(2):
+            of_head = (head_lane < HEAD) == (i == 0)
+            q_head = jnp.where(of_head, q, jnp.zeros_like(q))
+            u = jnp.dot(q_head, w, preferred_element_type=jnp.float32)
+            on_sine, on_cosine = u[:, : 2 * FREQ], u[:, 2 * FREQ :]
+            cosine, sine = table[0], table[1]
+            b_cosine = (on_sine * sine + on_cosine * cosine).astype(jnp.bfloat16)
+            b_sine = (on_cosine * sine - on_sine * cosine).astype(jnp.bfloat16)
+            s = dot_t(q_head, k) + dot_t(b_cosine, keys[0]) + dot_t(b_sine, keys[1])
+            s = jnp.where(valid, s, MASKED)
+            top = jnp.max(s, axis=1, keepdims=True)
+            e = jnp.exp((s - top) * (HEAD**-0.5))
+            probs = (e * (1.0 / jnp.sum(e, axis=1, keepdims=True))).astype(jnp.bfloat16)
+            p_slots[slot, i] = probs
+            outs.append(jnp.dot(probs, v, preferred_element_type=jnp.float32))
+        mixed = jnp.where(head_lane < HEAD, outs[0], outs[1])
+        o_own[:, lanes(p * 128, 128)] = mixed
+        o_low[:, lanes(p * 128, 128)] = mixed.astype(jnp.bfloat16)
+        p_copy(p, slot).start()
+        return carry
+
+    lax.fori_loop(0, HEADS // 2, pair, 0)
+    position[0] += len(per_pair)
+    p_copy(4, 0).wait()
+    p_copy(5, 1).wait()
+    send_out(o_own, o_out)
+
+    def last_of(name):
+        return [g for g, group in enumerate(groups) if group[0] == name][-1]
+
+    def weight_out(name):
+        send_out(full[name], full_out[name])
+
+    weight_out("qkv")
+    weight_out("box")
+    need(last_of("out"))
+    weight_out("out")
+    for h in range(2):
+        w = full["out"].at[h][...].reshape(width, 384)
+        cut = slice(h * 384, (h + 1) * 384)
+        o_own_part = jnp.dot(o_low[...], w, preferred_element_type=jnp.float32)
+        unit2[:, cut] = x_own[:, cut].astype(jnp.float32) + o_own_part + vec[:, BO + h * 384 : BO + (h + 1) * 384]
+
+    def norm(hidden_sum):
+        mean = jnp.mean(hidden_sum, axis=1, keepdims=True)
+        centered = hidden_sum - mean
+        inverse = lax.rsqrt(jnp.mean(centered * centered, axis=1, keepdims=True) + EPSILON)
+        return centered * inverse, inverse
+
+    unit, inverse = norm(unit2[...])
+    unit1[...] = unit
+    inv1[...] = jnp.broadcast_to(inverse, (page_len, 128))
+    y1 = unit * vector(G1) + vector(E1)
+    y1_low[...] = y1.astype(jnp.bfloat16)
+    unit2[...] = y1 + vector(B2)
+    send_out(unit1, unit1_out)
+    send_out(inv1, inv1_out)
+
+    def up_tile(first, h, t):
+        start = pl.multiple_of(first + t * 256, 128)
+        w = full["up"].at[h][:, :, :, :, pl.ds(start, 256)].reshape(width, 256)
+        at = lanes(h * 1536 + start, 256)
+        pre = jnp.dot(y1_low[...], w, preferred_element_type=jnp.float32)
+        pre = pre + vec[:, lanes(B1 + h * 1536 + start, 256)]
+        half = 0.5 + 0.5 * lax.erf(pre * (2.0**-0.5))
+        hidden[:, at] = (pre * half).astype(jnp.bfloat16)
+        bell = jnp.exp(pre * pre * -0.5) * ((2.0 * math.pi) ** -0.5)
+        slope[:, at] = (half + pre * bell).astype(jnp.bfloat16)
+
+    for g, (name, left, right, cut) in enumerate(groups):
+        if name == "up":
+            need(g)
+            tiles = cut[3] // 256
+
+            def body(i, carry, first=cut[2], tiles=tiles):
+                up_tile(first, lax.div(i, tiles), lax.rem(i, tiles))
+                return carry
+
+            lax.fori_loop(0, 2 * tiles, body, 0)
+    send_out(hidden, g_out)
+    send_out(slope, d_out)
+    weight_out("up")
+
+    for g, (name, left, right, cut) in enumerate(groups):
+        if name == "down":
+            need(g)
+            first, count = cut[2], cut[3]
+
+            def body(h, carry, first=first, count=count):
+                w = full["down"].at[h][:, :, :, :, first : first + count].reshape(4 * width, count)
+                at = lanes(h * 384 + first, count)
+                unit2[:, at] += jnp.dot(hidden[...], w, preferred_element_type=jnp.float32)
+                return carry
+
+            lax.fori_loop(0, 2, body, 0)
+        if name == "up" and g == last_of("up"):
+            swap(1, cotangent, ct_out).start()
+    weight_out("down")
+    unit, inverse = norm(unit2[...])
+    unit2[...] = unit
+    inv2[...] = jnp.broadcast_to(inverse, (page_len, 128))
+    send_out(unit2, unit2_out)
+    send_out(inv2, inv2_out)
+
+    gather.drain()
+    for k in range(depth - 1):
+        vector_z(k).wait_send()
+    vector_xy(0).wait_send()
+    vector_xy(1).wait_send()
+    vector_c().wait_send()
+    box_swap.wait_send()
+    swap(0, tokens, x_own).wait_send()
+    swap(1, cotangent, ct_out).wait_send()
+    swap(1, cotangent, ct_out, True).wait_recv()
+    keep(1, cotangent, ct_out).wait()
+    for copy in outgoing:
+        copy.wait()
+
+
+AHEAD = 2
+PAIR_TICKS = (1, 4)
+
+
+def forward_call(depth, tokens, cotangent, boxes, lengths, piece, shards):
+    page_len = tokens.shape[1] * 2
+    width = tokens.shape[2]
+    heights = {n: s.shape[0] for n, s in zip(WEIGHTS, shards)}
+    groups = [
+        by_columns("qkv", heights["qkv"], 0, 256, 384),
+        by_columns("qkv", heights["qkv"], 640, 256, 256),
+        by_columns("box", heights["box"], 0, 128, 256),
+        by_columns("out", heights["out"], 0, 256, 128),
+        by_columns("up", heights["up"], 0, 384, 384),
+        by_columns("up", heights["up"], 768, 384, 384),
+        by_rows("down", heights["down"], 0, 256),
+        by_rows("down", heights["down"], 256, 128),
+    ]
+    count = len(groups)
+    frequency = np.exp(np.arange(FREQ) * (-math.log(10000.0) / FREQ)).astype(np.float32)
+    frequency = jnp.asarray(np.tile(frequency, 2)[None, :])
+    full = [jax.ShapeDtypeStruct((2, depth, 2, 2) + s.shape, jnp.bfloat16) for s in shards]
+    low, single = jnp.bfloat16, jnp.float32
+    kinds = dict(
+        x=((page_len, width), low),
+        ct=((page_len, width), low),
+        qkv=((page_len, 3 * width), low),
+        table=((2, page_len, 2 * FREQ), single),
+        p=((HEADS // 2, 2, page_len, page_len), low),
+        o=((page_len, width), single),
+        unit1=((page_len, width), single),
+        inv1=((page_len, 128), single),
+        g=((page_len, 4 * width), low),
+        d=((page_len, 4 * width), low),
+        unit2=((page_len, width), single),
+        inv2=((page_len, 128), single),
+        vec=((1, VECTORS + 128), single),
+    )
+    outs = full + [jax.ShapeDtypeStruct(*kinds[k]) for k in kinds]
+    anywhere = pl.BlockSpec(memory_space=pl.ANY)
+    vmem = pl.BlockSpec(memory_space=pltpu.VMEM)
+    smem = pl.BlockSpec(memory_space=pltpu.SMEM)
+    dma = pltpu.SemaphoreType.DMA
+    scratch = [pltpu.VMEM(f.shape, f.dtype) for f in full]
+    scratch += [
+        pltpu.VMEM((page_len, width), low),
+        pltpu.VMEM(boxes.shape, jnp.int32),
+        pltpu.VMEM((2, depth, 2, 2, 1, 384), single),
+        pltpu.VMEM((1, VECTORS + 128), single),
+        pltpu.VMEM((page_len, 3 * width), low),
+        pltpu.VMEM((2, page_len, 2 * FREQ), single),
+        pltpu.VMEM((2, page_len, 2 * FREQ), low),
+        pltpu.VMEM((width, BOX_DIM), low),
+        pltpu.VMEM((2, 2, page_len, page_len), low),
+        pltpu.VMEM((page_len, width), single),
+        pltpu.VMEM((page_len, width), low),
+        pltpu.VMEM((page_len, width), single),
+        pltpu.VMEM((page_len, 128), single),
+        pltpu.VMEM((page_len, width), low),
+        pltpu.VMEM((page_len, 4 * width), low),
+        pltpu.VMEM((page_len, 4 * width), low),
+        pltpu.VMEM((page_len, width), single),
+        pltpu.VMEM((page_len, 128), single),
+    ]
+    scratch += [dma((count, depth - 1))] * 2 + [dma((count, 4))] * 2 + [dma((count,))] * 2
+    scratch += [dma((count,))]
+    scratch += [dma((depth - 1,))] * 2 + [dma((2,))] * 2 + [dma((1,))] * 2
+    scratch += [dma((3,))] * 2 + [dma((3,)), dma((2,)), dma((18,))]
+    scratch += [pltpu.VMEM((1, 3 * width), single)]
+    plan = (depth, groups, page_len, width)
+    results = pl.pallas_call(
+        partial(forward_kernel, plan),
+        out_shape=outs,
+        in_specs=[anywhere, anywhere, vmem, smem, vmem, vmem] + [anywhere] * 5,
+        out_specs=[anywhere] * len(outs),
+        scratch_shapes=scratch,
+        compiler_params=pltpu.CompilerParams(
+            collective_id=0, has_side_effects=True, vmem_limit_bytes=VMEM_LIMIT
+        ),
+    )(tokens, cotangent, boxes, lengths, piece, frequency, *shards)
+    return dict(zip(WEIGHTS, results[:5])), dict(zip(kinds, results[5:]))
+
+
+VMEM_LIMIT = 60 * 2**20
+
+
+def fast_layer(tokens, boxes, lengths, wqkv, wbox, wout, wup, wdown, vectors, cotangent):
+    depth = lax.axis_size("dp") // 4
+    width = tokens.shape[2]
+    device = lax.axis_index("dp") * 2 + lax.axis_index("blk")
+    own = vectors.shape[0]
+    offset = lax.rem(device * own, 128)
+    piece = lax.dynamic_update_slice(
+        jnp.zeros((384,), jnp.float32), vectors.astype(jnp.float32), (offset,)
+    )[None, :]
+    shards = (wqkv, wbox, wout, wup, wdown)
+    full, kept = forward_call(depth, tokens, cotangent, boxes, lengths, piece, shards)
+
+    def whole(name):
+        w = full[name]
+        w = w.reshape(2, -1, w.shape[-1])
+        return jnp.concatenate([w[0], w[1]], axis=1)
+
+    vec = kept["vec"][0, :VECTORS]
+    bq, bv, bo, g1, e1, b1, b2, g2, e2 = unpack(vec, width, 4 * width)
+    x = kept["x"]
+    page_len = x.shape[0]
+    head_shape = (page_len, HEADS, HEAD)
+    q, k, v = (kept["qkv"][:, i * width : (i + 1) * width].reshape(head_shape) for i in range(3))
+    cosine, sine = kept["table"][0], kept["table"][1]
+    table = jnp.concatenate(
+        [cosine[:, :FREQ], sine[:, :FREQ], cosine[:, FREQ:], sine[:, FREQ:]], axis=1
+    )
+    keys = table.astype(jnp.bfloat16)
+    probs = kept["p"].reshape(HEADS, page_len, page_len)
+    mixed_low = kept["o"].astype(jnp.bfloat16)
+    unit1, inv1, unit2, inv2 = kept["unit1"], kept["inv1"][:, :1], kept["unit2"], kept["inv2"][:, :1]
+    hidden = kept["g"]
+    y1_low = (unit1 * g1 + e1).astype(jnp.bfloat16)
+    output = (unit2 * g2 + e2).astype(jnp.bfloat16)
+    seed = kept["ct"].astype(jnp.float32)
+    d_h2, d_g2, d_e2 = normalize_back(seed, unit2, inv2, g2)
+    d_f = d_h2.astype(jnp.bfloat16)
+    d_hidden = dot32(d_f, whole("down").T)
+    d_pre = (d_hidden * kept["d"].astype(jnp.float32)).astype(jnp.bfloat16)
+    d_wdown = dot32(hidden.T, d_f)
+    d_wup = dot32(y1_low.T, d_pre)
+    d_y1 = dot32(d_pre, whole("up").T) + d_h2
+    d_h1, d_g1, d_e1 = normalize_back(d_y1, unit1, inv1, g1)
+    d_a = d_h1.astype(jnp.bfloat16)
+    d_wout = dot32(mixed_low.T, d_a)
+    d_mixed = dot32(d_a, whole("out").T).astype(jnp.bfloat16).reshape(head_shape)
+    row_delta = jnp.einsum("qhd,qhd->hq", d_mixed.astype(jnp.float32), kept["o"].reshape(head_shape))
+    d_probs = jnp.einsum("qhd,khd->hqk", d_mixed, v, preferred_element_type=jnp.float32)
+    d_raw = (probs * (d_probs - row_delta[..., None])).astype(jnp.bfloat16)
+    scale = HEAD**-0.5
+    d_q = jnp.einsum("hqk,khd->qhd", d_raw, k, preferred_element_type=jnp.float32)
+    d_box_q = jnp.einsum("hqk,kc->qhc", d_raw, keys, preferred_element_type=jnp.float32)
+    d_k = jnp.einsum("hqk,qhd->khd", d_raw, q, preferred_element_type=jnp.float32)
+    d_v = jnp.einsum("hqk,qhd->khd", probs, d_mixed, preferred_element_type=jnp.float32)
+    d_coeffs = unrotate(d_box_q * scale, table).astype(jnp.bfloat16)
+    box_heads = whole("box").reshape(HEADS, HEAD, BOX_DIM)
+    d_q = d_q * scale + jnp.einsum(
+        "qhc,hdc->qhd", d_coeffs, box_heads, preferred_element_type=jnp.float32
+    )
+    d_wbox = jnp.einsum("qhd,qhc->hdc", q, d_coeffs, preferred_element_type=jnp.float32)
+    flat = (-1, width)
+    d_q = d_q.astype(jnp.bfloat16).reshape(flat)
+    d_k = (d_k * scale).astype(jnp.bfloat16).reshape(flat)
+    d_v = d_v.astype(jnp.bfloat16).reshape(flat)
+    d_c = jnp.concatenate([d_q, d_k, d_v], axis=1)
+    d_wqkv = dot32(x.T, d_c)
+    d_x = dot32(d_c, whole("qkv").T) + d_h1
+    total = partial(jnp.sum, axis=0, dtype=jnp.float32)
+    vector_grad = jnp.concatenate(
+        [total(d_q), total(d_v), total(d_a), d_g1, d_e1, total(d_pre), total(d_f), d_g2, d_e2]
+    )
+    from_pages = partial(
+        lax.all_to_all, axis_name="blk", split_axis=1, concat_axis=0, tiled=True
+    )
+    return (
+        from_pages(output[None]),
+        from_pages(d_x[None]),
+        scatter_weight(d_wqkv),
+        scatter_weight(d_wbox.reshape(width, BOX_DIM)),
+        scatter_weight(d_wout),
+        scatter_weight(d_wup),
+        scatter_weight(d_wdown),
+        lax.psum_scatter(vector_grad, ("dp", "blk"), scatter_dimension=0, tiled=True),
+    )
+
+
+def on_device(*args):
+    tokens, wqkv, wbox, wdown = args[0], args[3], args[4], args[7]
+    blocks, groups = lax.axis_size("blk"), lax.axis_size("dp")
+    fits = (
+        blocks == 2
+        and groups % 4 == 0
+        and tokens.shape[0] == 2
+        and wqkv.shape[0] % 16 == 0
+        and wdown.shape[0] % 32 == 0
+        and wbox.shape[1] == 2 * FREQ
+    )
+    return fast_layer(*args) if fits else general_layer(*args)
+
+
 def solution(mesh):
     in_specs = (
         P("dp", "blk", None),
@@ -217,5 +921,5 @@
         P(("dp", "blk")),
     )
     return jax.shard_map(
-        general_layer, mesh=mesh, in_specs=in_specs, out_specs=out_specs, check_vma=False
-    )
+        on_device, mesh=mesh, in_specs=in_specs, out_specs=out_specs, check_vma=False
+    )

time: 767 us -> 561 us (0.73)
  waiting for transfers between devices: 339 us -> 241 us
  Pallas kernels: 0 us -> 93.2 us
  matrix products: 157 us -> 70.5 us
  blocking collectives: 113 us -> 39.8 us
  other arithmetic: 62.5 us -> 21.7 us
  starting transfers between devices: 18.5 us -> 7.96 us
  local copies, waits for them, and re-layouts: 53.1 us -> 63.3 us
    pallas_call x0 -> x1, Pallas kernels: none -> 93.2 us  [forward_call(): pl.pallas_call(partial(forward_kernel, plan), out_shape=outs, in_specs=[a...]
    unnamed x19 -> x14, waiting for transfers between devices: 79.6 us -> 10.5 us
    all_gather x5 -> x0, waiting for transfers between devices: 45.4 us -> none  [gather_weight(): return lax.all_gather(part, 'dp', axis=0, tiled=True)]
    dot_general x12 -> x8, matrix products: 78.2 us -> 33 us  [dot32(): return jnp.dot(a, b, preferred_element_type=jnp.float32)]
    dot_general x11 -> x7, matrix products: 79 us -> 37.5 us  [the longest x1 10.2 us: fast_layer(): jnp.einsum('hqk,kc->qhc', d_raw, keys, preferred_element_type=jnp.float32)]
    unnamed x2 -> x1, blocking collectives: 79.7 us -> 39.8 us
    all_gather x5 -> x0, blocking collectives: 33.1 us -> none  [gather_weight(): part = lax.all_gather(shard, 'blk', axis=1, tiled=True)]
    concatenate x2 -> x0, other arithmetic: 30.4 us -> none  [the longest x1 15.8 us: rotate(): jnp.concatenate([sa * sin_across + ca * cos_across, ca * sin_across - sa...]
  transfers between devices with their start and end apart: 20 -> 12, of which waited for: 11 -> 6; matrix products, arithmetic and copies ran while one was open for 24% -> 23% of each run, Pallas kernels for 0% -> 0%
where the time goes in v2:
time: 561 us; the launch traced here: 553 us
  waiting for transfers between devices  241 us (43%)
  Pallas kernels  93.2 us (17%)
  matrix products  70.5 us (13%)
  local copies, waits for them, and re-layouts  63.3 us (11%)
  blocking collectives  39.8 us (7%)
  other arithmetic  21.7 us (4%)
  between operations  15.2 us (3%)
  starting transfers between devices  7.96 us (1%)
    reduce_scatter x5, waiting for transfers between devices, scatter_weight(): lax.psum_scatter(grad.astype(jnp.bfloat16), 'dp', scatter_dimension=0, ti...  218 us
    pallas_call x1, Pallas kernels, forward_call(): pl.pallas_call(partial(forward_kernel, plan), out_shape=outs, in_specs=[a...  93.2 us
    unnamed x1, blocking collectives  39.8 us
    dot_general x8, matrix products, dot32(): return jnp.dot(a, b, preferred_element_type=jnp.float32)  33 us
    unnamed x119, local copies, waits for them, and re-layouts  27.1 us
    reduce_scatter x1, waiting for transfers between devices, scatter_weight(): lax.psum_scatter(part, 'blk', scatter_dimension=1, tiled=True)  12.4 us
  transfers between devices with their start and end apart: 12, of which 6 were waited for; matrix products, arithmetic and copies ran while one was open for 23% of the time, Pallas kernels for 0%

profile of v2, /device:TPU:0, one launch (start us, length us, event | category | flops | bytes accessed | tf_op | source)
XLA Modules:
  0.0 552.7 jit_solution(10411482473194154126)
XLA Ops:
  8.6 93.2 %shard_map.170 = (bf16[2,4,2,2,48,1152]{5,4,3,2,1,0:T(8,128)(2,1)}, bf16[2,4,2,2,48,384]{5,4,3,2,1,0:T(8,128)(2,1)}, bf16[2,4,2,2,48,384]{5,4,3,2,1,0:T(8,128)(2...) custom-call(bf16[2,256,768]{2,1,0:T(8,128)(2,1)} %refs_0_.1, ...), custom_call_target="tpu_custom_call" | custom-call | tf_op jit(solution)/shard_map/pallas_call | solution.py:784
  101.7 1.3 slice_reduce_fusion.2
  103.1 1.1 slice_reduce_fusion.1
  104.2 1.2 slice_reduce_fusion
  105.4 3.1 fusion.54
  110.7 2.0 convert_reduce_fusion.2
  112.9 3.5 convert_reduce_fusion
  116.4 3.4 multiply_reduce_fusion
  120.3 1.1 copy-done.3
  121.4 1.8 convolution_convert_fusion.3
  123.3 1.7 copy.83
  125.0 1.5 slice_bitcast_fusion.1
  127.2 1.1 slice_bitcast_fusion.5
  128.4 1.2 copy.64
  129.6 0.9 copy.67
  130.6 1.0 copy.66
  131.5 0.9 copy.65
  132.5 3.0 fusion.56
  135.4 1.4 copy.69
  136.9 1.2 copy.61
  138.0 3.0 fusion.57
  141.0 1.7 convolution_convert_fusion.4
  142.8 1.5 copy.60
  145.5 4.5 multiply_convert_fusion
  150.0 10.2 %multiply_bitcast_fusion = f32[512,12,768]{0,2,1:T(8,128)} fusion(bf16[12,512,512]{2,1,0:T(8,128)(2,1)S(1)} %multiply_convert_fusion, f32[512,192]{1,0:T(8,128)S(1)} %copy-done.23, f32[512,192]{1,0:T(8,128)S(1)} %copy-done.21, f32[512,192]{1,0:T(8,128)S(1)} %copy-done.25, f32[512,192]{1,0:T(8,128)S(1)} %copy-done.19), kind=kOutput, calls=%fused_computation | convolution fusion | flops 4839702528 | bytes 26738688 | tf_op jit(solution)/shard_map/hqk,kc->qhc/dot_general | solution.py:851
  160.3 8.2 %subtract_convert_fusion.1 = (bf16[512,12,192]{0,2,1:T(8,128)(2,1)S(1)}, bf16[512,12,192]{0,2,1:T(8,128)(2,1)S(1)}, bf16[512,12,192]{0,2,1:T(8,128)(2,1)S(1)}, bf16[512,12,192]{0,2,1:T(8,128)(2,1)S(1)}) fusion(f32[512,12,768]{0,2,1:T(8,128)} %multiply_bitcast_fusion, f32[512,192]{0,1:T(8,128)S(1)} %copy-done.28, f32[512,192]{0,1:T(8,128)S(1)} %copy.64, ...), kind=kLoop, calls=%fused_computation.18 | loop fusion | flops 18874368 | bytes 29884416 | tf_op jit(solution)/shard_map/convert.1
  168.6 5.6 %fusion.21 = bf16[12,64,768]{2,1,0:T(8,128)(2,1)} fusion(bf16[512,12,64]{0,2,1:T(8,128)(2,1)S(1)} %bitcast.93, bf16[512,12,192]{0,2,1:T(8,128)(2,1)S(1)} %get-tuple-element.64, bf16[512,12,192]{0,2,1:T(8,128)(2,1)S(1)} %get-tuple-element.65, bf16[512,12,192]{0,2,1:T(8,128)(2,1)S(1)} %get-tuple-element.61, bf16[512,12,192]{0,2,1:T(8,128)(2,1)S(1)} %get-tuple-element.60), kind=kOutput, calls=%fused_computation.51 | convolution fusion | flops 642318336 | bytes 11403264 | tf_op jit(solution)/shard_map/qhd,qhc->hdc/dot_general | solution.py:859
  174.2 4.8 convert_reduce_fusion.4
  179.0 5.0 multiply_convert_fusion.2
  184.0 1.2 copy.59
  185.1 5.4 fusion.15
  190.8 2.1 convert_reduce_fusion.5
  193.8 3.9 convolution_convert_fusion.2
  197.7 1.4 copy-done.32
  199.1 6.8 %convolution_convert_fusion = bf16[3072,768]{1,0:T(8,128)(2,1)} fusion(bf16[512,3072]{1,0:T(8,128)(2,1)} %get-tuple-element.43, f32[512,768]{1,0:T(8,128)S(1)} %copy-done.32), kind=kOutput, calls=%fused_computation.5 | convolution fusion | flops 2418671616 | bytes 9437184 | tf_op jit(solution)/shard_map/dot_general | solution.py:84
  206.0 1.3 copy-done.30
  207.3 6.2 %convolution_convert_fusion.1 = bf16[768,3072]{1,0:T(8,128)(2,1)} fusion(bf16[512,3072]{1,0:T(8,128)(2,1)} %copy-done.43, f32[512,768]{1,0:T(8,128)S(1)} %copy-done.30, f32[768]{0:T(1024)S(1)} %copy-done.38, f32[768]{0:T(1024)S(1)} %get-tuple-element.53), kind=kOutput, calls=%fused_computation.6 | convolution fusion | flops 2419458048 | bytes 9443328 | tf_op jit(solution)/shard_map/dot_general | solution.py:84
  213.6 1.8 copy.89
  215.7 25.9 %reduce-scatter.21.cloned.1.call-done = bf16[48,768]{1,0:T(8,128)(2,1)} async-done(((bf16[768,768]{1,0:T(8,128)(2,1)}), bf16[48,768]{1,0:T(8,128)(2,1)}) %reduce-scatter.21.cloned.1.call-update) | async-done | bytes 73744 | tf_op jit(solution)/shard_map/reduce_scatter | solution.py:93
  241.6 1.7 copy.87
  243.3 1.2 copy.97
  245.0 5.4 reduce.16
  250.5 1.0 reshape.139
  251.5 3.5 all-to-all-start
  255.1 57.5 %reduce-scatter.19.cloned.1.call-done = bf16[48,2304]{1,0:T(8,128)(2,1)} async-done(((bf16[768,2304]{1,0:T(8,128)(2,1)}), bf16[48,2304]{1,0:T(8,128)(2,1)}) %reduce-scatter.19.cloned.1.call-update) | async-done | bytes 221200 | tf_op jit(solution)/shard_map/reduce_scatter | solution.py:93
  312.6 2.0 copy.85
  314.7 4.2 fusion.55
  318.9 71.8 %reduce-scatter.29.cloned.1.call-done = bf16[192,768]{1,0:T(8,128)(2,1)} async-done(((bf16[3072,768]{1,0:T(8,128)(2,1)}), bf16[192,768]{1,0:T(8,128)(2,1)}) %reduce-scatter.29.cloned.1.call-update) | async-done | bytes 294928 | tf_op jit(solution)/shard_map/reduce_scatter | solution.py:93
  390.7 1.9 copy.91
  392.6 5.7 %add_bitcast_fusion = f32[1,512,768]{2,1,0:T(8,128)} fusion(f32[512,768]{1,0:T(8,128)S(1)} %copy-done.2, bf16[768,1152]{1,0:T(8,128)(2,1)} %bitcast.112, bf16[768,1152]{1,0:T(8,128)(2,1)} %bitcast.111, bf16[512,768]{0,1:T(8,128)(2,1)S(1)} %bitcast.103, bf16[512,768]{0,1:T(8,128)(2,1)} %bitcast.104, bf16[512,768]{0,1:T(8,128)(2,1)} %bitcast.120), kind=kOutput, calls=%fused_computation.45 | convolution fusion | flops 1826488320 | bytes 9043968 | tf_op jit(solution)/shard_map/dot_general | solution.py:84
  398.5 4.4 copy.70
  402.9 3.7 all-to-all-start.1
  406.7 62.9 %reduce-scatter.25.cloned.1.call-done = bf16[48,3072]{1,0:T(8,128)(2,1)} async-done(((bf16[768,3072]{1,0:T(8,128)(2,1)}), bf16[48,3072]{1,0:T(8,128)(2,1)}) %reduce-scatter.25.cloned.1.call-update) | async-done | bytes 294928 | tf_op jit(solution)/shard_map/reduce_scatter | solution.py:93
  469.7 39.8 %all-reduce = f32[9216]{0:T(1024)S(1)} all-reduce(f32[9216]{0:T(1024)S(1)} %constant_dynamic-update-slice_fusion), channel_id=12, replica_groups=mesh['dp'=16,'blk'=2] {'dp','blk'}, use_global_device_ids=true, to_apply=%region_23.0.clone | all-reduce | flops 9216 | bytes 73728
  510.2 1.7 reshape.140
  511.9 1.0 copy.94
  512.9 1.2 copy.95
  514.2 1.0 copy.90
  515.8 1.0 copy.88
  517.4 1.1 copy.86
  519.2 10.3 %reduce-scatter.37.cloned.1.call-done = bf16[384,192]{1,0:T(8,128)(2,1)} async-done(((bf16[768,192]{1,0:T(8,128)(2,1)}), bf16[384,192]{1,0:T(8,128)(2,1)}) %reduce-scatter.37.cloned.1.call-update) | async-done | bytes 147472
  529.6 1.1 copy.92
  531.4 12.4 %reduce-scatter.27.cloned.1.call-done = bf16[48,1536]{1,0:T(8,128)(2,1)} async-done(((bf16[48,3072]{1,0:T(8,128)(2,1)}), bf16[48,1536]{1,0:T(8,128)(2,1)}) %reduce-scatter.27.cloned.1.call-update) | async-done | bytes 147472 | tf_op jit(solution)/shard_map/reduce_scatter | solution.py:94
  543.8 1.6 convert_element_type.133
  (151 shorter events, 12.2 us)
Async XLA Ops:
  7.2 206.4 %reduce-scatter.23.cloned.1.call-start = ((), (), s32[]{:S(2)}) async-start(), calls=%async_computation.14 | async-start | bytes 1253376 | tf_op jit(solution)/shard_map/reduce_scatter | solution.py:93
  8.0 0.6 copy-start.37
  104.1 4.4 slice-start.2
  105.4 3.1 slice-start.3
  108.5 1.4 copy-start.5
  108.6 1.6 copy-start.10
  110.7 2.2 copy-start.41
  112.7 3.7 copy-start.31
  112.9 3.5 copy-start.29
  116.4 3.4 copy-start.43
  119.9 1.5 copy-start.3
  120.3 20.7 %copy-start.1 = (f32[512,768]{1,0:T(8,128)}, f32[512,768]{1,0:T(8,128)S(1)}, u32[]{:S(2)}) copy-start(f32[512,768]{1,0:T(8,128)S(1)} %get-tuple-element.59) | copy-start | bytes 4718596
  123.2 118.3 %reduce-scatter.21.cloned.1.call-start = ((), (), s32[]{:S(2)}) async-start(), calls=%async_computation.13 | async-start | bytes 1253376 | tf_op jit(solution)/shard_map/reduce_scatter | solution.py:93
  126.8 1.6 copy-start.18
  126.8 1.6 copy-start.20
  126.8 1.6 copy-start.22
  126.8 1.6 copy-start.24
  142.8 1.6 copy-start.4
  144.3 1.2 copy-start.7
  145.4 4.5 copy-start.19
  145.5 4.5 copy-start.21
  145.5 4.5 copy-start.23
  145.5 4.5 copy-start.25
  150.0 10.3 %copy-start = (bf16[12,512,512]{2,1,0:T(8,128)(2,1)}, bf16[12,512,512]{2,1,0:T(8,128)(2,1)S(1)}, u32[]{:S(2)}) copy-start(bf16[12,512,512]{2,1,0:T(8,128)(2,1)S(1)} %multiply_convert_fusion) | copy-start | bytes 18874372
  150.0 10.3 %copy-start.26 = (f32[512,192]{0,1:T(8,128)S(1)}, f32[512,192]{0,1:T(8,128)}, u32[]{:S(2)}) copy-start(f32[512,192]{0,1:T(8,128)} %copy.67) | copy-start | bytes 1179652
  150.0 10.2 %copy-start.27 = (f32[512,192]{0,1:T(8,128)S(1)}, f32[512,192]{0,1:T(8,128)}, u32[]{:S(2)}) copy-start(f32[512,192]{0,1:T(8,128)} %copy.66) | copy-start | bytes 1179652
  150.0 10.2 %copy-start.28 = (f32[512,192]{0,1:T(8,128)S(1)}, f32[512,192]{0,1:T(8,128)}, u32[]{:S(2)}) copy-start(f32[512,192]{0,1:T(8,128)} %copy.65) | copy-start | bytes 1179652
  168.5 5.6 %copy-start.14 = (bf16[512,12,192]{0,2,1:T(8,128)(2,1)}, bf16[512,12,192]{0,2,1:T(8,128)(2,1)S(1)}, u32[]{:S(2)}) copy-start(bf16[512,12,192]{0,2,1:T(8,128)(2,1)S(1)} %get-tuple-element.60) | copy-start | bytes 7077892
  168.5 5.6 %copy-start.15 = (bf16[512,12,192]{0,2,1:T(8,128)(2,1)}, bf16[512,12,192]{0,2,1:T(8,128)(2,1)S(1)}, u32[]{:S(2)}) copy-start(bf16[512,12,192]{0,2,1:T(8,128)(2,1)S(1)} %get-tuple-element.61) | copy-start | bytes 7077892
  168.5 5.6 %copy-start.16 = (bf16[512,12,192]{0,2,1:T(8,128)(2,1)}, bf16[512,12,192]{0,2,1:T(8,128)(2,1)S(1)}, u32[]{:S(2)}) copy-start(bf16[512,12,192]{0,2,1:T(8,128)(2,1)S(1)} %get-tuple-element.64) | copy-start | bytes 7077892
  168.5 5.6 %copy-start.17 = (bf16[512,12,192]{0,2,1:T(8,128)(2,1)}, bf16[512,12,192]{0,2,1:T(8,128)(2,1)S(1)}, u32[]{:S(2)}) copy-start(bf16[512,12,192]{0,2,1:T(8,128)(2,1)S(1)} %get-tuple-element.65) | copy-start | bytes 7077892
  174.2 138.4 %reduce-scatter.19.cloned.1.call-start = ((), (), s32[]{:S(2)}) async-start(), calls=%async_computation.12 | async-start | bytes 3760128 | tf_op jit(solution)/shard_map/reduce_scatter | solution.py:93
  179.0 5.0 copy-start.6
  179.0 6.1 %copy-start.34 = (bf16[1,4,2,2,48,384]{5,4,3,2,1,0:T(8,128)(2,1)S(1)}, bf16[1,4,2,2,48,384]{5,4,3,2,1,0:T(8,128)(2,1)}, u32[]{:S(2)}) copy-start(bf16[1,4,2,2,48,384]{5,4,3,2,1,0:T(8,128)(2,1)} %get-tuple-element.82) | copy-start | bytes 1769476
  184.0 6.6 %slice-start = ((s8[6291456]{0:T(1024)(128)(4,1)}), s8[2097152]{0:T(1024)(128)(4,1)S(1)}, s32[]{:S(2)}) async-start(s8[6291456]{0:T(1024)(128)(4,1)} %bitcast.86), calls=%async_computation.22 | async-start | bytes 4194304
  185.1 5.5 slice-start.1
  185.1 5.6 %copy-start.11 = (bf16[512,768]{0,1:T(8,128)(2,1)S(1)}, bf16[512,768]{0,1:T(8,128)(2,1)}, u32[]{:S(2)}) copy-start(bf16[512,768]{0,1:T(8,128)(2,1)} %copy.59) | copy-start | bytes 2359300
  190.8 3.0 copy-start.12
  190.8 3.0 copy-start.13
  190.8 3.0 copy-start.42
  192.9 0.9 copy-start.33
  197.7 1.4 copy-start.32
  197.7 193.0 %reduce-scatter.29.cloned.1.call-start = ((), (), s32[]{:S(2)}) async-start(), calls=%async_computation.17 | async-start | bytes 5013504 | tf_op jit(solution)/shard_map/reduce_scatter | solution.py:93
  205.9 1.4 copy-start.30
  205.9 1.4 copy-start.38
  205.9 263.7 %reduce-scatter.25.cloned.1.call-start = ((), (), s32[]{:S(2)}) async-start(), calls=%async_computation.15 | async-start | bytes 5013504 | tf_op jit(solution)/shard_map/reduce_scatter | solution.py:93
  213.5 29.8 %copy-start.9 = (bf16[1,512,768]{2,1,0:T(8,128)(2,1)S(1)}, bf16[1,512,768]{2,1,0:T(8,128)(2,1)}, u32[]{:S(2)}) copy-start(bf16[1,512,768]{2,1,0:T(8,128)(2,1)} %get-tuple-element.75) | copy-start | bytes 2359300
  213.5 300.6 %reduce-scatter.35.cloned.1.call-start = ((), (), s32[]{:S(2)}) async-start(), calls=%async_computation.20 | async-start | bytes 294912
  215.4 300.4 %reduce-scatter.33.cloned.1.call-start = ((), (), s32[]{:S(2)}) async-start(), calls=%async_computation.19 | async-start | bytes 294912
  251.5 151.4 %all-to-all-start = ((bf16[2,2,98304]{2,1,0:T(2,128)(2,1)}), bf16[2,2,98304]{2,1,0:T(2,128)(2,1)S(1)}, u32[]{:S(2)}, u32[]{:S(2)}) async-start(bf16[2,2,98304]{2,1,0:T(2,128)(2,1)} %reshape.139), calls=%async_computation | async-start | bytes 1572864 | tf_op jit(solution)/shard_map/all_to_all | solution.py:875
  255.0 262.4 %reduce-scatter.31.cloned.1.call-start = ((), (), s32[]{:S(2)}) async-start(), calls=%async_computation.18 | async-start | bytes 884736
  314.6 214.9 %reduce-scatter.37.cloned.1.call-start = ((), (), s32[]{:S(2)}) async-start(), calls=%async_computation.21 | async-start | bytes 589824
  314.7 77.9 %copy-start.2 = (f32[512,768]{1,0:T(8,128)S(1)}, f32[512,768]{1,0:T(8,128)}, u32[]{:S(2)}) copy-start(f32[512,768]{1,0:T(8,128)} %copy-done.1) | copy-start | bytes 4718596
  402.8 66.8 %copy-start.40 = (f32[768]{0:T(1024)S(1)}, f32[768]{0:T(1024)}, u32[]{:S(2)}) copy-start(f32[768]{0:T(1024)} %get-tuple-element.44) | copy-start | bytes 9220
  402.8 66.8 %copy-start.39 = (f32[768]{0:T(1024)S(1)}, f32[768]{0:T(1024)}, u32[]{:S(2)}) copy-start(f32[768]{0:T(1024)} %get-tuple-element.49) | copy-start | bytes 9220
  402.8 66.8 %copy-start.36 = (f32[3072]{0:T(1024)S(1)}, f32[3072]{0:T(1024)}, u32[]{:S(2)}) copy-start(f32[3072]{0:T(1024)} %get-tuple-element.95) | copy-start | bytes 36868
  402.8 66.8 %copy-start.35 = (f32[768]{0:T(1024)S(1)}, f32[768]{0:T(1024)}, u32[]{:S(2)}) copy-start(f32[768]{0:T(1024)} %get-tuple-element.56) | copy-start | bytes 9220
  402.9 106.7 %copy-start.8 = (bf16[2,2,98304]{2,1,0:T(2,128)(2,1)}, bf16[2,2,98304]{2,1,0:T(2,128)(2,1)S(1)}, u32[]{:S(2)}) copy-start(bf16[2,2,98304]{2,1,0:T(2,128)(2,1)S(1)} %all-to-all-done) | copy-start | bytes 2359300
  402.9 110.0 %all-to-all-start.1 = ((f32[1,512,768]{2,0,1:T(1,128)}), f32[1,512,768]{2,0,1:T(1,128)S(1)}, u32[]{:S(2)}, u32[]{:S(2)}) async-start(f32[1,512,768]{2,0,1:T(1,128)} %copy.70), calls=%async_computation.1 | async-start | bytes 3145728 | tf_op jit(solution)/shard_map/all_to_all | solution.py:876
  406.6 137.1 %reduce-scatter.27.cloned.1.call-start = ((), (), s32[]{:S(2)}) async-start(), calls=%async_computation.16 | async-start | bytes 442368 | tf_op jit(solution)/shard_map/reduce_scatter | solution.py:94
Sparse Core Ops, SparseCore 0:
  123.4 57.3 reduce-scatter.22
  184.4 57.1 reduce-scatter.20
  245.4 67.0 reduce-scatter.18
  316.3 74.3 reduce-scatter.28
  394.9 74.5 reduce-scatter.24
  472.2 9.9 reduce-scatter.34
  485.0 11.0 reduce-scatter.32
  498.4 15.7 reduce-scatter.30
  516.5 13.0 reduce-scatter.36
  531.7 12.0 reduce-scatter.26

commit v3 on v2

--- a/solution.py
+++ b/solution.py
@@ -797,9 +797,602 @@
 VMEM_LIMIT = 60 * 2**20
 
 
+class Scatter:
+    def __init__(self, place, groups, stored, landing, summed, sems):
+        self.place, self.groups, self.stored, self.summed = place, groups, stored, summed
+        self.c_land, self.a1, self.b1, self.a2, self.b2, self.z_land = landing
+        self.c_sems, self.xy_sems, self.z_sems = sems
+        self.sent = set()
+
+    def c_copy(self, g):
+        p = self.place
+        _, store, _, _, both, _ = self.groups[g]
+        ref = self.stored[store].at[(ALL, ALL, ALL, 1 - p.c) + window(both)]
+        return remote(ref, self.c_land[g], self.c_sems, (g,), p.c_peer)
+
+    def xy_copy(self, g, i):
+        p = self.place
+        _, store, left, right, _, _ = self.groups[g]
+        a, b = window(left), window(right)
+        index, land, peer = (
+            ((1 - p.y, ALL, ALL, p.c) + a, self.a1[g], p.y_peer),
+            ((ALL, ALL, 1 - p.x, p.c) + b, self.b1[g], p.x_peer),
+            ((p.y, ALL, 1 - p.x, p.c) + a, self.a2[g], p.x_peer),
+            ((1 - p.y, ALL, p.x, p.c) + b, self.b2[g], p.y_peer),
+        )[i]
+        return remote(self.stored[store].at[index], land, self.xy_sems, (g, i), peer)
+
+    def z_copy(self, g, k):
+        p = self.place
+        _, store, _, _, both, _ = self.groups[g]
+        there = lax.rem(p.z + k + 1, p.depth)
+        ref = self.stored[store].at[(p.y, there, p.x, p.c) + window(both)]
+        return remote(ref, self.z_land[g].at[k], self.z_sems, (g, k), p.z_peers[k])
+
+    def add(self, g, piece, outer, arrived):
+        store = self.stored[self.groups[g][1]]
+        cut = window(piece)
+
+        def body(i, carry):
+            here, there = outer(i)
+            store[here + cut] = (
+                store[here + cut].astype(jnp.float32) + arrived[there].astype(jnp.float32)
+            ).astype(jnp.bfloat16)
+            return carry
+
+        return body
+
+    def run(self, count, body):
+        lax.fori_loop(0, count, body, 0)
+
+    def start(self, g):
+        self.c_copy(g).start()
+
+    def first(self, g):
+        p, d = self.place, self.place.depth
+        _, _, left, right, both, _ = self.groups[g]
+        self.c_copy(g).wait_recv()
+
+        def outer(i):
+            dy, dz, dx = lax.div(i, 2 * d), lax.rem(lax.div(i, 2), d), lax.rem(i, 2)
+            return (dy, dz, dx, p.c), (dy, dz, dx)
+
+        self.run(4 * d, self.add(g, both, outer, self.c_land[g]))
+        self.xy_copy(g, 0).start()
+        self.xy_copy(g, 1).start()
+
+    def second(self, g):
+        p, d = self.place, self.place.depth
+        _, _, left, right, _, _ = self.groups[g]
+        self.xy_copy(g, 0).wait_recv()
+
+        def outer_a(i):
+            dz, dx = lax.div(i, 2), lax.rem(i, 2)
+            return (p.y, dz, dx, p.c), (dz, dx)
+
+        self.run(2 * d, self.add(g, left, outer_a, self.a1[g]))
+        self.xy_copy(g, 2).start()
+        self.xy_copy(g, 1).wait_recv()
+
+        def outer_b(i):
+            dy, dz = lax.div(i, d), lax.rem(i, d)
+            return (dy, dz, p.x, p.c), (dy, dz)
+
+        self.run(2 * d, self.add(g, right, outer_b, self.b1[g]))
+        self.xy_copy(g, 3).start()
+
+    def third(self, g):
+        p, d = self.place, self.place.depth
+        _, _, left, right, _, _ = self.groups[g]
+
+        def outer(i):
+            return (p.y, i, p.x, p.c), (i,)
+
+        self.xy_copy(g, 2).wait_recv()
+        self.run(d, self.add(g, left, outer, self.a2[g]))
+        self.xy_copy(g, 3).wait_recv()
+        self.run(d, self.add(g, right, outer, self.b2[g]))
+        for k in range(d - 1):
+            self.z_copy(g, k).start()
+
+    def fourth(self, g):
+        p, d = self.place, self.place.depth
+        name, store, _, _, both, result = self.groups[g]
+        for k in range(d - 1):
+            self.z_copy(g, k).wait_recv()
+        total = self.stored[store][(p.y, p.z, p.x, p.c) + window(both)].astype(jnp.float32)
+        for k in range(d - 1):
+            total = total + self.z_land[g][k].astype(jnp.float32)
+        self.summed[name][window(result)] = total
+
+    def left(self, g):
+        if g in self.sent:
+            return
+        self.sent.add(g)
+        self.c_copy(g).wait_send()
+        for i in range(4):
+            self.xy_copy(g, i).wait_send()
+        for k in range(self.place.depth - 1):
+            self.z_copy(g, k).wait_send()
+
+
+def backward_kernel(plan, *refs):
+    depth, groups, page_len, width = plan
+    block = page_len // 2
+    refs = iter(refs)
+    take = lambda n: [next(refs) for _ in range(n)]
+    w_in = dict(zip(WEIGHTS, take(5)))
+    (x_in, ct_in, qkv_in, table_in, p_in, o_in, unit1_in, inv1_in) = take(8)
+    (g_in, d_in, unit2_in, inv2_in, vec_in) = take(5)
+    out_out, dx_out = take(2)
+    grad_out = dict(zip(WEIGHTS, take(5)))
+    (piece_out,) = take(1)
+    stored = dict(zip(("box", "out", "up", "down"), take(4)))
+    count = len(groups)
+    landing = [take(count) for _ in range(6)]
+    summed = dict(zip(WEIGHTS, take(5)))
+    w_box, w_out, box_w, box_g = take(4)
+    (x_own, ct, qkv, table, keys, o_own, unit1, inv1, hidden, slope, unit2, inv2, vec) = take(13)
+    (y1_low, d_a, d_mixed, out_low, dx_low, vec_g) = take(6)
+    pieces, pc_land, py_land, px_land, pz_land, piece_sum = take(6)
+    c_sems, xy_sems, z_sems = take(2), take(2), take(2)
+    v_sems, vz_sems, ex_sems = take(2), take(2), take(2)
+    in_sem, p_sem, out_sem = take(3)
+
+    place = Place(depth)
+    y, z, x, c = place.y, place.z, place.x, place.c
+    scatter = Scatter(place, groups, stored, landing, summed, (c_sems, xy_sems, z_sems))
+
+    sources = dict(
+        unit2=(unit2_in, unit2),
+        ct=(ct_in, ct),
+        inv2=(inv2_in, inv2),
+        vec=(vec_in, vec),
+        g=(g_in, hidden),
+        d=(d_in, slope),
+        unit1=(unit1_in, unit1),
+        inv1=(inv1_in, inv1),
+        w_out=(w_in["out"], w_out),
+        w_box=(w_in["box"], w_box),
+        o=(o_in, o_own),
+        qkv=(qkv_in, qkv),
+        table=(table_in, table),
+        x=(x_in, x_own),
+    )
+    order = list(sources)
+
+    def fetch(name):
+        source, target = sources[name]
+        return pltpu.make_async_copy(source, target, in_sem.at[order.index(name)])
+
+    def fetch_weight(name, target):
+        at = len(order) + ("down", "up", "qkv").index(name)
+        return pltpu.make_async_copy(w_in[name], target, in_sem.at[at])
+
+    def vector(start, size=width):
+        return vec[:, start : start + size]
+
+    def total(value):
+        return jnp.sum(value.astype(jnp.float32), axis=0, keepdims=True)
+
+    def norm_back(grad, unit, inverse, gain):
+        scaled = grad * gain
+        mean_grad = jnp.mean(scaled, axis=1, keepdims=True)
+        mean_unit = jnp.mean(scaled * unit, axis=1, keepdims=True)
+        return inverse * (scaled - mean_grad - unit * mean_unit)
+
+    names = [group[0] for group in groups]
+    pending = []
+
+    def stages(g):
+        tick = []
+        if 0 <= g < count:
+            tick.append(partial(scatter.first, g))
+        if 0 <= g - 1 < count:
+            tick.append(partial(scatter.second, g - 1))
+        if 0 <= g - 2 < count:
+            tick.append(partial(scatter.third, g - 2))
+        if 0 <= g - 3 < count:
+            tick.append(partial(scatter.fourth, g - 3))
+        return tick
+
+    timeline = [stages(t) for t in range(count + 3)]
+    position = [0]
+
+    def tick(n=1):
+        for _ in range(n):
+            for event in timeline[position[0]]:
+                event()
+            position[0] += 1
+
+    for name in order:
+        fetch(name).start()
+
+    fetch("unit2").wait()
+    fetch("ct").wait()
+    fetch("inv2").wait()
+    fetch("vec").wait()
+    unit = unit2[...]
+    out_low[...] = (unit * vector(G2) + vector(E2)).astype(jnp.bfloat16)
+    seed = ct[...].astype(jnp.float32)
+    vec_g[:, G2 : G2 + width] = total(seed * unit)
+    vec_g[:, E2 : E2 + width] = total(seed)
+    d_h2 = norm_back(seed, unit, inv2[:, 0:1], vector(G2))
+    unit2[...] = d_h2
+    ct[...] = d_h2.astype(jnp.bfloat16)
+    d_f = ct
+    vec_g[:, B2 : B2 + width] = total(d_f[...])
+
+    def rows(at):
+        return pl.ds(pl.multiple_of(at * block, block), block)
+
+    out_swap = remote(out_low.at[rows(1 - y)], out_out.at[y], ex_sems, (0,), place.y_peer)
+    out_keep = pltpu.make_async_copy(out_low.at[rows(y)], out_out.at[y], out_sem.at[0])
+    dx_swap = remote(dx_low.at[0], dx_low.at[1], ex_sems, (1,), place.y_peer)
+
+    def with_down(w_down):
+        fetch_weight("down", w_down).start()
+        fetch("g").wait()
+
+        def grad_tile(t, carry):
+            rows_g = hidden[:, lanes(t * width, width)]
+            part = dot_n(rows_g, d_f[...]).astype(jnp.bfloat16)
+            stored["down"][0, t] = part[:, :384].reshape(2, 2, -1, 384)
+            stored["down"][1, t] = part[:, 384:].reshape(2, 2, -1, 384)
+            return carry
+
+        lax.fori_loop(0, depth, grad_tile, 0)
+        place.greet()
+        for g in range(count):
+            if names[g] == "down":
+                scatter.start(g)
+        out_swap.start()
+        out_keep.start()
+        fetch_weight("down", w_down).wait()
+        fetch("d").wait()
+
+        def slope_tile(t, carry):
+            w0 = w_down.at[0, t][...].reshape(width, 384)
+            w1 = w_down.at[1, t][...].reshape(width, 384)
+            d_hidden = dot_t(d_f[:, :384], w0) + dot_t(d_f[:, 384:], w1)
+            at = lanes(t * width, width)
+            d_pre = (d_hidden * slope[:, at].astype(jnp.float32)).astype(jnp.bfloat16)
+            slope[:, at] = d_pre
+            vec_g[:, lanes(B1 + t * width, width)] = total(d_pre)
+            return carry
+
+        lax.fori_loop(0, depth, slope_tile, 0)
+
+    pl.run_scoped(with_down, pltpu.VMEM(w_in["down"].shape, jnp.bfloat16))
+    tick()
+
+    fetch("unit1").wait()
+    fetch("inv1").wait()
+    y1_low[...] = (unit1[...] * vector(G1) + vector(E1)).astype(jnp.bfloat16)
+
+    def with_up(w_up):
+        fetch_weight("up", w_up).start()
+
+        def up_tile(i, carry):
+            h, part = lax.rem(i, 2), lax.div(i, 2)
+            tile = dot_n(y1_low[...], slope[:, lanes(h * 1536 + part * width, width)])
+            stored["up"][h, :, :, :, :, lanes(part * width, width)] = tile.astype(
+                jnp.bfloat16
+            ).reshape(depth, 2, 2, -1, width)
+            return carry
+
+        lax.fori_loop(0, 4, up_tile, 0)
+        for g in range(count):
+            if names[g] == "up":
+                scatter.start(g)
+        tick()
+        fetch_weight("up", w_up).wait()
+
+        def back_tile(h, carry):
+            w = w_up.at[h][...].reshape(width, 1536)
+            unit2[...] += dot_t(slope[:, lanes(h * 1536, 1536)], w)
+            return carry
+
+        lax.fori_loop(0, 2, back_tile, 0)
+
+    pl.run_scoped(with_up, pltpu.VMEM(w_in["up"].shape, jnp.bfloat16))
+
+    unit = unit1[...]
+    d_y1 = unit2[...]
+    vec_g[:, G1 : G1 + width] = total(d_y1 * unit)
+    vec_g[:, E1 : E1 + width] = total(d_y1)
+    d_h1 = norm_back(d_y1, unit, inv1[:, 0:1], vector(G1))
+    unit1[...] = d_h1
+    d_a[...] = d_h1.astype(jnp.bfloat16)
+    vec_g[:, BO : BO + width] = total(d_a[...])
+    fetch("w_out").wait()
+    fetch("o").wait()
+    d_mixed[...] = (
+        dot_t(d_a[:, :384], w_out.at[0][...].reshape(width, 384))
+        + dot_t(d_a[:, 384:], w_out.at[1][...].reshape(width, 384))
+    ).astype(jnp.bfloat16)
+    part = dot_n(o_own[...].astype(jnp.bfloat16), d_a[...]).astype(jnp.bfloat16)
+    for h in range(2):
+        stored["out"][h] = part[:, h * 384 : (h + 1) * 384].reshape(depth, 2, 2, -1, 384)
+    scatter.start(names.index("out"))
+
+    for name in ("w_box", "qkv", "table", "x"):
+        fetch(name).wait()
+    low = w_box.at[0][...].reshape(width, 2 * FREQ)
+    high = w_box.at[1][...].reshape(width, 2 * FREQ)
+    box_w[...] = jnp.concatenate(
+        [low[:, :FREQ], high[:, :FREQ], low[:, FREQ:], high[:, FREQ:]], axis=1
+    )
+    keys[...] = table[...].astype(jnp.bfloat16)
+    table[...] = table[...] * (HEAD**-0.5)
+    head_lane = lax.broadcasted_iota(jnp.int32, (1, 128), 1)
+
+    def p_copy(p, slot, i):
+        at = lanes((slot * 2 + i) * page_len, page_len)
+        return pltpu.make_async_copy(p_in.at[p, i], hidden.at[:, at], p_sem.at[slot, i])
+
+    p_copy(0, 0, 0).start()
+    p_copy(0, 0, 1).start()
+
+    def with_qkv(w_qkv):
+        fetch_weight("qkv", w_qkv).start()
+        first_tick = position[0]
+
+        def pair(p, carry):
+            for i, at in enumerate(BACK_TICKS):
+                @pl.when(p == at)
+                def _():
+                    for event in timeline[first_tick + i]:
+                        event()
+
+            slot = lax.rem(p, 2)
+
+            @pl.when(p < HEADS // 2 - 1)
+            def _():
+                p_copy(p + 1, 1 - slot, 0).start()
+                p_copy(p + 1, 1 - slot, 1).start()
+
+            p_copy(p, slot, 0).wait()
+            p_copy(p, slot, 1).wait()
+            q = qkv[:, lanes(p * 128, 128)]
+            k = qkv[:, lanes(width + p * 128, 128)]
+            v = qkv[:, lanes(2 * width + p * 128, 128)]
+            w = box_w[pl.ds(pl.multiple_of(p * 128, 128), 128), :]
+            d_o = d_mixed[:, lanes(p * 128, 128)]
+            weighted = d_o.astype(jnp.float32) * o_own[:, lanes(p * 128, 128)]
+            grads = []
+            d_w = jnp.zeros((128, BOX_DIM), jnp.float32)
+            for i in range(2):
+                of_head = (head_lane < HEAD) == (i == 0)
+                probs = hidden[:, lanes((slot * 2 + i) * page_len, page_len)]
+                delta = jnp.sum(jnp.where(of_head, weighted, 0.0), axis=1, keepdims=True)
+                d_probs = dot_t(jnp.where(of_head, d_o, jnp.zeros_like(d_o)), v)
+                d_s = (probs.astype(jnp.float32) * (d_probs - delta)).astype(jnp.bfloat16)
+                d_q = jnp.dot(d_s, k, preferred_element_type=jnp.float32)
+                d_1 = jnp.dot(d_s, keys[0], preferred_element_type=jnp.float32)
+                d_2 = jnp.dot(d_s, keys[1], preferred_element_type=jnp.float32)
+                cosine, sine = table[0], table[1]
+                d_sine = (d_1 * sine - d_2 * cosine).astype(jnp.bfloat16)
+                d_cosine = (d_1 * cosine + d_2 * sine).astype(jnp.bfloat16)
+                d_u = jnp.concatenate([d_sine, d_cosine], axis=1)
+                d_q = d_q * (HEAD**-0.5) + dot_t(d_u, w)
+                d_w = d_w + dot_n(jnp.where(of_head, q, jnp.zeros_like(q)), d_u)
+                grads.append((d_q, dot_n(d_s, q) * (HEAD**-0.5), dot_n(probs, d_o)))
+            first_head = head_lane < HEAD
+            for n, (one, two) in enumerate(zip(*grads)):
+                value = jnp.where(first_head, one, two).astype(jnp.bfloat16)
+                slope[:, lanes(n * width + p * 128, 128)] = value
+                if n == 0:
+                    vec_g[:, lanes(BQ + p * 128, 128)] = total(value)
+                if n == 2:
+                    vec_g[:, lanes(BV + p * 128, 128)] = total(value)
+            box_g[pl.ds(pl.multiple_of(p * 128, 128), 128), :] = d_w.astype(jnp.bfloat16)
+            return carry
+
+        lax.fori_loop(0, HEADS // 2, pair, 0)
+        position[0] += len(BACK_TICKS)
+
+        part = box_g[...]
+        stored["box"][0] = jnp.concatenate(
+            [part[:, :FREQ], part[:, 2 * FREQ : 3 * FREQ]], axis=1
+        ).reshape(depth, 2, 2, -1, 384)
+        stored["box"][1] = jnp.concatenate(
+            [part[:, FREQ : 2 * FREQ], part[:, 3 * FREQ :]], axis=1
+        ).reshape(depth, 2, 2, -1, 384)
+        scatter.start(names.index("box"))
+        for g in range(count):
+            if names[g] == "down":
+                scatter.left(g)
+
+        height = stored["box"].shape[4]
+        for t in range(3):
+            def qkv_tile(h, carry, t=t):
+                tile = dot_n(x_own[...], slope[:, lanes(h * 1152 + t * 384, 384)])
+                stored["down"][h, :, :, :, t * height : (t + 1) * height, :] = tile.astype(
+                    jnp.bfloat16
+                ).reshape(depth, 2, 2, -1, 384)
+                return carry
+
+            lax.fori_loop(0, 2, qkv_tile, 0)
+            scatter.start([g for g in range(count) if names[g] == "qkv"][t])
+
+        for dz in range(depth):
+            for dx in range(2):
+                for dc in range(2):
+                    for dy in range(2):
+                        device = ((dz * 2 + dx) * 2 + dc) * 2 + dy
+                        start = device * (VECTORS // (8 * depth)) // 128 * 128
+                        pieces[dy, dz, dx, dc] = vec_g[:, start : start + 384]
+        vector_c.start()
+        fetch_weight("qkv", w_qkv).wait()
+
+        def back_tile(h, carry):
+            w = w_qkv.at[h][...].reshape(width, 1152)
+            unit1[...] += dot_t(slope[:, lanes(h * 1152, 1152)], w)
+            return carry
+
+        lax.fori_loop(0, 2, back_tile, 0)
+        dx_low[0] = unit1[rows(1 - y), :].astype(jnp.bfloat16)
+        dx_swap.start()
+        pltpu.make_async_copy(unit1.at[rows(y)], dx_out.at[y], out_sem.at[1]).start()
+
+    vector_c = remote(pieces.at[:, :, :, 1 - c], pc_land, v_sems, (0,), place.c_peer)
+    vector_y = remote(pieces.at[1 - y, :, :, c], py_land, v_sems, (1,), place.y_peer)
+    vector_x = remote(pieces.at[y, :, 1 - x, c], px_land, v_sems, (2,), place.x_peer)
+
+    def vector_z(k):
+        there = lax.rem(z + k + 1, depth)
+        return remote(
+            pieces.at[y, there, x, c], pz_land.at[k], vz_sems, (k,), place.z_peers[k]
+        )
+
+    pl.run_scoped(with_qkv, pltpu.VMEM(w_in["qkv"].shape, jnp.bfloat16))
+
+    vector_c.wait_recv()
+    pieces[:, :, :, c] += pc_land[...]
+    vector_y.start()
+    tick()
+    vector_y.wait_recv()
+    pieces[y, :, :, c] += py_land[...]
+    vector_x.start()
+    tick()
+    vector_x.wait_recv()
+    pieces[y, :, x, c] += px_land[...]
+    for k in range(depth - 1):
+        vector_z(k).start()
+    dx_swap.wait_recv()
+    unit2[0:block, :] = dx_low[1].astype(jnp.float32)
+    pltpu.make_async_copy(unit2.at[0:block], dx_out.at[1 - y], out_sem.at[2]).start()
+    while position[0] < len(timeline):
+        tick()
+    for k in range(depth - 1):
+        vector_z(k).wait_recv()
+    piece_total = pieces[y, z, x, c]
+    for k in range(depth - 1):
+        piece_total = piece_total + pz_land[k]
+    piece_sum[...] = piece_total
+    finals = [pltpu.make_async_copy(piece_sum, piece_out, out_sem.at[3])]
+    for i, name in enumerate(WEIGHTS):
+        finals.append(pltpu.make_async_copy(summed[name], grad_out[name], out_sem.at[4 + i]))
+    for copy in finals:
+        copy.start()
+    for g in range(count):
+        scatter.left(g)
+    for copy in (vector_c, vector_y, vector_x, out_swap, dx_swap):
+        copy.wait_send()
+    for k in range(depth - 1):
+        vector_z(k).wait_send()
+    out_swap.wait_recv()
+    out_keep.wait()
+    pltpu.make_async_copy(unit1.at[rows(y)], dx_out.at[y], out_sem.at[1]).wait()
+    pltpu.make_async_copy(unit2.at[0:block], dx_out.at[1 - y], out_sem.at[2]).wait()
+    for copy in finals:
+        copy.wait()
+
+
+BACK_TICKS = (0, 2, 4)
+
+
+def backward_call(depth, full, kept, shards):
+    low, single = jnp.bfloat16, jnp.float32
+    page_len, width = kept["x"].shape
+    heights = {n: s.shape[0] for n, s in zip(WEIGHTS, shards)}
+    tall, short = heights["down"], heights["qkv"]
+
+    def columns(name, first, left, right):
+        pieces = by_columns(name, short, first, left, right)
+        return (name, name) + pieces[1:] + (pieces[3],)
+
+    def third(t, left):
+        top = t * short
+        return (
+            "qkv",
+            "down",
+            (top, short, 0, left),
+            (top, short, left, 384 - left),
+            (top, short, 0, 384),
+            (0, short, t * 384, 384),
+        )
+
+    def slab(first, size):
+        pieces = by_rows("down", tall, first, size)
+        return ("down", "down") + pieces[1:] + (pieces[3],)
+
+    groups = [
+        slab(0, 256),
+        slab(256, 128),
+        columns("up", 0, 384, 384),
+        columns("up", 768, 384, 384),
+        columns("out", 0, 256, 128),
+        columns("box", 0, 128, 256),
+        third(0, 256),
+        third(1, 128),
+        third(2, 256),
+    ]
+    count = len(groups)
+    outs = [
+        jax.ShapeDtypeStruct((2, page_len // 2, width), low),
+        jax.ShapeDtypeStruct((2, page_len // 2, width), single),
+    ]
+    outs += [jax.ShapeDtypeStruct(s.shape, single) for s in shards]
+    outs += [jax.ShapeDtypeStruct((1, 384), single)]
+    by_name = dict(zip(WEIGHTS, shards))
+
+    def vmem(*shape, kind=low):
+        return pltpu.VMEM(shape, kind)
+
+    size = lambda cut: (cut[1], cut[3])
+    dma = pltpu.SemaphoreType.DMA
+    scratch = [vmem(2, depth, 2, 2, *by_name[n].shape) for n in ("box", "out", "up", "down")]
+    scratch += [vmem(2, depth, 2, *size(g[4])) for g in groups]
+    scratch += [vmem(depth, 2, *size(g[2])) for g in groups]
+    scratch += [vmem(2, depth, *size(g[3])) for g in groups]
+    scratch += [vmem(depth, *size(g[2])) for g in groups]
+    scratch += [vmem(depth, *size(g[3])) for g in groups]
+    scratch += [vmem(depth - 1, *size(g[4])) for g in groups]
+    scratch += [vmem(*s.shape, kind=single) for s in shards]
+    scratch += [vmem(*full[n].shape) for n in ("box", "out")]
+    scratch += [vmem(width, BOX_DIM), vmem(width, BOX_DIM)]
+    scratch += [vmem(*kept[n].shape, kind=kept[n].dtype) for n in ("x", "ct", "qkv", "table")]
+    scratch += [vmem(*kept["table"].shape)]
+    scratch += [
+        vmem(*kept[n].shape, kind=kept[n].dtype)
+        for n in ("o", "unit1", "inv1", "g", "d", "unit2", "inv2", "vec")
+    ]
+    scratch += [vmem(page_len, width)] * 4
+    scratch += [vmem(2, page_len // 2, width), vmem(1, VECTORS + 128, kind=single)]
+    scratch += [
+        vmem(2, depth, 2, 2, 1, 384, kind=single),
+        vmem(2, depth, 2, 1, 384, kind=single),
+        vmem(depth, 2, 1, 384, kind=single),
+        vmem(depth, 1, 384, kind=single),
+        vmem(depth - 1, 1, 384, kind=single),
+        vmem(1, 384, kind=single),
+    ]
+    scratch += [dma((count,))] * 2 + [dma((count, 4))] * 2 + [dma((count, depth - 1))] * 2
+    scratch += [dma((3,))] * 2 + [dma((depth - 1,))] * 2 + [dma((2,))] * 2
+    scratch += [dma((17,)), dma((2, 2)), dma((9,))]
+    anywhere = pl.BlockSpec(memory_space=pl.ANY)
+    operands = [full[n] for n in WEIGHTS] + list(kept.values())
+    plan = (depth, groups, page_len, width)
+    results = pl.pallas_call(
+        partial(backward_kernel, plan),
+        out_shape=outs,
+        in_specs=[anywhere] * len(operands),
+        out_specs=[anywhere] * len(outs),
+        scratch_shapes=scratch,
+        compiler_params=pltpu.CompilerParams(
+            collective_id=1, has_side_effects=True, vmem_limit_bytes=VMEM_BACK
+        ),
+    )(*operands)
+    return results
+
+
+VMEM_BACK = 63 * 2**20
+
+
 def fast_layer(tokens, boxes, lengths, wqkv, wbox, wout, wup, wdown, vectors, cotangent):
     depth = lax.axis_size("dp") // 4
-    width = tokens.shape[2]
     device = lax.axis_index("dp") * 2 + lax.axis_index("blk")
     own = vectors.shape[0]
     offset = lax.rem(device * own, 128)
@@ -808,79 +1401,9 @@
     )[None, :]
     shards = (wqkv, wbox, wout, wup, wdown)
     full, kept = forward_call(depth, tokens, cotangent, boxes, lengths, piece, shards)
-
-    def whole(name):
-        w = full[name]
-        w = w.reshape(2, -1, w.shape[-1])
-        return jnp.concatenate([w[0], w[1]], axis=1)
-
-    vec = kept["vec"][0, :VECTORS]
-    bq, bv, bo, g1, e1, b1, b2, g2, e2 = unpack(vec, width, 4 * width)
-    x = kept["x"]
-    page_len = x.shape[0]
-    head_shape = (page_len, HEADS, HEAD)
-    q, k, v = (kept["qkv"][:, i * width : (i + 1) * width].reshape(head_shape) for i in range(3))
-    cosine, sine = kept["table"][0], kept["table"][1]
-    table = jnp.concatenate(
-        [cosine[:, :FREQ], sine[:, :FREQ], cosine[:, FREQ:], sine[:, FREQ:]], axis=1
-    )
-    keys = table.astype(jnp.bfloat16)
-    probs = kept["p"].reshape(HEADS, page_len, page_len)
-    mixed_low = kept["o"].astype(jnp.bfloat16)
-    unit1, inv1, unit2, inv2 = kept["unit1"], kept["inv1"][:, :1], kept["unit2"], kept["inv2"][:, :1]
-    hidden = kept["g"]
-    y1_low = (unit1 * g1 + e1).astype(jnp.bfloat16)
-    output = (unit2 * g2 + e2).astype(jnp.bfloat16)
-    seed = kept["ct"].astype(jnp.float32)
-    d_h2, d_g2, d_e2 = normalize_back(seed, unit2, inv2, g2)
-    d_f = d_h2.astype(jnp.bfloat16)
-    d_hidden = dot32(d_f, whole("down").T)
-    d_pre = (d_hidden * kept["d"].astype(jnp.float32)).astype(jnp.bfloat16)
-    d_wdown = dot32(hidden.T, d_f)
-    d_wup = dot32(y1_low.T, d_pre)
-    d_y1 = dot32(d_pre, whole("up").T) + d_h2
-    d_h1, d_g1, d_e1 = normalize_back(d_y1, unit1, inv1, g1)
-    d_a = d_h1.astype(jnp.bfloat16)
-    d_wout = dot32(mixed_low.T, d_a)
-    d_mixed = dot32(d_a, whole("out").T).astype(jnp.bfloat16).reshape(head_shape)
-    row_delta = jnp.einsum("qhd,qhd->hq", d_mixed.astype(jnp.float32), kept["o"].reshape(head_shape))
-    d_probs = jnp.einsum("qhd,khd->hqk", d_mixed, v, preferred_element_type=jnp.float32)
-    d_raw = (probs * (d_probs - row_delta[..., None])).astype(jnp.bfloat16)
-    scale = HEAD**-0.5
-    d_q = jnp.einsum("hqk,khd->qhd", d_raw, k, preferred_element_type=jnp.float32)
-    d_box_q = jnp.einsum("hqk,kc->qhc", d_raw, keys, preferred_element_type=jnp.float32)
-    d_k = jnp.einsum("hqk,qhd->khd", d_raw, q, preferred_element_type=jnp.float32)
-    d_v = jnp.einsum("hqk,qhd->khd", probs, d_mixed, preferred_element_type=jnp.float32)
-    d_coeffs = unrotate(d_box_q * scale, table).astype(jnp.bfloat16)
-    box_heads = whole("box").reshape(HEADS, HEAD, BOX_DIM)
-    d_q = d_q * scale + jnp.einsum(
-        "qhc,hdc->qhd", d_coeffs, box_heads, preferred_element_type=jnp.float32
-    )
-    d_wbox = jnp.einsum("qhd,qhc->hdc", q, d_coeffs, preferred_element_type=jnp.float32)
-    flat = (-1, width)
-    d_q = d_q.astype(jnp.bfloat16).reshape(flat)
-    d_k = (d_k * scale).astype(jnp.bfloat16).reshape(flat)
-    d_v = d_v.astype(jnp.bfloat16).reshape(flat)
-    d_c = jnp.concatenate([d_q, d_k, d_v], axis=1)
-    d_wqkv = dot32(x.T, d_c)
-    d_x = dot32(d_c, whole("qkv").T) + d_h1
-    total = partial(jnp.sum, axis=0, dtype=jnp.float32)
-    vector_grad = jnp.concatenate(
-        [total(d_q), total(d_v), total(d_a), d_g1, d_e1, total(d_pre), total(d_f), d_g2, d_e2]
-    )
-    from_pages = partial(
-        lax.all_to_all, axis_name="blk", split_axis=1, concat_axis=0, tiled=True
-    )
-    return (
-        from_pages(output[None]),
-        from_pages(d_x[None]),
-        scatter_weight(d_wqkv),
-        scatter_weight(d_wbox.reshape(width, BOX_DIM)),
-        scatter_weight(d_wout),
-        scatter_weight(d_wup),
-        scatter_weight(d_wdown),
-        lax.psum_scatter(vector_grad, ("dp", "blk"), scatter_dimension=0, tiled=True),
-    )
+    results = backward_call(depth, full, kept, shards)
+    d_vectors = lax.dynamic_slice(results[7][0], (offset,), (own,))
+    return (*results[:7], d_vectors)
 
 
 def on_device(*args):

time: 561 us -> 208 us (0.37); the launches traced: 553 us -> 208 us
  waiting for transfers between devices: 241 us -> 0 us
  Pallas kernels: 93.2 us -> 198 us
  matrix products: 70.5 us -> 0 us
  local copies, waits for them, and re-layouts: 63.3 us -> 9.37 us
  blocking collectives: 39.8 us -> 0 us
  other arithmetic: 21.7 us -> 0 us
  between operations: 15.2 us -> 0.71 us
  starting transfers between devices: 7.96 us -> 0 us
    reduce_scatter x6 -> x0, waiting for transfers between devices: 230 us -> none  [the longest x5 218 us: scatter_weight(): lax.psum_scatter(grad.astype(jnp.bfloat16), 'dp', scatter_dimension=0, ti...]
    pallas_call x0 -> x1, Pallas kernels: none -> 105 us  [backward_call(): pl.pallas_call(partial(backward_kernel, plan), out_shape=outs, in_specs=[...]
    dot_general x15 -> x0, matrix products: 70.5 us -> none  [the longest x8 33 us: dot32(): return jnp.dot(a, b, preferred_element_type=jnp.float32)]
    unnamed x1 -> x0, blocking collectives: 39.8 us -> none
    slice x12 -> x0, local copies, waits for them, and re-layouts: 21.5 us -> none  [the longest x4 10.7 us: whole(): return jnp.concatenate([w[0], w[1]], axis=1)]
    unnamed x119 -> x21, local copies, waits for them, and re-layouts: 27.1 us -> 7.17 us
    unnamed x14 -> x0, waiting for transfers between devices: 10.5 us -> none
    another operation x1 -> x0, other arithmetic: 8.22 us -> none
  transfers between devices with their start and end apart: 12 -> 0, of which waited for: 6 -> 0; matrix products, arithmetic and copies ran while one was open for 23% -> 0% of each run, Pallas kernels for 0% -> 0%
where the time goes in v3:
time: 208 us
  Pallas kernels  198 us (95%)
  local copies, waits for them, and re-layouts  9.37 us (5%)
    pallas_call x1, Pallas kernels, backward_call(): pl.pallas_call(partial(backward_kernel, plan), out_shape=outs, in_specs=[...  105 us
    pallas_call x1, Pallas kernels, forward_call(): pl.pallas_call(partial(forward_kernel, plan), out_shape=outs, in_specs=[a...  92.9 us
    unnamed x21, local copies, waits for them, and re-layouts  7.17 us

profile of v3, /device:TPU:0, one launch (start us, length us, event | category | flops | bytes accessed | tf_op | source)
XLA Modules:
  0.0 208.2 jit_solution(18168776460026639752)
XLA Ops:
  0.6 0.7 reshape.20
  1.3 0.1 dynamic_update_slice.4.refs_4_
  1.4 0.0 copy-start.6
  1.4 0.6 copy-done.6
  2.0 92.9 %shard_map.170 = (bf16[2,4,2,2,48,1152]{5,4,3,2,1,0:T(8,128)(2,1)}, bf16[2,4,2,2,48,384]{5,4,3,2,1,0:T(8,128)(2,1)}, bf16[2,4,2,2,48,384]{5,4,3,2,1,0:T(8,128)(2...) custom-call(bf16[2,256,768]{2,1,0:T(8,128)(2,1)} %refs_0_.1, ...), custom_call_target="tpu_custom_call" | custom-call | tf_op jit(solution)/shard_map/pallas_call | solution.py:784
  94.8 105.3 %shard_map.171 = (bf16[2,256,768]{2,1,0:T(8,128)(2,1)}, f32[2,256,768]{2,1,0:T(8,128)}, f32[48,1152]{1,0:T(8,128)}, f32[48,384]{1,0:T(8,128)}, f32[48,384]{1,0:T...) custom-call(bf16[2,4,2,2,48,1152]{5,4,3,2,1,0:T(8,128)(2,1)} %get-tuple-element.34.refs_0_, ...), custom_call_target="tpu_custom_call" | custom-call | tf_op jit(solution)/shard_map/pallas_call | solution.py:1378
  200.1 0.0 copy-start
  200.1 1.4 dynamic-slice_reduce_fusion
  201.6 2.1 copy.27
  203.6 0.0 copy-done
  203.7 0.0 copy-start.3
  203.7 0.0 copy-start.5
  203.7 0.0 copy-start.4
  203.7 0.0 copy-start.2
  203.7 0.0 copy-start.1
  203.7 1.1 copy.28
  204.8 0.0 copy-done.3
  204.8 0.7 copy.29
  205.5 0.0 copy-done.5
  205.5 0.6 copy.30
  206.1 0.0 copy-done.4
  206.2 0.6 copy.31
  206.8 0.0 copy-done.2
  206.8 0.7 copy.32
  207.5 0.0 copy-done.1
  207.5 0.7 copy.33
  (1 shorter events, 0.0 us)
Async XLA Ops:
  1.4 0.6 copy-start.6
  200.1 3.5 %copy-start = (f32[2,256,768]{2,1,0:T(8,128)S(1)}, f32[2,256,768]{2,1,0:T(8,128)}, u32[]{:S(2)}) copy-start(f32[2,256,768]{2,1,0:T(8,128)} %get-tuple-element.69) | copy-start | bytes 4718596
  203.7 1.2 copy-start.3
  203.7 1.9 copy-start.5
  203.7 2.5 %copy-start.4 = (f32[48,384]{1,0:T(8,128)S(1)}, f32[48,384]{1,0:T(8,128)}, u32[]{:S(2)}) copy-start(f32[48,384]{1,0:T(8,128)} %get-tuple-element.72) | copy-start | bytes 221188
  203.7 3.1 %copy-start.2 = (f32[48,1536]{1,0:T(8,128)S(1)}, f32[48,1536]{1,0:T(8,128)}, u32[]{:S(2)}) copy-start(f32[48,1536]{1,0:T(8,128)} %get-tuple-element.73) | copy-start | bytes 884740
  203.7 3.8 %copy-start.1 = (f32[192,384]{1,0:T(8,128)S(1)}, f32[192,384]{1,0:T(8,128)}, u32[]{:S(2)}) copy-start(f32[192,384]{1,0:T(8,128)} %get-tuple-element.74) | copy-start | bytes 884740

commit v4 on v3

--- a/solution.py
+++ b/solution.py
@@ -196,58 +196,327 @@
     )
 
 
+GATHER_GROUPS = (
+    ("qkv", (0, 48, 0, 384), (("zxy", (0, 48, 0, 384)),)),
+    ("qkv", (0, 48, 384, 384), (("zyx", (0, 48, 384, 384)),)),
+    ("qkv", (0, 48, 768, 384), (("zyx", (0, 48, 768, 256)), ("yxz", (0, 48, 1024, 128)),)),
+    ("box", (0, 48, 0, 384), (("zxy", (0, 48, 0, 256)), ("yxz", (0, 48, 256, 128)),)),
+    ("out", (0, 48, 0, 384), (("zxy", (0, 48, 0, 256)), ("yzx", (0, 48, 256, 128)),)),
+    ("up", (0, 48, 0, 384), (("zyx", (0, 48, 0, 256)), ("yzx", (0, 48, 256, 128)),)),
+    ("up", (0, 48, 384, 384), (("zxy", (0, 48, 384, 384)),)),
+    ("up", (0, 48, 768, 384), (("zxy", (0, 48, 768, 128)), ("yxz", (0, 48, 896, 256)),)),
+    ("up", (0, 48, 1152, 384), (("zyx", (0, 48, 1152, 384)),)),
+    ("down", (0, 192, 0, 128), (("zyx", (0, 64, 0, 128)), ("yxz", (64, 128, 0, 128)),)),
+    ("down", (0, 192, 128, 128), (("zxy", (0, 128, 128, 128)), ("zyx", (128, 64, 128, 128)),)),
+    ("down", (0, 192, 256, 128), (("yxz", (0, 192, 256, 128)),)),
+)
+GATHER_EVENTS = (
+    (4.0, 0, 0, 0),
+    (4.0, 1, 0, 0),
+    (4.0, 2, 0, 0),
+    (4.0, 2, 1, 0),
+    (4.0, 3, 0, 0),
+    (4.0, 3, 1, 0),
+    (4.0, 4, 1, 0),
+    (4.0, 5, 1, 0),
+    (8.2, 0, 0, 10),
+    (10.1, 0, 0, 1),
+    (10.1, 4, 0, 0),
+    (10.5, 1, 0, 10),
+    (12.3, 2, 0, 10),
+    (12.5, 1, 0, 1),
+    (12.5, 5, 0, 0),
+    (13.8, 3, 0, 10),
+    (14.1, 2, 0, 1),
+    (14.1, 6, 0, 0),
+    (14.9, 2, 1, 1),
+    (14.9, 7, 1, 0),
+    (15.2, 3, 1, 1),
+    (15.2, 9, 1, 0),
+    (15.4, 4, 0, 10),
+    (15.4, 4, 1, 1),
+    (15.4, 11, 0, 0),
+    (15.5, 0, 0, 2),
+    (15.7, 5, 1, 1),
+    (15.8, 3, 0, 1),
+    (15.8, 7, 0, 0),
+    (17.3, 8, 0, 0),
+    (17.3, 4, 0, 1),
+    (17.6, 5, 0, 10),
+    (18.3, 2, 1, 2),
+    (18.8, 3, 1, 2),
+    (19.1, 1, 0, 2),
+    (20.0, 9, 0, 0),
+    (20.0, 5, 0, 1),
+    (20.1, 3, 0, 2),
+    (20.3, 4, 1, 11),
+    (21.4, 6, 0, 10),
+    (21.9, 5, 1, 11),
+    (22.1, 2, 0, 2),
+    (23.9, 7, 1, 1),
+    (24.2, 4, 1, 2),
+    (24.3, 4, 0, 2),
+    (24.6, 9, 1, 1),
+    (25.2, 10, 0, 0),
+    (25.2, 10, 1, 0),
+    (25.2, 6, 0, 1),
+    (25.6, 7, 0, 10),
+    (26.1, 11, 0, 1),
+    (26.4, 2, 1, 12),
+    (27.5, 5, 1, 2),
+    (28.5, 1, 0, 3),
+    (28.7, 0, 0, 3),
+    (29.0, 7, 0, 1),
+    (30.4, 0, 0, 4),
+    (30.6, 1, 0, 4),
+    (30.9, 8, 0, 10),
+    (31.1, 3, 1, 12),
+    (31.7, 2, 1, 3),
+    (32.8, 2, 1, 4),
+    (33.4, 8, 0, 1),
+    (33.7, 9, 0, 10),
+    (34.0, 5, 0, 2),
+    (35.0, 2, 0, 3),
+    (35.1, 3, 0, 3),
+    (35.1, 3, 1, 3),
+    (35.3, 9, 0, 1),
+    (35.6, 10, 0, 10),
+    (35.9, 7, 1, 2),
+    (36.4, 3, 1, 4),
+    (36.5, 2, 0, 4),
+    (36.6, 3, 0, 4),
+    (36.9, 10, 1, 10),
+    (37.8, 9, 1, 2),
+    (38.1, 10, 0, 1),
+    (39.1, 10, 1, 1),
+    (39.2, 4, 1, 3),
+    (40.3, 6, 0, 2),
+    (40.4, 4, 0, 3),
+    (40.4, 4, 1, 4),
+    (40.9, 7, 1, 12),
+    (41.0, 11, 0, 2),
+    (41.8, 4, 0, 4),
+    (42.7, 5, 1, 3),
+    (43.4, 7, 0, 2),
+    (43.5, 8, 0, 2),
+    (43.8, 5, 1, 4),
+    (44.9, 9, 0, 2),
+    (47.9, 7, 1, 3),
+    (48.5, 9, 1, 12),
+    (49.3, 7, 1, 4),
+    (50.0, 10, 1, 2),
+    (50.5, 5, 0, 3),
+    (51.9, 5, 0, 4),
+    (52.4, 6, 0, 3),
+    (53.3, 10, 0, 2),
+    (54.2, 6, 0, 4),
+    (54.9, -1, 0, 0),
+    (54.9, 7, 0, 3),
+    (56.1, 7, 0, 4),
+    (58.7, 9, 1, 3),
+    (59.6, 8, 0, 3),
+    (60.5, 11, 0, 12),
+    (60.6, 9, 1, 4),
+    (61.3, 10, 0, 3),
+    (61.3, 8, 0, 4),
+    (62.4, 9, 0, 3),
+    (63.0, 10, 0, 4),
+    (63.8, 9, 0, 4),
+    (65.2, 10, 1, 3),
+    (66.7, 10, 1, 4),
+    (69.4, 11, 0, 3),
+    (71.5, 11, 0, 4),
+)
+SCATTER_GROUPS = (
+    ("down", "down", (0, 192, 0, 128), (0, 192, 0, 128), (("xyz", (0, 128, 0, 128)), ("zyx", (128, 64, 0, 128)),)),
+    ("down", "down", (0, 192, 128, 128), (0, 192, 128, 128), (("yxz", (0, 128, 128, 128)), ("xzy", (128, 64, 128, 128)),)),
+    ("down", "down", (0, 192, 256, 128), (0, 192, 256, 128), (("xyz", (0, 128, 256, 128)), ("zxy", (128, 64, 256, 128)),)),
+    ("up", "up", (0, 48, 0, 384), (0, 48, 0, 384), (("yxz", (0, 48, 0, 256)), ("xyz", (0, 48, 256, 128)),)),
+    ("up", "up", (0, 48, 384, 384), (0, 48, 384, 384), (("xyz", (0, 48, 384, 256)), ("zxy", (0, 48, 640, 128)),)),
+    ("up", "up", (0, 48, 768, 384), (0, 48, 768, 384), (("yxz", (0, 48, 768, 256)), ("zxy", (0, 48, 1024, 128)),)),
+    ("up", "up", (0, 48, 1152, 384), (0, 48, 1152, 384), (("yxz", (0, 48, 1152, 256)), ("zyx", (0, 48, 1408, 128)),)),
+    ("out", "out", (0, 48, 0, 384), (0, 48, 0, 384), (("xyz", (0, 48, 0, 256)), ("zyx", (0, 48, 256, 128)),)),
+    ("box", "box", (0, 48, 0, 384), (0, 48, 0, 384), (("yxz", (0, 48, 0, 256)), ("zxy", (0, 48, 256, 128)),)),
+    ("qkv", "down", (0, 48, 0, 384), (0, 48, 0, 384), (("yxz", (0, 48, 0, 128)), ("xzy", (0, 48, 128, 256)),)),
+    ("qkv", "down", (48, 48, 0, 384), (0, 48, 384, 384), (("yxz", (48, 48, 0, 128)), ("xyz", (48, 48, 128, 128)), ("zyx", (48, 48, 256, 128)),)),
+    ("qkv", "down", (96, 48, 0, 384), (0, 48, 768, 384), (("yxz", (96, 48, 0, 128)), ("xyz", (96, 48, 128, 128)), ("xzy", (96, 48, 256, 128)),)),
+)
+SCATTER_EVENTS = (
+    (9.0, 0, 0, 0),
+    (10.1, 1, 0, 0),
+    (11.3, 2, 0, 0),
+    (13.6, 0, 1, 10),
+    (15.2, 3, 0, 0),
+    (16.2, 4, 0, 0),
+    (17.2, 5, 0, 0),
+    (17.4, 0, 1, 1),
+    (17.8, 0, 0, 1),
+    (18.2, 6, 0, 0),
+    (18.4, 2, 1, 10),
+    (19.0, 1, 0, 1),
+    (20.7, 1, 1, 1),
+    (22.6, 4, 1, 10),
+    (23.2, 2, 1, 1),
+    (23.2, 3, 0, 1),
+    (24.7, 7, 0, 0),
+    (26.3, 2, 0, 1),
+    (26.9, 5, 1, 10),
+    (27.0, 4, 1, 1),
+    (27.4, 0, 1, 2),
+    (27.7, 5, 0, 1),
+    (28.4, 3, 1, 1),
+    (30.0, -1, 0, 0),
+    (30.4, 5, 1, 1),
+    (30.6, 0, 0, 2),
+    (31.1, 6, 1, 10),
+    (32.6, 4, 0, 1),
+    (33.9, 1, 1, 11),
+    (34.3, 6, 1, 1),
+    (35.1, 6, 0, 1),
+    (35.4, 1, 0, 2),
+    (36.6, 1, 1, 2),
+    (37.0, 7, 1, 10),
+    (37.2, 2, 1, 2),
+    (37.9, 3, 0, 2),
+    (37.9, 2, 0, 2),
+    (39.0, 3, 1, 2),
+    (39.9, 0, 0, 12),
+    (40.2, 7, 1, 1),
+    (42.3, 0, 1, 3),
+    (42.6, 7, 0, 1),
+    (42.7, 1, 0, 12),
+    (43.1, 0, 0, 3),
+    (44.2, 4, 1, 2),
+    (45.0, 5, 0, 2),
+    (45.4, 3, 0, 12),
+    (45.6, 1, 0, 3),
+    (45.8, 5, 1, 2),
+    (47.6, 2, 0, 12),
+    (47.7, 8, 0, 0),
+    (47.9, 3, 0, 3),
+    (48.0, 6, 0, 2),
+    (49.5, 4, 0, 2),
+    (49.8, 3, 1, 12),
+    (50.0, 6, 1, 2),
+    (50.2, 2, 0, 3),
+    (50.4, 1, 1, 3),
+    (50.8, 2, 1, 3),
+    (50.8, 5, 0, 12),
+    (50.9, 9, 0, 0),
+    (50.9, 10, 0, 0),
+    (50.9, 11, 0, 0),
+    (51.3, 7, 1, 2),
+    (52.3, 3, 1, 3),
+    (53.0, 6, 0, 12),
+    (53.4, 7, 0, 2),
+    (53.6, 4, 1, 3),
+    (53.9, 5, 1, 3),
+    (54.3, 5, 0, 3),
+    (55.6, 8, 1, 10),
+    (55.9, 6, 0, 3),
+    (56.2, 9, 1, 1),
+    (56.4, 6, 1, 3),
+    (58.1, 8, 0, 1),
+    (58.5, 10, 1, 1),
+    (59.1, 8, 1, 1),
+    (59.3, 4, 0, 12),
+    (60.2, 9, 0, 1),
+    (60.6, 11, 1, 1),
+    (61.8, 4, 0, 3),
+    (61.9, 10, 2, 10),
+    (62.3, 10, 0, 1),
+    (62.7, 11, 2, 1),
+    (63.0, 7, 1, 3),
+    (64.4, 11, 0, 1),
+    (64.9, 7, 0, 12),
+    (65.1, 8, 0, 2),
+    (65.2, 10, 2, 1),
+    (65.6, 8, 1, 2),
+    (66.7, 9, 0, 2),
+    (67.4, 7, 0, 3),
+    (67.6, 9, 1, 11),
+    (67.7, 10, 0, 2),
+    (68.8, 11, 0, 2),
+    (71.1, 9, 1, 2),
+    (71.3, 11, 2, 11),
+    (73.4, 8, 0, 12),
+    (73.6, 11, 2, 2),
+    (73.9, 10, 1, 2),
+    (74.8, 9, 0, 12),
+    (75.0, 11, 1, 2),
+    (75.5, 8, 0, 3),
+    (75.5, 8, 1, 3),
+    (75.6, 10, 0, 12),
+    (75.6, 10, 2, 2),
+    (76.3, 9, 1, 3),
+    (76.4, 11, 0, 12),
+    (76.6, 9, 0, 3),
+    (77.0, 11, 2, 3),
+    (77.2, 10, 1, 12),
+    (77.3, 10, 0, 3),
+    (78.1, 11, 0, 3),
+    (78.2, 11, 1, 12),
+    (78.6, 10, 2, 3),
+    (79.0, 10, 1, 3),
+    (79.9, 11, 1, 3),
+)
+
+
 MESH = pl.DeviceIdType.MESH
 WEIGHTS = ("qkv", "box", "out", "up", "down")
 ROT = 4
 ALL = slice(None)
 
 
-def by_columns(name, height, first, left, right):
-    return (
-        name,
-        (0, height, first, left),
-        (0, height, first + left, right),
-        (0, height, first, left + right),
-    )
-
-
-def by_rows(name, height, first, count):
-    half = height // 2
-    return (
-        name,
-        (0, half, first, count),
-        (half, half, first, count),
-        (0, height, first, count),
-    )
-
-
 def window(piece):
     return (pl.ds(piece[0], piece[1]), pl.ds(piece[2], piece[3]))
 
 
 class Place:
-    def __init__(self, depth):
-        self.depth = depth
+    def __init__(self):
         dp = lax.axis_index("dp")
         self.y = lax.axis_index("blk")
         self.z = lax.div(dp, 4)
         self.x = lax.rem(lax.div(dp, 2), 2)
         self.c = lax.rem(dp, 2)
         x, y, z, c = self.x, self.y, self.z, self.c
-        self.z_peers = [(lax.rem(z + k, depth) * 4 + x * 2 + c, y) for k in range(1, depth)]
-        self.z_from = [lax.rem(z + depth - k, depth) for k in range(1, depth)]
+        self.near = z + 1 - 2 * lax.rem(z, 2)
+        self.far = lax.rem(z + 2, 4)
+        self.mirror = 3 - z
+        self.inner = jnp.logical_or(z == 1, z == 2)
+        self.end = jnp.logical_or(z == 0, z == 3)
+        at = lambda other: (other * 4 + x * 2 + c, y)
+        self.near_peer, self.far_peer, self.mirror_peer = at(self.near), at(self.far), at(self.mirror)
         self.x_peer = (dp + 2 - 4 * x, y)
         self.y_peer = (dp, 1 - y)
         self.c_peer = (dp + 1 - 2 * c, y)
 
+    def own(self):
+        return dict(y=self.y, z=self.z, x=self.x)
+
+    def vector_offset(self):
+        device = ((self.z * 2 + self.x) * 2 + self.c) * 2 + self.y
+        return lax.rem(device * (VECTORS // 32), 128)
+
     def greet(self):
         barrier = pltpu.get_barrier_semaphore()
-        peers = self.z_peers + [self.x_peer, self.y_peer, self.c_peer]
+        peers = [self.near_peer, self.far_peer, self.mirror_peer]
+        peers += [self.x_peer, self.y_peer, self.c_peer]
         for peer in peers:
             pl.semaphore_signal(barrier, inc=1, device_id=peer, device_id_type=MESH)
         pl.semaphore_wait(barrier, len(peers))
 
 
+def semaphore_table(groups):
+    table = {}
+    for g, group in enumerate(groups):
+        for part, (path, _) in enumerate(group[-1]):
+            for hop, axis in enumerate(path):
+                for slot in range(4 if axis == "z" else 1):
+                    table[g, part, hop, slot] = len(table)
+    return table
+
+
 def remote(src, dst, sems, at, peer):
     return pltpu.make_async_remote_copy(
         src, dst, sems[0].at[at], sems[1].at[at], device_id=peer, device_id_type=MESH
@@ -255,27 +524,38 @@
 
 
 class Gather:
-    def __init__(self, place, groups, shards, full, z_sems, xy_sems, c_sems, own_sem):
+    def __init__(self, place, groups, shards, full, sems, c_sems, own_sem):
         self.place, self.groups, self.shards, self.full = place, groups, shards, full
-        self.z_sems, self.xy_sems, self.c_sems, self.own_sem = z_sems, xy_sems, c_sems, own_sem
+        self.sems, self.c_sems, self.own_sem = sems, c_sems, own_sem
         self.count = len(groups)
-
-    def z_copy(self, g, k, arriving=False):
+        self.table = semaphore_table(groups)
+        self.owned = False
+
+    def copy(self, g, part, hop, slot, arriving=False):
         p = self.place
-        name, _, _, both = self.groups[g]
-        cut = window(both)
-        z = p.z_from[k] if arriving else p.z
-        return remote(
-            self.shards[name].at[cut],
-            self.full[name].at[(p.y, z, p.x, p.c) + cut],
-            self.z_sems,
-            (g, k),
-            p.z_peers[k],
-        )
+        name, _, parts = self.groups[g]
+        path, piece = parts[part]
+        cut = window(piece)
+        axis = path[hop]
+        at = p.own()
+        at.update({earlier: ALL for earlier in path[:hop]})
+        if axis == "z":
+            peer = (p.near_peer, p.far_peer, p.mirror_peer, p.near_peer)[slot]
+            if slot == 3:
+                at["z"] = p.mirror if arriving else p.far
+            elif arriving:
+                at["z"] = (p.near, p.far, p.mirror)[slot]
+        else:
+            peer = p.x_peer if axis == "x" else p.y_peer
+            if arriving:
+                at[axis] = 1 - at[axis]
+        ref = self.full[name].at[(at["y"], at["z"], at["x"], p.c) + cut]
+        source = self.shards[name].at[cut] if hop == 0 and slot < 3 else ref
+        return remote(source, ref, self.sems, (self.table[g, part, hop, slot],), peer)
 
     def own_copy(self, g):
         p = self.place
-        name, _, _, both = self.groups[g]
+        name, both, _ = self.groups[g]
         cut = window(both)
         return pltpu.make_async_copy(
             self.shards[name].at[cut],
@@ -283,78 +563,135 @@
             self.own_sem.at[g],
         )
 
-    def xy_copy(self, g, i, arriving=False):
+    def c_copy(self, g, part, arriving=False):
         p = self.place
-        name, left, right, _ = self.groups[g]
-        a, b = window(left), window(right)
-        y = 1 - p.y if arriving else p.y
-        x = 1 - p.x if arriving else p.x
-        index, peer = (
-            ((y, ALL, p.x, p.c) + b, p.y_peer),
-            ((p.y, ALL, x, p.c) + a, p.x_peer),
-            ((y, ALL, ALL, p.c) + a, p.y_peer),
-            ((ALL, ALL, x, p.c) + b, p.x_peer),
-        )[i]
-        ref = self.full[name].at[index]
-        return remote(ref, ref, self.xy_sems, (g, i), peer)
-
-    def c_copy(self, g, arriving=False):
-        p = self.place
-        name, _, _, both = self.groups[g]
+        name, _, parts = self.groups[g]
         c = 1 - p.c if arriving else p.c
-        ref = self.full[name].at[(ALL, ALL, ALL, c) + window(both)]
-        return remote(ref, ref, self.c_sems, (g,), p.c_peer)
-
-    def start(self, g):
-        for k in range(self.place.depth - 1):
-            self.z_copy(g, k).start()
-        self.own_copy(g).start()
-
-    def first(self, g):
-        self.own_copy(g).wait()
-        for k in range(self.place.depth - 1):
-            self.z_copy(g, k, True).wait_recv()
-        self.xy_copy(g, 0).start()
-        self.xy_copy(g, 1).start()
-
-    def second(self, g):
-        self.xy_copy(g, 1, True).wait_recv()
-        self.xy_copy(g, 2).start()
-        self.xy_copy(g, 0, True).wait_recv()
-        self.xy_copy(g, 3).start()
-
-    def third(self, g):
-        self.xy_copy(g, 2, True).wait_recv()
-        self.xy_copy(g, 3, True).wait_recv()
-        self.c_copy(g).start()
-
-    def ready(self, g):
-        self.c_copy(g, True).wait_recv()
-
-    def ticks(self, ahead):
-        out = [[partial(self.start, g) for g in range(min(ahead, self.count))]]
-        for t in range(self.count + 3):
-            tick = []
-            if t < self.count:
-                if t + ahead < self.count:
-                    tick.append(partial(self.start, t + ahead))
-                tick.append(partial(self.first, t))
-            if 0 <= t - 1 < self.count:
-                tick.append(partial(self.second, t - 1))
-            if 0 <= t - 2 < self.count:
-                tick.append(partial(self.third, t - 2))
-            if 0 <= t - 3 < self.count:
-                tick.append(partial(self.ready, t - 3))
-            out.append(tick)
-        return out
+        ref = self.full[name].at[(ALL, ALL, ALL, c) + window(parts[part][1])]
+        return remote(ref, ref, self.c_sems, (g, part), p.c_peer)
+
+    def relay(self, g, part, hop):
+        @pl.when(self.place.inner)
+        def _():
+            self.copy(g, part, hop, 1, True).wait_recv()
+            self.copy(g, part, hop, 3).start()
+
+    def start(self, g, part, hop):
+        if self.groups[g][2][part][0][hop] != "z":
+            self.copy(g, part, hop, 0).start()
+            return
+        self.copy(g, part, hop, 1).start()
+        self.copy(g, part, hop, 0).start()
+
+        @pl.when(self.place.inner)
+        def _():
+            self.copy(g, part, hop, 2).start()
+
+    def finish(self, g, part, hop):
+        self.copy(g, part, hop, 0, True).wait_recv()
+        if self.groups[g][2][part][0][hop] != "z":
+            return
+
+        @pl.when(self.place.inner)
+        def _():
+            self.copy(g, part, hop, 2, True).wait_recv()
+
+        @pl.when(self.place.end)
+        def _():
+            self.copy(g, part, hop, 1, True).wait_recv()
+            self.copy(g, part, hop, 3, True).wait_recv()
+
+    def own(self):
+        for g in range(self.count):
+            self.own_copy(g).start()
+
+    def step(self, g, part, step):
+        if step >= 10:
+            self.relay(g, part, step - 10)
+            return
+        if step >= 1 and not self.owned:
+            self.owned = True
+            for other in range(self.count):
+                self.own_copy(other).wait()
+        if 1 <= step <= 3:
+            self.finish(g, part, step - 1)
+        if step <= 2:
+            self.start(g, part, step)
+        if step == 3:
+            self.c_copy(g, part).start()
+        if step == 4:
+            self.c_copy(g, part, True).wait_recv()
 
     def drain(self):
-        for g in range(self.count):
-            for k in range(self.place.depth - 1):
-                self.z_copy(g, k).wait_send()
-            for i in range(4):
-                self.xy_copy(g, i).wait_send()
-            self.c_copy(g).wait_send()
+        for (g, part, hop, slot), _ in self.table.items():
+            copy = self.copy(g, part, hop, slot)
+            if slot < 2:
+                copy.wait_send()
+            else:
+                pl.when(self.place.inner)(copy.wait_send)
+        for g, (_, _, parts) in enumerate(self.groups):
+            for part in range(len(parts)):
+                self.c_copy(g, part).wait_send()
+
+
+class Clock:
+    def __init__(self, events, run, now, begun=None):
+        self.events, self.run, self.now, self.at, self.begun = events, run, now, 0, begun
+
+    def may(self, event):
+        return self.begun is None or event[1] < 0 or event[1] in self.begun
+
+    def take(self, until):
+        first = self.at
+        while self.at < len(self.events):
+            event = self.events[self.at]
+            if event[0] > until or not self.may(event):
+                break
+            self.at += 1
+        return self.events[first : self.at]
+
+    def catch_up(self):
+        for _, *event in self.take(self.now):
+            self.run(*event)
+
+    def spend(self, time):
+        self.now += time
+        self.catch_up()
+
+    def upto(self, *wanted):
+        last = max(i for i, (_, *event) in enumerate(self.events) if tuple(event) in wanted)
+        self.now = max(self.now, self.events[last][0])
+        while self.at <= last:
+            assert self.may(self.events[self.at])
+            _, *event = self.events[self.at]
+            self.at += 1
+            self.run(*event)
+
+    def loop(self, count, each, body, points=1):
+        due = [
+            [self.take(self.now + each * (i + k / points)) for k in range(points)]
+            for i in range(count)
+        ]
+        self.now += count * each
+
+        def wrapped(i, carry):
+            point = iter(range(points))
+
+            def serve():
+                k = next(point)
+                for n in range(count):
+                    if due[n][k]:
+
+                        @pl.when(i == n)
+                        def _():
+                            for _, *event in due[n][k]:
+                                self.run(*event)
+
+            serve()
+            return body(i, carry, serve)
+
+        lax.fori_loop(0, count, wrapped, 0)
+        self.catch_up()
 
 
 def sine_cosine(angle):
@@ -403,11 +740,11 @@
 
 
 def forward_kernel(plan, *refs):
-    depth, groups, page_len, width = plan
+    groups, page_len, width = plan
     block = page_len // 2
     refs = iter(refs)
     take = lambda n: [next(refs) for _ in range(n)]
-    tokens, cotangent, boxes, lengths, piece, frequency = take(6)
+    tokens, cotangent, boxes, lengths, vectors = take(5)
     shards = dict(zip(WEIGHTS, take(5)))
     full_out = dict(zip(WEIGHTS, take(5)))
     (x_out, ct_out, qkv_out, table_out, p_out, o_out, unit1_out, inv1_out) = take(8)
@@ -415,15 +752,16 @@
     full = dict(zip(WEIGHTS, take(5)))
     (x_own, boxes_peer, pieces, vec, qkv, table, keys, box_w, p_slots, o_own, o_low) = take(11)
     (unit1, inv1, y1_low, hidden, slope, unit2, inv2) = take(7)
-    z_sems, xy_sems, c_sems = take(2), take(2), take(2)
+    w_sems, c_sems = take(2), take(2)
     (own_sem,) = take(1)
     vz_sems, vxy_sems, vc_sems = take(2), take(2), take(2)
     ex_sems = take(2)
     (local_sem, p_sem, out_sem) = take(3)
-
-    place = Place(depth)
+    bias_qkv, piece = take(2)
+
+    place = Place()
     y, z, x, c = place.y, place.z, place.x, place.c
-    gather = Gather(place, groups, shards, full, z_sems, xy_sems, c_sems, own_sem)
+    gather = Gather(place, groups, shards, full, w_sems, c_sems, own_sem)
 
     def swap(i, source, target, arriving=False):
         at = (1 - y) if arriving else y
@@ -441,8 +779,9 @@
     box_swap = remote(boxes, boxes_peer, ex_sems, (2,), place.y_peer)
 
     def vector_z(k, arriving=False):
-        at = place.z_from[k] if arriving else z
-        return remote(piece, pieces.at[y, at, x, c], vz_sems, (k,), place.z_peers[k])
+        at = lax.rem(z + 4 - k, 4) if arriving else z
+        peer = (lax.rem(z + k, 4) * 4 + x * 2 + c, y)
+        return remote(piece, pieces.at[y, at, x, c], vz_sems, (k - 1,), peer)
 
     def vector_xy(i, arriving=False):
         at_x = 1 - x if arriving else x
@@ -457,20 +796,16 @@
 
     vector_own = pltpu.make_async_copy(piece, pieces.at[y, z, x, c], local_sem.at[2])
 
-    ready = [False] * gather.count
-    ticks = gather.ticks(AHEAD)
-    position = [0]
-
-    def tick(n=1):
-        for _ in range(n):
-            if position[0] < len(ticks):
-                for event in ticks[position[0]]:
-                    event()
-                position[0] += 1
+    def event(g, part, step):
+        if g < 0:
+            swap(1, cotangent, ct_out).start()
+        else:
+            gather.step(g, part, step)
+
+    clock = Clock(GATHER_EVENTS, event, 4.0)
 
     def need(g):
-        while position[0] < g + 5:
-            tick()
+        clock.upto(*((g, part, 4) for part in range(len(groups[g][2]))))
 
     outgoing = []
 
@@ -479,21 +814,28 @@
         copy.start()
         outgoing.append(copy)
 
+    own_vector = vectors[...].astype(jnp.float32).reshape(1, -1)
+    own_vector = jnp.concatenate(
+        [own_vector, jnp.zeros((1, 384 - own_vector.shape[1]), jnp.float32)], axis=1
+    )
+    own_vector = jnp.broadcast_to(own_vector, (8, 384))
+    piece[...] = pltpu.roll(own_vector, place.vector_offset(), 1)[0:1, :]
     place.greet()
+    gather.own()
     box_swap.start()
-    swap(0, tokens, x_own).start()
-    for k in range(depth - 1):
+    for k in range(1, 4):
         vector_z(k).start()
     vector_own.start()
-    tick()
+    swap(0, tokens, x_own).start()
+    clock.catch_up()
     keep(0, tokens, x_own).start()
     keep(1, cotangent, ct_out).start()
-
+    clock.spend(3.0)
     vector_own.wait()
-    for k in range(depth - 1):
+    for k in range(1, 4):
         vector_z(k, True).wait_recv()
     vector_xy(0).start()
-    tick()
+    clock.spend(3.0)
     vector_xy(0, True).wait_recv()
     vector_xy(1).start()
 
@@ -508,27 +850,29 @@
     both = jnp.concatenate([both, jnp.zeros((6, page_len), jnp.float32)], axis=0)
     across_up = both.T
     lane = lax.broadcasted_iota(jnp.int32, (1, 2 * FREQ), 1)
-    angle = jnp.where(lane < FREQ, across_up[:, 0:1], across_up[:, 1:2]) * frequency[...]
+    step = jnp.where(lane < FREQ, lane, lane - FREQ).astype(jnp.float32)
+    frequency = jnp.exp(step * (-math.log(10000.0) / FREQ))
+    angle = jnp.where(lane < FREQ, across_up[:, 0:1], across_up[:, 1:2]) * frequency
     sine, cosine = sine_cosine(angle)
     table[0], table[1] = cosine, sine
     keys[0], keys[1] = cosine.astype(jnp.bfloat16), sine.astype(jnp.bfloat16)
     send_out(table, table_out)
-    tick()
+    clock.spend(3.0)
     vector_xy(1, True).wait_recv()
     vector_c().start()
 
     keep(0, tokens, x_own).wait()
     swap(0, tokens, x_own, True).wait_recv()
     send_out(x_own, x_out)
-    tick()
+    clock.catch_up()
     vector_c(True).wait_recv()
     vec[...] = jnp.zeros_like(vec)
-    for dz in range(depth):
+    for dz in range(4):
         for dx in range(2):
             for dc in range(2):
                 for dy in range(2):
                     device = ((dz * 2 + dx) * 2 + dc) * 2 + dy
-                    start = device * (VECTORS // (8 * depth)) // 128 * 128
+                    start = device * (VECTORS // 32) // 128 * 128
                     vec[:, start : start + 384] += pieces[dy, dz, dx, dc]
     send_out(vec, vec_out)
 
@@ -536,7 +880,7 @@
         return vec[:, start : start + size]
 
     def project(first, count):
-        def body(h, carry):
+        def project_tile(h, carry):
             w = full["qkv"].at[h][:, :, :, :, first : first + count].reshape(width, count)
             out = jnp.dot(x_own[...], w, preferred_element_type=jnp.float32)
             start = pl.multiple_of(h * 1152 + first, 128)
@@ -545,16 +889,16 @@
             qkv[:, lanes(start, count)] = (out + bias).astype(jnp.bfloat16)
             return carry
 
-        lax.fori_loop(0, 2, body, 0)
-
-    bias_qkv = next(refs)
+        lax.fori_loop(0, 2, project_tile, 0)
+
     bias_qkv[:, 0:width] = vector(BQ)
     bias_qkv[:, width : 2 * width] = jnp.zeros((1, width), jnp.float32)
     bias_qkv[:, 2 * width : 3 * width] = vector(BV)
-    for g, (name, left, right, cut) in enumerate(groups):
+    for g, (name, cut, _) in enumerate(groups):
         if name == "qkv":
             need(g)
             project(cut[2], cut[3])
+            clock.spend(1.3)
     send_out(qkv, qkv_out)
 
     box_group = [g for g, group in enumerate(groups) if group[0] == "box"][-1]
@@ -571,16 +915,7 @@
     def p_copy(p, slot):
         return pltpu.make_async_copy(p_slots.at[slot], p_out.at[p], p_sem.at[slot])
 
-    first_tick = position[0]
-    per_pair = PAIR_TICKS
-
-    def pair(p, carry):
-        for i, event_list in enumerate(ticks[first_tick : first_tick + len(per_pair)]):
-            @pl.when(p == per_pair[i])
-            def _():
-                for event in event_list:
-                    event()
-
+    def pair(p, carry, serve):
         slot = lax.rem(p, 2)
 
         @pl.when(p >= 2)
@@ -593,6 +928,8 @@
         w = box_w[pl.ds(pl.multiple_of(p * 128, 128), 128), :]
         outs = []
         for i in range(2):
+            if i:
+                serve()
             of_head = (head_lane < HEAD) == (i == 0)
             q_head = jnp.where(of_head, q, jnp.zeros_like(q))
             u = jnp.dot(q_head, w, preferred_element_type=jnp.float32)
@@ -613,8 +950,7 @@
         p_copy(p, slot).start()
         return carry
 
-    lax.fori_loop(0, HEADS // 2, pair, 0)
-    position[0] += len(per_pair)
+    clock.loop(HEADS // 2, PAIR_TIME, pair, 2)
     p_copy(4, 0).wait()
     p_copy(5, 1).wait()
     send_out(o_own, o_out)
@@ -651,44 +987,46 @@
     send_out(inv1, inv1_out)
 
     def up_tile(first, h, t):
-        start = pl.multiple_of(first + t * 256, 128)
-        w = full["up"].at[h][:, :, :, :, pl.ds(start, 256)].reshape(width, 256)
-        at = lanes(h * 1536 + start, 256)
+        start = pl.multiple_of(first + t * UP_TILE, 128)
+        w = full["up"].at[h][:, :, :, :, pl.ds(start, UP_TILE)].reshape(width, UP_TILE)
+        at = lanes(h * 1536 + start, UP_TILE)
         pre = jnp.dot(y1_low[...], w, preferred_element_type=jnp.float32)
-        pre = pre + vec[:, lanes(B1 + h * 1536 + start, 256)]
+        pre = pre + vec[:, lanes(B1 + h * 1536 + start, UP_TILE)]
         half = 0.5 + 0.5 * lax.erf(pre * (2.0**-0.5))
         hidden[:, at] = (pre * half).astype(jnp.bfloat16)
         bell = jnp.exp(pre * pre * -0.5) * ((2.0 * math.pi) ** -0.5)
         slope[:, at] = (half + pre * bell).astype(jnp.bfloat16)
 
-    for g, (name, left, right, cut) in enumerate(groups):
+    clock.spend(2.0)
+    for g, (name, cut, _) in enumerate(groups):
         if name == "up":
             need(g)
-            tiles = cut[3] // 256
-
-            def body(i, carry, first=cut[2], tiles=tiles):
+            tiles = cut[3] // UP_TILE
+
+            def up_body(i, carry, first=cut[2], tiles=tiles):
                 up_tile(first, lax.div(i, tiles), lax.rem(i, tiles))
                 return carry
 
-            lax.fori_loop(0, 2 * tiles, body, 0)
+            lax.fori_loop(0, 2 * tiles, up_body, 0)
+            clock.spend(1.7)
     send_out(hidden, g_out)
     send_out(slope, d_out)
     weight_out("up")
 
-    for g, (name, left, right, cut) in enumerate(groups):
+    for g, (name, cut, _) in enumerate(groups):
         if name == "down":
             need(g)
             first, count = cut[2], cut[3]
 
-            def body(h, carry, first=first, count=count):
+            def down_body(h, carry, first=first, count=count):
                 w = full["down"].at[h][:, :, :, :, first : first + count].reshape(4 * width, count)
                 at = lanes(h * 384 + first, count)
                 unit2[:, at] += jnp.dot(hidden[...], w, preferred_element_type=jnp.float32)
                 return carry
 
-            lax.fori_loop(0, 2, body, 0)
-        if name == "up" and g == last_of("up"):
-            swap(1, cotangent, ct_out).start()
+            lax.fori_loop(0, 2, down_body, 0)
+            clock.spend(1.0)
+    clock.upto(*(tuple(event) for _, *event in GATHER_EVENTS))
     weight_out("down")
     unit, inverse = norm(unit2[...])
     unit2[...] = unit
@@ -697,7 +1035,7 @@
     send_out(inv2, inv2_out)
 
     gather.drain()
-    for k in range(depth - 1):
+    for k in range(1, 4):
         vector_z(k).wait_send()
     vector_xy(0).wait_send()
     vector_xy(1).wait_send()
@@ -711,28 +1049,16 @@
         copy.wait()
 
 
-AHEAD = 2
-PAIR_TICKS = (1, 4)
-
-
-def forward_call(depth, tokens, cotangent, boxes, lengths, piece, shards):
+PAIR_TIME = 3.3
+UP_TILE = 384
+
+
+def forward_call(tokens, cotangent, boxes, lengths, vectors, shards):
     page_len = tokens.shape[1] * 2
     width = tokens.shape[2]
-    heights = {n: s.shape[0] for n, s in zip(WEIGHTS, shards)}
-    groups = [
-        by_columns("qkv", heights["qkv"], 0, 256, 384),
-        by_columns("qkv", heights["qkv"], 640, 256, 256),
-        by_columns("box", heights["box"], 0, 128, 256),
-        by_columns("out", heights["out"], 0, 256, 128),
-        by_columns("up", heights["up"], 0, 384, 384),
-        by_columns("up", heights["up"], 768, 384, 384),
-        by_rows("down", heights["down"], 0, 256),
-        by_rows("down", heights["down"], 256, 128),
-    ]
+    groups = GATHER_GROUPS
     count = len(groups)
-    frequency = np.exp(np.arange(FREQ) * (-math.log(10000.0) / FREQ)).astype(np.float32)
-    frequency = jnp.asarray(np.tile(frequency, 2)[None, :])
-    full = [jax.ShapeDtypeStruct((2, depth, 2, 2) + s.shape, jnp.bfloat16) for s in shards]
+    full = [jax.ShapeDtypeStruct((2, 4, 2, 2) + s.shape, jnp.bfloat16) for s in shards]
     low, single = jnp.bfloat16, jnp.float32
     kinds = dict(
         x=((page_len, width), low),
@@ -758,7 +1084,7 @@
     scratch += [
         pltpu.VMEM((page_len, width), low),
         pltpu.VMEM(boxes.shape, jnp.int32),
-        pltpu.VMEM((2, depth, 2, 2, 1, 384), single),
+        pltpu.VMEM((2, 4, 2, 2, 1, 384), single),
         pltpu.VMEM((1, VECTORS + 128), single),
         pltpu.VMEM((page_len, 3 * width), low),
         pltpu.VMEM((2, page_len, 2 * FREQ), single),
@@ -775,149 +1101,182 @@
         pltpu.VMEM((page_len, width), single),
         pltpu.VMEM((page_len, 128), single),
     ]
-    scratch += [dma((count, depth - 1))] * 2 + [dma((count, 4))] * 2 + [dma((count,))] * 2
+    scratch += [dma((len(semaphore_table(groups)),))] * 2 + [dma((count, 3))] * 2
     scratch += [dma((count,))]
-    scratch += [dma((depth - 1,))] * 2 + [dma((2,))] * 2 + [dma((1,))] * 2
+    scratch += [dma((3,))] * 2 + [dma((2,))] * 2 + [dma((1,))] * 2
     scratch += [dma((3,))] * 2 + [dma((3,)), dma((2,)), dma((18,))]
-    scratch += [pltpu.VMEM((1, 3 * width), single)]
-    plan = (depth, groups, page_len, width)
+    scratch += [pltpu.VMEM((1, 3 * width), single), pltpu.VMEM((1, 384), single)]
+    plan = (groups, page_len, width)
     results = pl.pallas_call(
         partial(forward_kernel, plan),
         out_shape=outs,
-        in_specs=[anywhere, anywhere, vmem, smem, vmem, vmem] + [anywhere] * 5,
+        in_specs=[anywhere, anywhere, vmem, smem, vmem] + [anywhere] * 5,
         out_specs=[anywhere] * len(outs),
         scratch_shapes=scratch,
         compiler_params=pltpu.CompilerParams(
             collective_id=0, has_side_effects=True, vmem_limit_bytes=VMEM_LIMIT
         ),
-    )(tokens, cotangent, boxes, lengths, piece, frequency, *shards)
+    )(tokens, cotangent, boxes, lengths, vectors, *shards)
     return dict(zip(WEIGHTS, results[:5])), dict(zip(kinds, results[5:]))
 
 
 VMEM_LIMIT = 60 * 2**20
 
 
+def landing_shape(path, hop, piece):
+    sizes = dict(y=2, z=4, x=2)
+    to_come = [sizes[axis] for axis in "yzx" if axis in path[hop + 1 :]]
+    return (4 if path[hop] == "z" else 1, *to_come, piece[1], piece[3])
+
+
 class Scatter:
-    def __init__(self, place, groups, stored, landing, summed, sems):
+    def __init__(self, place, groups, stored, c_land, landing, summed, sems, c_sems):
         self.place, self.groups, self.stored, self.summed = place, groups, stored, summed
-        self.c_land, self.a1, self.b1, self.a2, self.b2, self.z_land = landing
-        self.c_sems, self.xy_sems, self.z_sems = sems
+        self.c_land, self.landing = c_land, landing
+        self.sems, self.c_sems = sems, c_sems
+        self.table = semaphore_table(groups)
         self.sent = set()
 
     def c_copy(self, g):
         p = self.place
-        _, store, _, _, both, _ = self.groups[g]
+        store, both = self.groups[g][1], self.groups[g][2]
         ref = self.stored[store].at[(ALL, ALL, ALL, 1 - p.c) + window(both)]
         return remote(ref, self.c_land[g], self.c_sems, (g,), p.c_peer)
 
-    def xy_copy(self, g, i):
+    def copy(self, g, part, hop, slot):
         p = self.place
-        _, store, left, right, _, _ = self.groups[g]
-        a, b = window(left), window(right)
-        index, land, peer = (
-            ((1 - p.y, ALL, ALL, p.c) + a, self.a1[g], p.y_peer),
-            ((ALL, ALL, 1 - p.x, p.c) + b, self.b1[g], p.x_peer),
-            ((p.y, ALL, 1 - p.x, p.c) + a, self.a2[g], p.x_peer),
-            ((1 - p.y, ALL, p.x, p.c) + b, self.b2[g], p.y_peer),
-        )[i]
-        return remote(self.stored[store].at[index], land, self.xy_sems, (g, i), peer)
-
-    def z_copy(self, g, k):
+        path, piece = self.groups[g][-1][part]
+        axis = path[hop]
+        at = p.own()
+        at.update({later: ALL for later in path[hop + 1 :]})
+        if axis == "z":
+            at["z"] = (p.near, p.far, p.mirror, p.mirror)[slot]
+            peer = (p.near_peer, p.far_peer, p.mirror_peer, p.near_peer)[slot]
+        else:
+            at[axis] = 1 - at[axis]
+            peer = p.x_peer if axis == "x" else p.y_peer
+        ref = self.stored[self.groups[g][1]].at[(at["y"], at["z"], at["x"], p.c) + window(piece)]
+        land = self.landing[g][part][hop].at[slot]
+        return remote(ref, land, self.sems, (self.table[g, part, hop, slot],), peer)
+
+    def add(self, g, part, hop, slots, place_z=None):
         p = self.place
-        _, store, _, _, both, _ = self.groups[g]
-        there = lax.rem(p.z + k + 1, p.depth)
-        ref = self.stored[store].at[(p.y, there, p.x, p.c) + window(both)]
-        return remote(ref, self.z_land[g].at[k], self.z_sems, (g, k), p.z_peers[k])
-
-    def add(self, g, piece, outer, arrived):
-        store = self.stored[self.groups[g][1]]
+        name, store, both, result, parts = self.groups[g]
+        store = self.stored[store]
+        path, piece = ("yzx", both) if hop < 0 else parts[part]
         cut = window(piece)
+        sizes = dict(y=2, z=4, x=2)
+        to_come = [axis for axis in "yzx" if axis in path[hop + 1 :]]
+        count = math.prod(sizes[axis] for axis in to_come)
+        land = self.c_land[g] if hop < 0 else self.landing[g][part][hop]
+
+        def block(i):
+            at = p.own()
+            if place_z is not None:
+                at["z"] = place_z
+            inner = []
+            for axis in to_come[::-1]:
+                at[axis] = lax.rem(i, sizes[axis])
+                i = lax.div(i, sizes[axis])
+                inner.insert(0, at[axis])
+            here = (at["y"], at["z"], at["x"], p.c) + cut
+            value = store[here].astype(jnp.float32)
+            for slot in slots:
+                arrived = land[tuple(inner)] if hop < 0 else land[(slot, *inner)]
+                value = value + arrived.astype(jnp.float32)
+            return here, value
+
+        if hop == 2 and place_z is None:
+            _, value = block(0)
+            top, height, first, size = piece
+            top, first = top - both[0] + result[0], first - both[2] + result[2]
+            self.summed[name][top : top + height, first : first + size] = value
+            return
 
         def body(i, carry):
-            here, there = outer(i)
-            store[here + cut] = (
-                store[here + cut].astype(jnp.float32) + arrived[there].astype(jnp.float32)
-            ).astype(jnp.bfloat16)
+            here, value = block(i)
+            store[here] = value.astype(jnp.bfloat16)
             return carry
 
-        return body
-
-    def run(self, count, body):
         lax.fori_loop(0, count, body, 0)
 
-    def start(self, g):
+    def begin(self, g):
         self.c_copy(g).start()
 
-    def first(self, g):
-        p, d = self.place, self.place.depth
-        _, _, left, right, both, _ = self.groups[g]
-        self.c_copy(g).wait_recv()
-
-        def outer(i):
-            dy, dz, dx = lax.div(i, 2 * d), lax.rem(lax.div(i, 2), d), lax.rem(i, 2)
-            return (dy, dz, dx, p.c), (dy, dz, dx)
-
-        self.run(4 * d, self.add(g, both, outer, self.c_land[g]))
-        self.xy_copy(g, 0).start()
-        self.xy_copy(g, 1).start()
-
-    def second(self, g):
-        p, d = self.place, self.place.depth
-        _, _, left, right, _, _ = self.groups[g]
-        self.xy_copy(g, 0).wait_recv()
-
-        def outer_a(i):
-            dz, dx = lax.div(i, 2), lax.rem(i, 2)
-            return (p.y, dz, dx, p.c), (dz, dx)
-
-        self.run(2 * d, self.add(g, left, outer_a, self.a1[g]))
-        self.xy_copy(g, 2).start()
-        self.xy_copy(g, 1).wait_recv()
-
-        def outer_b(i):
-            dy, dz = lax.div(i, d), lax.rem(i, d)
-            return (dy, dz, p.x, p.c), (dy, dz)
-
-        self.run(2 * d, self.add(g, right, outer_b, self.b1[g]))
-        self.xy_copy(g, 3).start()
-
-    def third(self, g):
-        p, d = self.place, self.place.depth
-        _, _, left, right, _, _ = self.groups[g]
-
-        def outer(i):
-            return (p.y, i, p.x, p.c), (i,)
-
-        self.xy_copy(g, 2).wait_recv()
-        self.run(d, self.add(g, left, outer, self.a2[g]))
-        self.xy_copy(g, 3).wait_recv()
-        self.run(d, self.add(g, right, outer, self.b2[g]))
-        for k in range(d - 1):
-            self.z_copy(g, k).start()
-
-    def fourth(self, g):
-        p, d = self.place, self.place.depth
-        name, store, _, _, both, result = self.groups[g]
-        for k in range(d - 1):
-            self.z_copy(g, k).wait_recv()
-        total = self.stored[store][(p.y, p.z, p.x, p.c) + window(both)].astype(jnp.float32)
-        for k in range(d - 1):
-            total = total + self.z_land[g][k].astype(jnp.float32)
-        self.summed[name][window(result)] = total
+    def start(self, g, part, hop):
+        p = self.place
+        if self.groups[g][-1][part][0][hop] != "z":
+            self.copy(g, part, hop, 0).start()
+            return
+
+        @pl.when(p.end)
+        def _():
+            self.copy(g, part, hop, 3).start()
+            self.copy(g, part, hop, 1).start()
+
+        self.copy(g, part, hop, 0).start()
+
+        @pl.when(p.inner)
+        def _():
+            self.copy(g, part, hop, 2).start()
+
+    def relay(self, g, part, hop):
+        p = self.place
+
+        @pl.when(p.inner)
+        def _():
+            self.copy(g, part, hop, 3).wait_recv()
+            self.add(g, part, hop, (3,), p.far)
+            self.copy(g, part, hop, 1).start()
+
+    def finish(self, g, part, hop):
+        p = self.place
+        self.copy(g, part, hop, 0).wait_recv()
+        if self.groups[g][-1][part][0][hop] != "z":
+            self.add(g, part, hop, (0,))
+            return
+        self.copy(g, part, hop, 1).wait_recv()
+
+        @pl.when(p.inner)
+        def _():
+            self.copy(g, part, hop, 2).wait_recv()
+            self.add(g, part, hop, (0, 1, 2))
+
+        @pl.when(p.end)
+        def _():
+            self.add(g, part, hop, (0, 1))
+
+    def step(self, g, part, step):
+        if step >= 10:
+            self.relay(g, part, step - 10)
+            return
+        if step == 0:
+            self.c_copy(g).wait_recv()
+            self.add(g, 0, -1, (0,))
+            for part in range(len(self.groups[g][-1])):
+                self.start(g, part, 0)
+            return
+        self.finish(g, part, step - 1)
+        if step < 3:
+            self.start(g, part, step)
 
     def left(self, g):
         if g in self.sent:
             return
         self.sent.add(g)
+        p = self.place
         self.c_copy(g).wait_send()
-        for i in range(4):
-            self.xy_copy(g, i).wait_send()
-        for k in range(self.place.depth - 1):
-            self.z_copy(g, k).wait_send()
+        for (group, part, hop, slot), _ in self.table.items():
+            if group == g:
+                wait = self.copy(g, part, hop, slot).wait_send
+                if slot < 2:
+                    wait()
+                else:
+                    pl.when(p.inner if slot == 2 else p.end)(wait)
 
 
 def backward_kernel(plan, *refs):
-    depth, groups, page_len, width = plan
+    groups, page_len, width = plan
     block = page_len // 2
     refs = iter(refs)
     take = lambda n: [next(refs) for _ in range(n)]
@@ -929,19 +1288,20 @@
     (piece_out,) = take(1)
     stored = dict(zip(("box", "out", "up", "down"), take(4)))
     count = len(groups)
-    landing = [take(count) for _ in range(6)]
+    c_land = take(count)
+    landing = [[take(3) for _ in group[-1]] for group in groups]
     summed = dict(zip(WEIGHTS, take(5)))
     w_box, w_out, box_w, box_g = take(4)
     (x_own, ct, qkv, table, keys, o_own, unit1, inv1, hidden, slope, unit2, inv2, vec) = take(13)
     (y1_low, d_a, d_mixed, out_low, dx_low, vec_g) = take(6)
     pieces, pc_land, py_land, px_land, pz_land, piece_sum = take(6)
-    c_sems, xy_sems, z_sems = take(2), take(2), take(2)
+    w_sems, c_sems = take(2), take(2)
     v_sems, vz_sems, ex_sems = take(2), take(2), take(2)
     in_sem, p_sem, out_sem = take(3)
 
-    place = Place(depth)
+    place = Place()
     y, z, x, c = place.y, place.z, place.x, place.c
-    scatter = Scatter(place, groups, stored, landing, summed, (c_sems, xy_sems, z_sems))
+    scatter = Scatter(place, groups, stored, c_land, landing, summed, w_sems, c_sems)
 
     sources = dict(
         unit2=(unit2_in, unit2),
@@ -982,31 +1342,22 @@
         return inverse * (scaled - mean_grad - unit * mean_unit)
 
     names = [group[0] for group in groups]
-    pending = []
-
-    def stages(g):
-        tick = []
-        if 0 <= g < count:
-            tick.append(partial(scatter.first, g))
-        if 0 <= g - 1 < count:
-            tick.append(partial(scatter.second, g - 1))
-        if 0 <= g - 2 < count:
-            tick.append(partial(scatter.third, g - 2))
-        if 0 <= g - 3 < count:
-            tick.append(partial(scatter.fourth, g - 3))
-        return tick
-
-    timeline = [stages(t) for t in range(count + 3)]
-    position = [0]
-
-    def tick(n=1):
-        for _ in range(n):
-            for event in timeline[position[0]]:
-                event()
-            position[0] += 1
-
-    for name in order:
+
+    def event(g, part, step):
+        if g < 0:
+            out_swap.start()
+        else:
+            scatter.step(g, part, step)
+
+    clock = Clock(SCATTER_EVENTS, event, 0.0, set())
+
+    def begin(g):
+        clock.begun.add(g)
+        scatter.begin(g)
+
+    for name in ("unit2", "ct", "inv2", "vec", "g"):
         fetch(name).start()
+    place.greet()
 
     fetch("unit2").wait()
     fetch("ct").wait()
@@ -1034,24 +1385,36 @@
         fetch_weight("down", w_down).start()
         fetch("g").wait()
 
-        def grad_tile(t, carry):
-            rows_g = hidden[:, lanes(t * width, width)]
-            part = dot_n(rows_g, d_f[...]).astype(jnp.bfloat16)
-            stored["down"][0, t] = part[:, :384].reshape(2, 2, -1, 384)
-            stored["down"][1, t] = part[:, 384:].reshape(2, 2, -1, 384)
-            return carry
-
-        lax.fori_loop(0, depth, grad_tile, 0)
-        place.greet()
-        for g in range(count):
-            if names[g] == "down":
-                scatter.start(g)
-        out_swap.start()
+        for name in ("d", "unit1", "inv1", "w_out", "o", "w_box", "qkv", "table", "x"):
+            fetch(name).start()
+
+        def down_grads(first, size):
+            left = d_f[:, first : first + size]
+            right = d_f[:, 384 + first : 384 + first + size]
+            both = jnp.concatenate([left, right], axis=1)
+
+            def grad_tile(t, carry):
+                part = dot_n(hidden[:, lanes(t * width, width)], both).astype(jnp.bfloat16)
+                for h in range(2):
+                    stored["down"][h, t, :, :, :, first : first + size] = part[
+                        :, h * size : (h + 1) * size
+                    ].reshape(2, 2, -1, size)
+                return carry
+
+            lax.fori_loop(0, 4, grad_tile, 0)
+            for g, group in enumerate(groups):
+                if group[0] == "down" and first <= group[2][2] < first + size:
+                    begin(g)
+            clock.spend(DOWN_TIME)
+
+        clock.now = START_TIME
+        down_grads(0, 128)
+        down_grads(128, 256)
         out_keep.start()
         fetch_weight("down", w_down).wait()
         fetch("d").wait()
 
-        def slope_tile(t, carry):
+        def slope_tile(t, carry, serve):
             w0 = w_down.at[0, t][...].reshape(width, 384)
             w1 = w_down.at[1, t][...].reshape(width, 384)
             d_hidden = dot_t(d_f[:, :384], w0) + dot_t(d_f[:, 384:], w1)
@@ -1061,10 +1424,9 @@
             vec_g[:, lanes(B1 + t * width, width)] = total(d_pre)
             return carry
 
-        lax.fori_loop(0, depth, slope_tile, 0)
+        clock.loop(4, SLOPE_TIME, slope_tile)
 
     pl.run_scoped(with_down, pltpu.VMEM(w_in["down"].shape, jnp.bfloat16))
-    tick()
 
     fetch("unit1").wait()
     fetch("inv1").wait()
@@ -1073,27 +1435,26 @@
     def with_up(w_up):
         fetch_weight("up", w_up).start()
 
-        def up_tile(i, carry):
-            h, part = lax.rem(i, 2), lax.div(i, 2)
-            tile = dot_n(y1_low[...], slope[:, lanes(h * 1536 + part * width, width)])
-            stored["up"][h, :, :, :, :, lanes(part * width, width)] = tile.astype(
+        def up_tile(i, carry, serve, part):
+            tile = dot_n(y1_low[...], slope[:, lanes(i * 1536 + part * width, width)])
+            stored["up"][i, :, :, :, :, part * width : (part + 1) * width] = tile.astype(
                 jnp.bfloat16
-            ).reshape(depth, 2, 2, -1, width)
+            ).reshape(4, 2, 2, -1, width)
             return carry
 
-        lax.fori_loop(0, 4, up_tile, 0)
-        for g in range(count):
-            if names[g] == "up":
-                scatter.start(g)
-        tick()
+        for part in range(2):
+            clock.loop(2, UP_TIME, partial(up_tile, part=part))
+            for g, group in enumerate(groups):
+                if group[0] == "up" and group[2][2] // width == part:
+                    begin(g)
         fetch_weight("up", w_up).wait()
 
-        def back_tile(h, carry):
+        def back_tile(h, carry, serve):
             w = w_up.at[h][...].reshape(width, 1536)
             unit2[...] += dot_t(slope[:, lanes(h * 1536, 1536)], w)
             return carry
 
-        lax.fori_loop(0, 2, back_tile, 0)
+        clock.loop(2, UP_BACK_TIME, back_tile)
 
     pl.run_scoped(with_up, pltpu.VMEM(w_in["up"].shape, jnp.bfloat16))
 
@@ -1113,8 +1474,9 @@
     ).astype(jnp.bfloat16)
     part = dot_n(o_own[...].astype(jnp.bfloat16), d_a[...]).astype(jnp.bfloat16)
     for h in range(2):
-        stored["out"][h] = part[:, h * 384 : (h + 1) * 384].reshape(depth, 2, 2, -1, 384)
-    scatter.start(names.index("out"))
+        stored["out"][h] = part[:, h * 384 : (h + 1) * 384].reshape(4, 2, 2, -1, 384)
+    begin(names.index("out"))
+    clock.spend(NORM_TIME)
 
     for name in ("w_box", "qkv", "table", "x"):
         fetch(name).wait()
@@ -1136,15 +1498,8 @@
 
     def with_qkv(w_qkv):
         fetch_weight("qkv", w_qkv).start()
-        first_tick = position[0]
-
-        def pair(p, carry):
-            for i, at in enumerate(BACK_TICKS):
-                @pl.when(p == at)
-                def _():
-                    for event in timeline[first_tick + i]:
-                        event()
-
+
+        def pair(p, carry, serve):
             slot = lax.rem(p, 2)
 
             @pl.when(p < HEADS // 2 - 1)
@@ -1163,6 +1518,8 @@
             grads = []
             d_w = jnp.zeros((128, BOX_DIM), jnp.float32)
             for i in range(2):
+                if i:
+                    serve()
                 of_head = (head_lane < HEAD) == (i == 0)
                 probs = hidden[:, lanes((slot * 2 + i) * page_len, page_len)]
                 delta = jnp.sum(jnp.where(of_head, weighted, 0.0), axis=1, keepdims=True)
@@ -1189,17 +1546,23 @@
             box_g[pl.ds(pl.multiple_of(p * 128, 128), 128), :] = d_w.astype(jnp.bfloat16)
             return carry
 
-        lax.fori_loop(0, HEADS // 2, pair, 0)
-        position[0] += len(BACK_TICKS)
+        clock.loop(HEADS // 2, PAIR_BACK_TIME, pair, 2)
 
         part = box_g[...]
         stored["box"][0] = jnp.concatenate(
             [part[:, :FREQ], part[:, 2 * FREQ : 3 * FREQ]], axis=1
-        ).reshape(depth, 2, 2, -1, 384)
+        ).reshape(4, 2, 2, -1, 384)
         stored["box"][1] = jnp.concatenate(
             [part[:, FREQ : 2 * FREQ], part[:, 3 * FREQ :]], axis=1
-        ).reshape(depth, 2, 2, -1, 384)
-        scatter.start(names.index("box"))
+        ).reshape(4, 2, 2, -1, 384)
+        begin(names.index("box"))
+        clock.spend(0.5)
+        clock.upto(*[
+            (g, part, 3)
+            for g, group in enumerate(groups)
+            if names[g] == "down"
+            for part in range(len(group[-1]))
+        ])
         for g in range(count):
             if names[g] == "down":
                 scatter.left(g)
@@ -1210,28 +1573,29 @@
                 tile = dot_n(x_own[...], slope[:, lanes(h * 1152 + t * 384, 384)])
                 stored["down"][h, :, :, :, t * height : (t + 1) * height, :] = tile.astype(
                     jnp.bfloat16
-                ).reshape(depth, 2, 2, -1, 384)
+                ).reshape(4, 2, 2, -1, 384)
                 return carry
 
             lax.fori_loop(0, 2, qkv_tile, 0)
-            scatter.start([g for g in range(count) if names[g] == "qkv"][t])
-
-        for dz in range(depth):
+            begin([g for g in range(count) if names[g] == "qkv"][t])
+            clock.spend(1.0)
+
+        for dz in range(4):
             for dx in range(2):
                 for dc in range(2):
                     for dy in range(2):
                         device = ((dz * 2 + dx) * 2 + dc) * 2 + dy
-                        start = device * (VECTORS // (8 * depth)) // 128 * 128
+                        start = device * (VECTORS // 32) // 128 * 128
                         pieces[dy, dz, dx, dc] = vec_g[:, start : start + 384]
         vector_c.start()
         fetch_weight("qkv", w_qkv).wait()
 
-        def back_tile(h, carry):
+        def back_tile(h, carry, serve):
             w = w_qkv.at[h][...].reshape(width, 1152)
             unit1[...] += dot_t(slope[:, lanes(h * 1152, 1152)], w)
             return carry
 
-        lax.fori_loop(0, 2, back_tile, 0)
+        clock.loop(2, 1.0, back_tile)
         dx_low[0] = unit1[rows(1 - y), :].astype(jnp.bfloat16)
         dx_swap.start()
         pltpu.make_async_copy(unit1.at[rows(y)], dx_out.at[y], out_sem.at[1]).start()
@@ -1241,34 +1605,32 @@
     vector_x = remote(pieces.at[y, :, 1 - x, c], px_land, v_sems, (2,), place.x_peer)
 
     def vector_z(k):
-        there = lax.rem(z + k + 1, depth)
-        return remote(
-            pieces.at[y, there, x, c], pz_land.at[k], vz_sems, (k,), place.z_peers[k]
-        )
+        there = lax.rem(z + k + 1, 4)
+        peer = (there * 4 + x * 2 + c, y)
+        return remote(pieces.at[y, there, x, c], pz_land.at[k], vz_sems, (k,), peer)
 
     pl.run_scoped(with_qkv, pltpu.VMEM(w_in["qkv"].shape, jnp.bfloat16))
 
     vector_c.wait_recv()
     pieces[:, :, :, c] += pc_land[...]
     vector_y.start()
-    tick()
+    clock.spend(3.0)
     vector_y.wait_recv()
     pieces[y, :, :, c] += py_land[...]
     vector_x.start()
-    tick()
+    clock.spend(3.0)
     vector_x.wait_recv()
     pieces[y, :, x, c] += px_land[...]
-    for k in range(depth - 1):
+    for k in range(3):
         vector_z(k).start()
+    clock.upto(*(tuple(event) for _, *event in SCATTER_EVENTS))
     dx_swap.wait_recv()
     unit2[0:block, :] = dx_low[1].astype(jnp.float32)
     pltpu.make_async_copy(unit2.at[0:block], dx_out.at[1 - y], out_sem.at[2]).start()
-    while position[0] < len(timeline):
-        tick()
-    for k in range(depth - 1):
+    for k in range(3):
         vector_z(k).wait_recv()
     piece_total = pieces[y, z, x, c]
-    for k in range(depth - 1):
+    for k in range(3):
         piece_total = piece_total + pz_land[k]
     piece_sum[...] = piece_total
     finals = [pltpu.make_async_copy(piece_sum, piece_out, out_sem.at[3])]
@@ -1280,7 +1642,7 @@
         scatter.left(g)
     for copy in (vector_c, vector_y, vector_x, out_swap, dx_swap):
         copy.wait_send()
-    for k in range(depth - 1):
+    for k in range(3):
         vector_z(k).wait_send()
     out_swap.wait_recv()
     out_keep.wait()
@@ -1290,45 +1652,19 @@
         copy.wait()
 
 
-BACK_TICKS = (0, 2, 4)
-
-
-def backward_call(depth, full, kept, shards):
+START_TIME = 6.0
+DOWN_TIME = 1.0
+SLOPE_TIME = 1.0
+UP_TIME = 0.8
+UP_BACK_TIME = 1.4
+NORM_TIME = 4.5
+PAIR_BACK_TIME = 3.4
+
+
+def backward_call(full, kept, shards):
     low, single = jnp.bfloat16, jnp.float32
     page_len, width = kept["x"].shape
-    heights = {n: s.shape[0] for n, s in zip(WEIGHTS, shards)}
-    tall, short = heights["down"], heights["qkv"]
-
-    def columns(name, first, left, right):
-        pieces = by_columns(name, short, first, left, right)
-        return (name, name) + pieces[1:] + (pieces[3],)
-
-    def third(t, left):
-        top = t * short
-        return (
-            "qkv",
-            "down",
-            (top, short, 0, left),
-            (top, short, left, 384 - left),
-            (top, short, 0, 384),
-            (0, short, t * 384, 384),
-        )
-
-    def slab(first, size):
-        pieces = by_rows("down", tall, first, size)
-        return ("down", "down") + pieces[1:] + (pieces[3],)
-
-    groups = [
-        slab(0, 256),
-        slab(256, 128),
-        columns("up", 0, 384, 384),
-        columns("up", 768, 384, 384),
-        columns("out", 0, 256, 128),
-        columns("box", 0, 128, 256),
-        third(0, 256),
-        third(1, 128),
-        third(2, 256),
-    ]
+    groups = SCATTER_GROUPS
     count = len(groups)
     outs = [
         jax.ShapeDtypeStruct((2, page_len // 2, width), low),
@@ -1343,13 +1679,11 @@
 
     size = lambda cut: (cut[1], cut[3])
     dma = pltpu.SemaphoreType.DMA
-    scratch = [vmem(2, depth, 2, 2, *by_name[n].shape) for n in ("box", "out", "up", "down")]
-    scratch += [vmem(2, depth, 2, *size(g[4])) for g in groups]
-    scratch += [vmem(depth, 2, *size(g[2])) for g in groups]
-    scratch += [vmem(2, depth, *size(g[3])) for g in groups]
-    scratch += [vmem(depth, *size(g[2])) for g in groups]
-    scratch += [vmem(depth, *size(g[3])) for g in groups]
-    scratch += [vmem(depth - 1, *size(g[4])) for g in groups]
+    scratch = [vmem(2, 4, 2, 2, *by_name[n].shape) for n in ("box", "out", "up", "down")]
+    scratch += [vmem(2, 4, 2, *size(g[2])) for g in groups]
+    for group in groups:
+        for path, piece in group[-1]:
+            scratch += [vmem(*landing_shape(path, hop, piece)) for hop in range(3)]
     scratch += [vmem(*s.shape, kind=single) for s in shards]
     scratch += [vmem(*full[n].shape) for n in ("box", "out")]
     scratch += [vmem(width, BOX_DIM), vmem(width, BOX_DIM)]
@@ -1362,19 +1696,19 @@
     scratch += [vmem(page_len, width)] * 4
     scratch += [vmem(2, page_len // 2, width), vmem(1, VECTORS + 128, kind=single)]
     scratch += [
-        vmem(2, depth, 2, 2, 1, 384, kind=single),
-        vmem(2, depth, 2, 1, 384, kind=single),
-        vmem(depth, 2, 1, 384, kind=single),
-        vmem(depth, 1, 384, kind=single),
-        vmem(depth - 1, 1, 384, kind=single),
+        vmem(2, 4, 2, 2, 1, 384, kind=single),
+        vmem(2, 4, 2, 1, 384, kind=single),
+        vmem(4, 2, 1, 384, kind=single),
+        vmem(4, 1, 384, kind=single),
+        vmem(3, 1, 384, kind=single),
         vmem(1, 384, kind=single),
     ]
-    scratch += [dma((count,))] * 2 + [dma((count, 4))] * 2 + [dma((count, depth - 1))] * 2
-    scratch += [dma((3,))] * 2 + [dma((depth - 1,))] * 2 + [dma((2,))] * 2
+    scratch += [dma((len(semaphore_table(groups)),))] * 2 + [dma((count,))] * 2
+    scratch += [dma((3,))] * 2 + [dma((3,))] * 2 + [dma((2,))] * 2
     scratch += [dma((17,)), dma((2, 2)), dma((9,))]
     anywhere = pl.BlockSpec(memory_space=pl.ANY)
     operands = [full[n] for n in WEIGHTS] + list(kept.values())
-    plan = (depth, groups, page_len, width)
+    plan = (groups, page_len, width)
     results = pl.pallas_call(
         partial(backward_kernel, plan),
         out_shape=outs,
@@ -1391,19 +1725,33 @@
 VMEM_BACK = 63 * 2**20
 
 
+def finish_kernel(*refs):
+    count = len(refs) // 2
+    ins, outs = refs[:count], refs[count:]
+    for i in range(count - 1):
+        outs[i][...] = ins[i][...]
+    rows = jnp.broadcast_to(ins[-1][...], (8, 384))
+    rows = pltpu.roll(rows, 384 - Place().vector_offset(), 1)
+    outs[-1][...] = rows[0:1, : VECTORS // 32].reshape(VECTORS // 32)
+
+
+def finish_call(results):
+    vmem = pl.BlockSpec(memory_space=pltpu.VMEM)
+    outs = [jax.ShapeDtypeStruct(r.shape, r.dtype) for r in results[:-1]]
+    outs += [jax.ShapeDtypeStruct((VECTORS // 32,), jnp.float32)]
+    return pl.pallas_call(
+        finish_kernel,
+        out_shape=outs,
+        in_specs=[vmem] * len(outs),
+        out_specs=[vmem] * len(outs),
+        compiler_params=pltpu.CompilerParams(vmem_limit_bytes=VMEM_BACK),
+    )(*results)
+
+
 def fast_layer(tokens, boxes, lengths, wqkv, wbox, wout, wup, wdown, vectors, cotangent):
-    depth = lax.axis_size("dp") // 4
-    device = lax.axis_index("dp") * 2 + lax.axis_index("blk")
-    own = vectors.shape[0]
-    offset = lax.rem(device * own, 128)
-    piece = lax.dynamic_update_slice(
-        jnp.zeros((384,), jnp.float32), vectors.astype(jnp.float32), (offset,)
-    )[None, :]
     shards = (wqkv, wbox, wout, wup, wdown)
-    full, kept = forward_call(depth, tokens, cotangent, boxes, lengths, piece, shards)
-    results = backward_call(depth, full, kept, shards)
-    d_vectors = lax.dynamic_slice(results[7][0], (offset,), (own,))
-    return (*results[:7], d_vectors)
+    full, kept = forward_call(tokens, cotangent, boxes, lengths, vectors, shards)
+    return tuple(finish_call(backward_call(full, kept, shards)))
 
 
 def on_device(*args):
@@ -1411,11 +1759,11 @@
     blocks, groups = lax.axis_size("blk"), lax.axis_size("dp")
     fits = (
         blocks == 2
-        and groups % 4 == 0
+        and groups == 16
         and tokens.shape[0] == 2
-        and wqkv.shape[0] % 16 == 0
-        and wdown.shape[0] % 32 == 0
-        and wbox.shape[1] == 2 * FREQ
+        and wqkv.shape == (48, 1152)
+        and wdown.shape == (192, 384)
+        and wbox.shape == (48, 2 * FREQ)
     )
     return fast_layer(*args) if fits else general_layer(*args)
 

time: 208 us -> 196 us (0.942)
  local copies, waits for them, and re-layouts: 9.37 us -> 0 us
  Pallas kernels: 198 us -> 195 us
    pallas_call x1, Pallas kernels: 105 us -> 97.9 us  [backward_call(): pl.pallas_call(partial(backward_kernel, plan), out_shape=outs, in_specs=[...]
    unnamed x21 -> x0, local copies, waits for them, and re-layouts: 7.17 us -> none
    pallas_call x0 -> x1, Pallas kernels: none -> 3.7 us  [finish_call(): pl.pallas_call(finish_kernel, out_shape=outs, in_specs=[vmem] * len(outs)...]
where the time goes in v4:
time: 196 us; the launch traced here: 195 us
  Pallas kernels  195 us (99%)
    pallas_call x1, Pallas kernels, backward_call(): pl.pallas_call(partial(backward_kernel, plan), out_shape=outs, in_specs=[...  97.9 us
    pallas_call x1, Pallas kernels, forward_call(): pl.pallas_call(partial(forward_kernel, plan), out_shape=outs, in_specs=[a...  93.1 us

profile of v4, /device:TPU:0, one launch (start us, length us, event | category | flops | bytes accessed | tf_op | source)
XLA Modules:
  0.0 195.4 jit_solution(9408476014900888763)
XLA Ops:
  0.6 93.1 %shard_map.161 = (bf16[2,4,2,2,48,1152]{5,4,3,2,1,0:T(8,128)(2,1)}, bf16[2,4,2,2,48,384]{5,4,3,2,1,0:T(8,128)(2,1)}, bf16[2,4,2,2,48,384]{5,4,3,2,1,0:T(8,128)(2...) custom-call(bf16[2,256,768]{2,1,0:T(8,128)(2,1)} %refs_0_.1, ...), custom_call_target="tpu_custom_call" | custom-call | tf_op jit(solution)/shard_map/pallas_call | solution.py:1110
  93.7 97.9 %shard_map.162 = (bf16[2,256,768]{2,1,0:T(8,128)(2,1)}, f32[2,256,768]{2,1,0:T(8,128)}, f32[48,1152]{1,0:T(8,128)}, f32[48,384]{1,0:T(8,128)}, f32[48,384]{1,0:T...) custom-call(bf16[2,4,2,2,48,1152]{5,4,3,2,1,0:T(8,128)(2,1)} %get-tuple-element.34.refs_0_, ...), custom_call_target="tpu_custom_call" | custom-call | tf_op jit(solution)/shard_map/pallas_call | solution.py:1712
  191.6 3.7 %shard_map.163 = (bf16[2,256,768]{2,1,0:T(8,128)(2,1)}, f32[2,256,768]{2,1,0:T(8,128)}, f32[48,1152]{1,0:T(8,128)}, f32[48,384]{1,0:T(8,128)}, f32[48,384]{1,0:T...) custom-call(bf16[2,256,768]{2,1,0:T(8,128)(2,1)} %get-tuple-element.52.refs_0_, ...), custom_call_target="tpu_custom_call" | custom-call | tf_op jit(solution)/shard_map/pallas_call | solution.py:1742
